TPU v7x, 32 devices: a whole 2x2x4 slice. The times are simulated.
32 devices in a mesh: dp: 16 (over z, y, core), seq: 2 (over x).
Axes of the slice: x: 2, y: 2, z: 4, core: 2. Of those that a mesh axis runs over, the one named last changes fastest.
Arguments:
- queries: bfloat16 [16, 256, 2048], P('dp', 'seq'), may hold values from -6 to 6
- keys: bfloat16 [16, 256, 2048], P('dp', 'seq'), may hold values from -6 to 6
- values: bfloat16 [16, 256, 2048], P('dp', 'seq'), may hold values from -6 to 6
- decay_bias: float32 [16, 16, 256], P('dp', None, 'seq'), may hold values from -14 to -1
- gate_matrix: bfloat16 [6144, 16], replicated, may hold values from -0.078125 to 0.078125
- resets: int32 [16, 2], P('dp', 'seq'), may hold values 0 or 1
- cotangent: bfloat16 [16, 256, 2048], P('dp', 'seq'), may hold values from -6 to 6
Outputs:
- output: bfloat16 [16, 256, 2048], P('dp', 'seq')
- grad_queries: bfloat16 [16, 256, 2048], P('dp', 'seq')
- grad_keys: bfloat16 [16, 256, 2048], P('dp', 'seq')
- grad_values: bfloat16 [16, 256, 2048], P('dp', 'seq')
- grad_gate: float32 [6144, 16], P(('dp', 'seq'))
All inputs are finite; a program needn't handle non-finite values. No bound on the sum of `resets` on one device may be relied on, other than what follows from the above.
Results may differ from a plain program's by a relative error of at most 0.012.
Values may be sent and summed in bfloat16 or wider, within the bound.
No kernel may reach another device: no remote copies, remote signals or barrier semaphores. Data moves between devices by JAX's collectives and lax.ppermute only.
A program may use at most 64 MiB of HBM per device.

v0:
```python
import jax
import jax.numpy as jnp
from jax import lax
from jax.sharding import PartitionSpec as P

BLOCK = 128


EPSILON = 1e-06


def block_updates(key_blocks, value_blocks, cumulative):
    totals = cumulative[:, -1, :]
    fading = jnp.exp(totals[:, None, :] - cumulative)
    decayed_keys = (fading[..., None] * key_blocks.astype(jnp.float32)).astype(jnp.bfloat16)
    return jnp.einsum(
        "nche,nchf->nhef", decayed_keys, value_blocks, preferred_element_type=jnp.float32
    )


def earlier_weights(factors, bound):
    positions = jnp.arange(factors.shape[0])[:, None]
    inside = positions < bound
    masked = jnp.where(inside, factors, 1.0)
    suffix = jnp.cumprod(masked[::-1], axis=0)[::-1]
    beyond = jnp.concatenate([suffix[1:], jnp.ones_like(suffix[:1])], axis=0)
    return jnp.where(inside, beyond, 0.0)


def later_weights(factors, bound):
    positions = jnp.arange(factors.shape[0])[:, None]
    inside = positions > bound
    masked = jnp.where(inside, factors, 1.0)
    prefix = jnp.cumprod(masked, axis=0)
    before = jnp.concatenate([jnp.ones_like(prefix[:1]), prefix[:-1]], axis=0)
    return jnp.where(inside, before, 0.0)


def weighted_states(weights, states):
    return jnp.sum(weights[:, :, None, None] * states, axis=0)


def body(queries, keys, values, decay_bias, gate_matrix, resets, cotangent):
    token_count = queries.shape[1]
    head_count = decay_bias.shape[1]
    model_width = queries.shape[2]
    head_size = model_width // head_count
    block_count = token_count // BLOCK
    shape_four = (block_count, BLOCK, head_count, head_size)
    question_vectors = queries[0]
    key_rows = keys[0]
    value_rows = values[0]
    query_blocks = question_vectors.reshape(shape_four)
    key_blocks = key_rows.reshape(shape_four)
    value_blocks = value_rows.reshape(shape_four)
    joined = jnp.concatenate([question_vectors, key_rows, value_rows], axis=1)
    logits = jnp.dot(joined, gate_matrix, preferred_element_type=jnp.float32) + decay_bias[0].T
    cumulative = jnp.cumsum(
        (-jax.nn.softplus(logits)).reshape(block_count, BLOCK, head_count), axis=1
    )
    totals = cumulative[:, -1, :]
    kept_flags = (1 - resets[0]).astype(jnp.float32)
    factors = kept_flags[:, None] * jnp.exp(totals)
    updates = block_updates(key_blocks, value_blocks, cumulative)
    first_index = lax.axis_index("seq") * block_count
    last_index = first_index + block_count - 1
    all_factors, all_updates = (
        lax.all_gather(factors, "seq", axis=0, tiled=True),
        lax.all_gather(updates, "seq", axis=0, tiled=True),
    )
    incoming = weighted_states(earlier_weights(all_factors, first_index), all_updates)

    def advance(carried_state, element):
        factor_row, flag_row, update_row = element
        return (factor_row[:, None, None] * carried_state + update_row, flag_row * carried_state)

    _, entering = lax.scan(advance, incoming, (factors, kept_flags, updates))
    ending = jnp.exp(totals)[:, :, None, None] * entering + updates
    scores = jnp.einsum(
        "nthe,nshe->nhts", query_blocks, key_blocks, preferred_element_type=jnp.float32
    )
    cum_heads = jnp.transpose(cumulative, (0, 2, 1))
    lower_mask = jnp.tril(jnp.ones((BLOCK, BLOCK), dtype=bool))
    differences = cum_heads[:, :, :, None] - cum_heads[:, :, None, :]
    decays = jnp.exp(jnp.where(lower_mask, differences, -jnp.inf))
    attn = decays * scores
    attn_b = attn.astype(jnp.bfloat16)
    within = jnp.einsum("nhts,nshf->nthf", attn_b, value_blocks, preferred_element_type=jnp.float32)
    entering_b = entering.astype(jnp.bfloat16)
    carried = jnp.exp(cumulative)[..., None] * jnp.einsum(
        "nthe,nhef->nthf", query_blocks, entering_b, preferred_element_type=jnp.float32
    )
    mixture = within + carried
    norm_root = jnp.sqrt(jnp.mean(mixture * mixture, axis=-1, keepdims=True) + EPSILON)
    normed = mixture / norm_root
    output = normed.astype(jnp.bfloat16).reshape(1, token_count, model_width)
    upstream = cotangent[0].reshape(shape_four).astype(jnp.float32)
    d_mixture = (
        upstream - normed * jnp.mean(upstream * normed, axis=-1, keepdims=True)
    ) / norm_root
    d_mixture_b = d_mixture.astype(jnp.bfloat16)
    d_attn = jnp.einsum(
        "nthf,nshf->nhts", d_mixture_b, value_blocks, preferred_element_type=jnp.float32
    )
    weighted = (decays * d_attn).astype(jnp.bfloat16)
    q_decay = (jnp.exp(cumulative)[..., None] * query_blocks.astype(jnp.float32)).astype(
        jnp.bfloat16
    )
    local_grad = jnp.einsum(
        "nthe,nthf->nhef", q_decay, d_mixture_b, preferred_element_type=jnp.float32
    )
    pushed = kept_flags[:, None, None, None] * local_grad
    all_pushed = lax.all_gather(pushed, "seq", axis=0, tiled=True)
    outgoing = weighted_states(later_weights(all_factors, last_index), all_pushed)

    def retreat(carried_grad, element):
        factor_row, pushed_row = element
        return (factor_row[:, None, None] * carried_grad + pushed_row, carried_grad)

    _, state_grads = lax.scan(retreat, outgoing, (factors, pushed), reverse=True)
    state_grads_b = state_grads.astype(jnp.bfloat16)
    fading = jnp.exp(totals[:, None, :] - cumulative)
    from_state = fading[..., None] * jnp.einsum(
        "nthf,nhef->nthe", value_blocks, state_grads_b, preferred_element_type=jnp.float32
    )
    products = attn * d_attn
    d_cumul = jnp.transpose(jnp.sum(products, axis=3) - jnp.sum(products, axis=2), (0, 2, 1))
    d_cumul = (
        d_cumul
        + jnp.sum(d_mixture * carried, axis=-1)
        - jnp.sum(key_blocks.astype(jnp.float32) * from_state, axis=-1)
    )
    d_cumul = d_cumul.at[:, -1, :].add(jnp.sum(state_grads * ending, axis=(2, 3)))
    d_logdecay = jnp.cumsum(d_cumul[:, ::-1, :], axis=1)[:, ::-1, :]
    d_logits = (-jax.nn.sigmoid(logits) * d_logdecay.reshape(token_count, head_count)).astype(
        jnp.bfloat16
    )
    gate_back = jnp.dot(d_logits, gate_matrix.T, preferred_element_type=jnp.float32)
    grad_q = jnp.einsum("nhts,nshe->nthe", weighted, key_blocks, preferred_element_type=jnp.float32)
    grad_q = grad_q + jnp.exp(cumulative)[..., None] * jnp.einsum(
        "nthf,nhef->nthe", d_mixture_b, entering_b, preferred_element_type=jnp.float32
    )
    grad_k = (
        jnp.einsum("nhts,nthe->nshe", weighted, query_blocks, preferred_element_type=jnp.float32)
        + from_state
    )
    grad_v = jnp.einsum("nhts,nthf->nshf", attn_b, d_mixture_b, preferred_element_type=jnp.float32)
    grad_v = grad_v + fading[..., None] * jnp.einsum(
        "nthe,nhef->nthf", key_blocks, state_grads_b, preferred_element_type=jnp.float32
    )
    grad_q = (grad_q.reshape(token_count, model_width) + gate_back[:, :model_width]).astype(
        jnp.bfloat16
    )
    grad_k = (
        grad_k.reshape(token_count, model_width) + gate_back[:, model_width : 2 * model_width]
    ).astype(jnp.bfloat16)
    grad_v = (grad_v.reshape(token_count, model_width) + gate_back[:, 2 * model_width :]).astype(
        jnp.bfloat16
    )
    grad_gate = lax.psum_scatter(
        lax.dot_general(
            joined, d_logits, (((0,), (0,)), ((), ())), preferred_element_type=jnp.float32
        ),
        ("dp", "seq"),
        scatter_dimension=0,
        tiled=True,
    )
    shape_out = (1, token_count, model_width)
    return (
        output,
        grad_q.reshape(shape_out),
        grad_k.reshape(shape_out),
        grad_v.reshape(shape_out),
        grad_gate,
    )


def solution(mesh):
    return jax.shard_map(
        body,
        mesh=mesh,
        in_specs=(
            P("dp", "seq", None),
            P("dp", "seq", None),
            P("dp", "seq", None),
            P("dp", None, "seq"),
            P(),
            P("dp", "seq"),
            P("dp", "seq", None),
        ),
        out_specs=(
            P("dp", "seq", None),
            P("dp", "seq", None),
            P("dp", "seq", None),
            P("dp", "seq", None),
            P(("dp", "seq"), None),
        ),
        check_vma=False,
    )
```

profile of v0, /device:TPU:0, one launch (start us, length us, event | category | flops | bytes accessed | tf_op | source)
XLA Modules:
  0.0 221.3 jit_solution(15675145330367030692)
XLA Ops:
  7.2 0.0 all-gather.6.cloned.1.call-start
  7.9 0.2 copy-done
  8.1 1.9 convolution_add_fusion
  10.1 0.1 copy.76
  10.2 0.2 reduce_window_sum.19
  10.3 0.1 copy.82
  10.4 0.0 copy-done.17
  10.4 0.1 copy.114
  10.6 0.5 copy.83
  11.0 0.0 copy-done.22
  11.1 0.1 copy.115
  11.2 0.1 fusion.37
  11.3 1.3 fusion.12
  12.6 0.0 all-gather.6.cloned.1.call-update
  12.7 0.0 all-gather.8.cloned.1.call-start
  12.7 5.1 %all-gather = f32[2,1,16]{2,1,0:T(1,128)S(1)} all-gather(f32[1,1,16]{2,1,0:T(1,128)S(1)} %get-tuple-element.73), channel_id=2, replica_groups=mesh['dp'=16,'seq'=2] {'seq'}, dimensions={0}, use_global_device_ids=true | all-gather | bytes 192 | tf_op jit(solution)/shard_map/all_gather | solution.py:68
  17.8 0.3 copy.113
  18.1 0.1 broadcast_select_fusion
  18.2 0.1 copy.77
  18.3 1.2 copy.87
  19.6 0.1 select_select_fusion
  19.6 0.6 convolution_multiply_fusion.1
  20.2 28.4 %all-gather.6.cloned.1.call-done = f32[32,128,128]{2,1,0:T(8,128)} async-done(((f32[16,128,128]{2,1,0:T(8,128)}), f32[32,128,128]{2,1,0:T(8,128)}) %all-gather.6.cloned.1.call-update) | async-done | bytes 2097168 | tf_op jit(solution)/shard_map/all_gather | solution.py:69
  48.6 1.9 multiply_reduce_fusion.1
  50.5 0.4 fusion.1
  50.9 0.5 multiply_reduce_fusion.6
  51.4 1.1 copy-done.9
  52.5 0.2 multiply_reduce_fusion.5
  52.7 1.5 fusion.44
  54.2 1.5 convolution_multiply_fusion
  55.7 0.0 all-gather.8.cloned.1.call-update
  55.7 0.0 reduce-scatter.4.cloned.1.call-start
  55.7 2.2 %copy.92 = f32[1,128,2048]{1,2,0:T(8,128)} copy(bf16[1,128,2048]{2,1,0:T(8,128)(2,1)} %param.10) | data formatting | bytes 1572864 | tf_op jit(solution)/shard_map/convert_element_type | solution.py:15
  58.0 0.1 pad_select_fusion
  58.1 2.0 copy.105
  60.1 0.3 fusion.3
  60.5 0.6 multiply_reduce_fusion.7
  61.1 1.1 copy-done.4
  62.1 1.5 fusion.2
  63.7 2.6 %copy.99 = f32[128,2048]{1,0:T(8,128)} copy(f32[128,2048]{0,1:T(8,128)} %bitcast.153) | data formatting | bytes 2097152 | tf_op jit(solution)/shard_map/reshape | solution.py:151
  66.3 1.3 multiply_reduce_fusion.4
  67.6 21.3 %all-gather.8.cloned.1.call-done = f32[32,128,128]{2,1,0:T(8,128)} async-done(((f32[16,128,128]{2,1,0:T(8,128)}), f32[32,128,128]{2,1,0:T(8,128)}) %all-gather.8.cloned.1.call-update) | async-done | bytes 2097168 | tf_op jit(solution)/shard_map/all_gather | solution.py:113
  89.0 1.9 multiply_reduce_fusion
  90.9 1.5 fusion.6
  92.4 0.4 multiply_reduce_fusion.2
  92.8 0.1 copy.96
  92.9 2.8 %multiply_reduce_fusion.3 = (f32[128,16]{0,1:T(8,128)S(1)}, f32[1,128,16,128]{1,3,2,0:T(8,128)}) fusion(f32[1,128,16,128]{1,3,2,0:T(8,128)} %bitcast.150, bf16[128,16,128]{2,1,0:T(8,128)(2,1)S(1)} %bitcast.138, f32[16,128,128]{2,1,0:T(8,128)S(1)} %multiply_reduce_fusion, f32[128,16]{0,1:T(8,128)S(1)} %get-tuple-element.75), kind=kOutput, calls=%fused_computation.29 | convolution fusion | flops 68155392 | bytes 3686400 | tf_op jit(solution)/shard_map/nthf,nhef->nthe/dot_general | solution.py:123
  95.7 0.1 slice_add_fusion.3
  95.7 0.1 scatter-add.4
  95.8 0.1 rev.11
  95.9 0.1 copy.97
  96.0 0.2 reduce_window_sum.21
  96.2 0.1 copy.98
  96.2 0.1 rev.12
  96.4 3.4 %fusion.11 = f32[6144,16]{1,0:T(8,128)} fusion(bf16[128,16]{0,1:T(8,128)(2,1)S(1)} %fusion.36, bf16[128,2048]{1,0:T(8,128)(2,1)} %bitcast.159, bf16[128,2048]{1,0:T(8,128)(2,1)S(1)} %bitcast.149, bf16[128,2048]{1,0:T(8,128)(2,1)S(1)} %bitcast.157), kind=kOutput, calls=%fused_computation.39 | convolution fusion | flops 29884416 | bytes 1970176
  99.8 2.3 %fusion.45 = f32[128,6144]{1,0:T(8,128)} fusion(bf16[128,16]{0,1:T(8,128)(2,1)S(1)} %fusion.36, bf16[6144,16]{0,1:T(8,128)(2,1)S(1)} %copy-done), kind=kOutput, calls=%fused_computation.93 | convolution fusion | flops 25165824 | bytes 3346432 | tf_op jit(solution)/shard_map/dot_general | solution.py:138
  102.1 2.6 %fusion.5 = f32[1,128,16,128]{1,3,2,0:T(8,128)} fusion(f32[1,128,16,128]{1,3,2,0:T(8,128)} %fusion.6, bf16[1,128,16,128]{1,3,2,0:T(8,128)(2,1)S(1)} %get-tuple-element.67, f32[16,128,128]{2,1,0:T(8,128)S(1)} %copy-done.3), kind=kOutput, calls=%fused_computation.18 | convolution fusion | flops 67633152 | bytes 3670016 | tf_op jit(solution)/shard_map/nhts,nthf->nshf/dot_general | solution.py:147
  104.7 2.6 %copy.104 = f32[128,2048]{1,0:T(8,128)} copy(f32[128,2048]{0,1:T(8,128)} %bitcast.152) | data formatting | bytes 2097152 | tf_op jit(solution)/shard_map/reshape | solution.py:157
  107.4 1.5 fusion.7
  108.9 2.6 %copy.101 = f32[128,2048]{1,0:T(8,128)} copy(f32[128,2048]{0,1:T(8,128)} %bitcast.151) | data formatting | bytes 2097152 | tf_op jit(solution)/shard_map/reshape | solution.py:155
  111.6 1.9 copy-done.1
  113.4 3.2 %fusion.15 = (bf16[1,128,2048]{2,1,0:T(8,128)(2,1)}, bf16[1,128,2048]{2,1,0:T(8,128)(2,1)}, bf16[1,128,2048]{2,1,0:T(8,128)(2,1)}) fusion(f32[128,2048]{1,0:T(8,128)} %copy.104, f32[128,6144]{1,0:T(8,128)S(1)} %copy-done.1, f32[128,2048]{1,0:T(8,128)} %copy.101, f32[128,2048]{1,0:T(8,128)} %copy.99), kind=kLoop, calls=%fused_computation.43 | loop fusion | flops 1572864 | bytes 7864320 | tf_op jit(solution)/shard_map/reshape | solution.py:173
  116.6 96.6 %reduce-scatter.4.cloned.1.call-done = f32[192,16]{1,0:T(8,128)} async-done(((f32[6144,16]{1,0:T(8,128)}), f32[192,16]{1,0:T(8,128)}) %reduce-scatter.4.cloned.1.call-update) | async-done | bytes 12304
  213.2 1.6 copy.112
  (59 shorter events, 0.3 us)
Async XLA Ops:
  7.2 0.9 copy-start
  7.2 41.4 %all-gather.6.cloned.1.call-start = ((), (), s32[]{:S(2)}) async-start(), calls=%async_computation.1 | async-start | bytes 3145728 | tf_op jit(solution)/shard_map/all_gather | solution.py:69
  8.1 2.3 %copy-start.17 = (bf16[1,128,2048]{2,1,0:T(8,128)(2,1)S(1)}, bf16[1,128,2048]{2,1,0:T(8,128)(2,1)}, u32[]{:S(2)}) copy-start(bf16[1,128,2048]{2,1,0:T(8,128)(2,1)} %param.10) | copy-start | bytes 1572868
  10.0 1.1 copy-start.22
  10.6 9.1 %copy-start.13 = (bf16[16,8,16,128]{3,2,1,0:T(8,128)(2,1)}, bf16[16,8,16,128]{3,2,1,0:T(8,128)(2,1)S(1)}, u32[]{:S(2)}) copy-start(bf16[16,8,16,128]{3,2,1,0:T(8,128)(2,1)S(1)} %copy.114) | copy-start | bytes 1572868
  11.0 1.6 copy-start.15
  11.1 6.7 %copy-start.20 = (bf16[1,128,2048]{2,1,0:T(8,128)(2,1)S(1)}, bf16[1,128,2048]{2,1,0:T(8,128)(2,1)}, u32[]{:S(2)}) copy-start(bf16[1,128,2048]{2,1,0:T(8,128)(2,1)} %param.9) | copy-start | bytes 1572868
  11.3 7.0 %copy-start.23 = (bf16[1,128,2048]{2,1,0:T(8,128)(2,1)S(1)}, bf16[1,128,2048]{2,1,0:T(8,128)(2,1)}, u32[]{:S(2)}) copy-start(bf16[1,128,2048]{2,1,0:T(8,128)(2,1)} %param.15) | copy-start | bytes 1572868
  12.6 6.9 %copy-start.24 = (pred[2]{0:T(512)(128)(4,1)S(1)}, pred[2]{0:T(512)(128)(4,1)}, u32[]{:S(2)}) copy-start(pred[2]{0:T(512)(128)(4,1)} %constant.82.clone.1) | copy-start | bytes 10
  12.7 76.3 %all-gather.8.cloned.1.call-start = ((), (), s32[]{:S(2)}) async-start(), calls=%async_computation.2 | async-start | bytes 3145728 | tf_op jit(solution)/shard_map/all_gather | solution.py:113
  18.1 32.4 %copy-start.10 = (bf16[1,128,2048]{1,2,0:T(8,128)(2,1)}, bf16[1,128,2048]{1,2,0:T(8,128)(2,1)S(1)}, u32[]{:S(2)}) copy-start(bf16[1,128,2048]{1,2,0:T(8,128)(2,1)S(1)} %copy.113) | copy-start | bytes 1572868
  20.2 40.2 %copy-start.2 = (f32[16,128,128]{2,1,0:T(8,128)}, f32[16,128,128]{2,1,0:T(8,128)S(1)}, u32[]{:S(2)}) copy-start(f32[16,128,128]{2,1,0:T(8,128)S(1)} %convolution_multiply_fusion.1) | copy-start | bytes 3145732
  50.9 1.8 copy-start.6
  50.9 1.6 copy-start.9
  52.7 1.5 copy-start.11
  55.7 157.5 %reduce-scatter.4.cloned.1.call-start = ((), (), s32[]{:S(2)}) async-start(), calls=%async_computation.3 | async-start | bytes 3244032
  60.4 1.7 copy-start.16
  61.1 1.1 copy-start.4
  62.1 4.1 %copy-start.7 = (f32[1,128,16,128]{1,3,2,0:T(8,128)S(1)}, f32[1,128,16,128]{1,3,2,0:T(8,128)}, u32[]{:S(2)}) copy-start(f32[1,128,16,128]{1,3,2,0:T(8,128)} %copy-done.6) | copy-start | bytes 3145732
  89.0 1.9 copy-start.14
  90.9 1.5 copy-start.8
  92.8 3.5 %copy-start.18 = (bf16[1,128,2048]{2,1,0:T(8,128)(2,1)S(1)}, bf16[1,128,2048]{2,1,0:T(8,128)(2,1)}, u32[]{:S(2)}) copy-start(bf16[1,128,2048]{2,1,0:T(8,128)(2,1)} %param.10) | copy-start | bytes 1572868
  92.8 3.5 %copy-start.21 = (bf16[1,128,2048]{2,1,0:T(8,128)(2,1)S(1)}, bf16[1,128,2048]{2,1,0:T(8,128)(2,1)}, u32[]{:S(2)}) copy-start(bf16[1,128,2048]{2,1,0:T(8,128)(2,1)} %param.9) | copy-start | bytes 1572868
  99.8 2.3 %copy-start.3 = (f32[16,128,128]{2,1,0:T(8,128)S(1)}, f32[16,128,128]{2,1,0:T(8,128)}, u32[]{:S(2)}) copy-start(f32[16,128,128]{2,1,0:T(8,128)} %copy-done.2) | copy-start | bytes 3145732
  102.1 5.3 %copy-start.5 = (f32[16,128,128]{2,1,0:T(8,128)S(1)}, f32[16,128,128]{2,1,0:T(8,128)}, u32[]{:S(2)}) copy-start(f32[16,128,128]{2,1,0:T(8,128)} %copy-done.4) | copy-start | bytes 3145732
  102.1 5.3 %copy-start.12 = (bf16[1,128,2048]{1,2,0:T(8,128)(2,1)S(1)}, bf16[1,128,2048]{1,2,0:T(8,128)(2,1)}, u32[]{:S(2)}) copy-start(bf16[1,128,2048]{1,2,0:T(8,128)(2,1)} %copy-done.10) | copy-start | bytes 1572868
  104.7 2.7 %copy-start.19 = (f32[1,128,16,128]{1,3,2,0:T(8,128)S(1)}, f32[1,128,16,128]{1,3,2,0:T(8,128)}, u32[]{:S(2)}) copy-start(f32[1,128,16,128]{1,3,2,0:T(8,128)} %get-tuple-element.82) | copy-start | bytes 3145732
  111.5 1.9 copy-start.1
Sparse Core Ops, SparseCore 0:
  12.8 35.8 all-gather.5
  55.8 33.1 all-gather.7
  111.7 101.4 reduce-scatter.3
where the time goes:
time: 222 us; the launch traced here: 221 us
  waiting for transfers between devices  146 us (66%)
  matrix products  22.8 us (10%)
  local copies, waits for them, and re-layouts  20.9 us (9%)
  between operations  14.8 us (7%)
  other arithmetic  11.3 us (5%)
  blocking collectives  5.1 us (2%)
    unnamed x4, waiting for transfers between devices  96.7 us
    all_gather x1, waiting for transfers between devices, body(): lax.all_gather(updates, 'seq', axis=0, tiled=True)  28.4 us
    all_gather x1, waiting for transfers between devices, body(): all_pushed = lax.all_gather(pushed, 'seq', axis=0, tiled=True)  21.3 us
    unnamed x54, local copies, waits for them, and re-layouts  8.16 us
    all_gather x1, blocking collectives, body(): lax.all_gather(factors, 'seq', axis=0, tiled=True)  5.1 us
  transfers between devices with their start and end apart: 3, of which 3 were waited for; matrix products, arithmetic and copies ran while one was open for 7% of the time, Pallas kernels for 0%

commit v1 on v0

v1 whole, which is shorter than its diff:
```python
import functools

import jax
import jax.numpy as jnp
from jax import lax
from jax.experimental import pallas as pl
from jax.experimental.pallas import tpu as pltpu
from jax.sharding import PartitionSpec as P

EPSILON = 1e-06
F32 = jnp.float32
BF16 = jnp.bfloat16
VMEM_LIMIT = 32 * 1024 * 1024


def dot_nn(a, b):
    return lax.dot_general(a, b, (((1,), (0,)), ((), ())), preferred_element_type=F32)


def dot_nt(a, b):
    return lax.dot_general(a, b, (((1,), (1,)), ((), ())), preferred_element_type=F32)


def dot_tn(a, b):
    return lax.dot_general(a, b, (((0,), (0,)), ((), ())), preferred_element_type=F32)


def exact_dot(x, ones):
    rows = x.shape[0]
    high = x.astype(BF16)
    rest = x - high.astype(F32)
    middle = rest.astype(BF16)
    low = (rest - middle.astype(F32)).astype(BF16)
    parts = dot_nn(jnp.concatenate([high, middle, low], axis=0), ones)
    return parts[:rows] + parts[rows : 2 * rows] + parts[2 * rows :]


def triangle(size, upper):
    rows = lax.broadcasted_iota(jnp.int32, (size, size), 0)
    columns = lax.broadcasted_iota(jnp.int32, (size, size), 1)
    keep = rows <= columns if upper else rows >= columns
    return jnp.where(keep, 1.0, 0.0).astype(BF16)


def decay_matrix(cum_column, cum_row):
    size = cum_row.shape[1]
    rows = lax.broadcasted_iota(jnp.int32, (size, size), 0)
    columns = lax.broadcasted_iota(jnp.int32, (size, size), 1)
    return jnp.exp(jnp.where(columns <= rows, cum_column - cum_row, -jnp.inf))


def spec():
    return pl.BlockSpec(memory_space=pltpu.VMEM)


def smem():
    return pl.BlockSpec(memory_space=pltpu.SMEM)


def lanes(rows, width, index):
    return pl.BlockSpec((rows, width), lambda i: (0, index))


def heads_block(count, size, index):
    return pl.BlockSpec((count, size, size), lambda i: (index, 0, 0))


def params():
    return pltpu.CompilerParams(vmem_limit_bytes=VMEM_LIMIT)


def gate_kernel(heads, q, k, v, bias, gate, logits_ref, cum_ref, updates_ref):
    width = q.shape[1]
    size = width // heads
    logits = (
        dot_nt(gate[:, :width], q[...])
        + dot_nt(gate[:, width : 2 * width], k[...])
        + dot_nt(gate[:, 2 * width :], v[...])
        + bias[...]
    )
    logits_ref[...] = logits
    soft = jnp.maximum(logits, 0.0) + jnp.log1p(jnp.exp(-jnp.abs(logits)))
    tokens = logits.shape[1]
    cum = exact_dot(-soft, triangle(tokens, True))
    cum_ref[...] = cum
    fading = jnp.exp(cum[:, tokens - 1 :] - cum)
    for h in range(heads):
        part = slice(h * size, (h + 1) * size)
        faded = (k[:, part].astype(F32).T * fading[h : h + 1, :]).astype(BF16)
        updates_ref[h] = dot_nn(faded, v[:, part]).astype(BF16)


def mix_kernel(first, count, q, k, v, cot, cum_ref, state, resets, out, d_mix, pushed, row_ref):
    size = state.shape[1]
    kept = (1 - resets[0, 0]).astype(F32)
    cum_columns = cum_ref[...].T
    row_terms = []
    for i in range(count):
        h = first + i
        part = slice(i * size, (i + 1) * size)
        q_h, v_h = q[:, part], v[:, part]
        column, row = cum_columns[:, h : h + 1], cum_ref[h : h + 1, :]
        attn = (decay_matrix(column, row) * dot_nt(q_h, k[:, part])).astype(BF16)
        carried = (kept * jnp.exp(column)) * dot_nn(q_h, state[i])
        mixture = dot_nn(attn, v_h) + carried
        square = jnp.mean(mixture * mixture, axis=1, keepdims=True) + EPSILON
        inverse = lax.rsqrt(square)
        normed = mixture * inverse
        out[:, part] = normed.astype(BF16)
        upstream = cot[:, part].astype(F32)
        along = jnp.mean(upstream * normed, axis=1, keepdims=True)
        d_h = ((upstream - normed * along) * inverse).astype(BF16)
        d_mix[:, part] = d_h
        row_terms.append(along * (size * EPSILON) * (inverse * inverse))
        faded = (q_h.astype(F32).T * (kept * jnp.exp(row))).astype(BF16)
        pushed[i] = dot_nn(faded, d_h).astype(BF16)
    row_ref[...] = jnp.concatenate(row_terms, axis=1)


def back_kernel(heads, q, k, v, d_mix, cum_ref, state, resets, gq, gk, gv, column_ref):
    size = state.shape[1]
    kept = (1 - resets[0, 0]).astype(F32)
    cum_columns = cum_ref[...].T
    sums = []
    for h in range(heads):
        part = slice(h * size, (h + 1) * size)
        q_h, k_h, v_h, d_h = q[:, part], k[:, part], v[:, part], d_mix[:, part]
        column, row = cum_columns[:, h : h + 1], cum_ref[h : h + 1, :]
        decays = decay_matrix(column, row)
        attn = (decays * dot_nt(q_h, k_h)).astype(BF16)
        weighted = (decays * dot_nt(d_h, v_h)).astype(BF16)
        gq[:, part] = dot_nn(weighted, k_h) + (kept * jnp.exp(column)) * dot_nt(d_h, state[h])
        gk_h = dot_tn(weighted, q_h)
        gk[:, part] = gk_h
        gv[:, part] = dot_tn(attn, d_h)
        sums.append(jnp.sum(k_h.astype(F32) * gk_h, axis=1, keepdims=True))
    column_ref[...] = jnp.concatenate(sums, axis=1)


def logit_kernel(
    heads, order, q, k, v, cum_ref, logits_ref, grads, terms, through, place, d_ref, *outs
):
    size = grads.shape[1]
    width = q.shape[1]
    cum = cum_ref[...]
    tokens = cum.shape[1]
    totals = cum[:, tokens - 1 :]
    sums = []
    for h in range(heads):
        part = slice(h * size, (h + 1) * size)
        sums.append(
            jnp.sum(k[:, part].astype(F32) * dot_nt(v[:, part], grads[h]), axis=1, keepdims=True)
        )
    from_state = jnp.concatenate(sums, axis=1).T * jnp.exp(totals - cum)
    ends = jnp.sum(from_state, axis=1, keepdims=True) + jnp.exp(totals) * through[...]
    last = lax.broadcasted_iota(jnp.int32, cum.shape, 1) == tokens - 1
    d_cum = terms[...].T - from_state + jnp.where(last, ends, 0.0)
    d_decay = exact_dot(d_cum, triangle(tokens, False))
    d_logits = (-jax.nn.sigmoid(logits_ref[...]) * d_decay).astype(BF16)
    d_ref[...] = d_logits
    arrays = (q, k, v)
    if order is None:
        for i in range(3):
            outs[0][:, i * width : (i + 1) * width] = dot_nn(d_logits, arrays[i][...])
        return
    chunks = 2 * outs[0].shape[0]
    share = outs[0].shape[2]
    whole = [dot_nn(d_logits, arrays[i][...]).astype(BF16) for i in range(3)]
    joined = jnp.concatenate(whole, axis=1)
    mine = place[0]
    for j in range(chunks):
        relative = mine ^ j
        position = 0
        for bit, mask in enumerate(order):
            position = position + jnp.where((relative & mask) != 0, chunks >> (bit + 1), 0)
        piece = joined[:, j * share : (j + 1) * share]

        @pl.when(position < chunks // 2)
        def _():
            outs[0][position] = piece

        @pl.when(position >= chunks // 2)
        def _():
            outs[1][position - chunks // 2] = piece


def finish_q_kernel(gq, d_logits, gate, out):
    out[...] = (gq[...] + dot_tn(d_logits[...], gate[...])).astype(BF16)


def finish_k_kernel(heads, gk, v, grads, cum_ref, d_logits, gate, out):
    size = grads.shape[1]
    cum = cum_ref[...]
    fading = jnp.exp(cum[:, cum.shape[1] - 1 :] - cum).T
    back = dot_tn(d_logits[...], gate[...])
    for h in range(heads):
        part = slice(h * size, (h + 1) * size)
        state_part = fading[:, h : h + 1] * dot_nt(v[:, part], grads[h])
        out[:, part] = (gk[:, part] + state_part + back[:, part]).astype(BF16)


def finish_v_kernel(heads, gv, k, grads, cum_ref, d_logits, gate, out):
    size = grads.shape[1]
    cum = cum_ref[...]
    fading = jnp.exp(cum[:, cum.shape[1] - 1 :] - cum).T
    back = dot_tn(d_logits[...], gate[...])
    for h in range(heads):
        part = slice(h * size, (h + 1) * size)
        state_part = fading[:, h : h + 1] * dot_nn(k[:, part], grads[h])
        out[:, part] = (gv[:, part] + state_part + back[:, part]).astype(BF16)


def shape(dims, dtype):
    return jax.ShapeDtypeStruct(dims, dtype)


GROUPS = 4


def body(dp_size, seq_size, queries, keys, values, decay_bias, gate_matrix, resets, cotangent):
    q, k, v, cot = queries[0], keys[0], values[0], cotangent[0]
    tokens, width = q.shape
    heads = decay_bias.shape[1]
    size = width // heads
    gate = gate_matrix.T
    forward = [(i, i + 1) for i in range(seq_size - 1)]
    backward = [(i + 1, i) for i in range(seq_size - 1)]
    kept = (1 - resets[0, 0]).astype(F32)

    logits, cum, updates = pl.pallas_call(
        functools.partial(gate_kernel, heads),
        out_shape=(
            shape((heads, tokens), F32),
            shape((heads, tokens), F32),
            shape((heads, size, size), BF16),
        ),
        in_specs=[spec()] * 5,
        out_specs=(spec(),) * 3,
        compiler_params=params(),
        name="gate",
    )(q, k, v, decay_bias[0], gate)
    totals = jnp.exp(cum[:, -1])[:, None, None]

    count = heads // GROUPS
    entering, outs, d_mixes, pushed, rows = [], [], [], [], []
    for g in range(GROUPS):
        own = updates[g * count : (g + 1) * count]
        arrived = lax.ppermute(own, "seq", forward)
        for _ in range(seq_size - 2):
            factor = kept * totals[g * count : (g + 1) * count]
            ending = factor * arrived.astype(F32) + own.astype(F32)
            arrived = lax.ppermute(ending.astype(BF16), "seq", forward)
        entering.append(arrived)
    state_grads = []
    for g in range(GROUPS):
        out_g, d_g, pushed_g, rows_g = pl.pallas_call(
            functools.partial(mix_kernel, g * count, count),
            grid=(1,),
            out_shape=(
                shape((tokens, count * size), BF16),
                shape((tokens, count * size), BF16),
                shape((count, size, size), BF16),
                shape((tokens, count), F32),
            ),
            in_specs=[lanes(tokens, count * size, g)] * 4 + [spec(), spec(), smem()],
            out_specs=(spec(),) * 4,
            compiler_params=params(),
            name="mix",
        )(q, k, v, cot, cum, entering[g], resets)
        outs.append(out_g)
        d_mixes.append(d_g)
        rows.append(rows_g)
        arrived = lax.ppermute(pushed_g, "seq", backward)
        for _ in range(seq_size - 2):
            factor = kept * totals[g * count : (g + 1) * count]
            total = factor * arrived.astype(F32) + pushed_g.astype(F32)
            arrived = lax.ppermute(total.astype(BF16), "seq", backward)
        state_grads.append(arrived)
    output = jnp.concatenate(outs, axis=1)
    d_mix = jnp.concatenate(d_mixes, axis=1)
    state = jnp.concatenate(entering, axis=0)
    grads = jnp.concatenate(state_grads, axis=0)

    gq, gk, gv, columns = pl.pallas_call(
        functools.partial(back_kernel, heads),
        out_shape=(
            shape((tokens, width), F32),
            shape((tokens, width), F32),
            shape((tokens, width), F32),
            shape((tokens, heads), F32),
        ),
        in_specs=[spec()] * 6 + [smem()],
        out_specs=(spec(),) * 4,
        compiler_params=params(),
        name="back",
    )(q, k, v, d_mix, cum, state, resets)
    terms = jnp.concatenate(rows, axis=1) - columns
    if seq_size > 2:
        through = kept * jnp.sum(grads.astype(F32) * state.astype(F32), axis=(1, 2))[:, None]
    else:
        through = jnp.zeros((heads, 1), F32)

    share = 3 * width // dp_size
    halving = (
        dp_size > 1 and dp_size & (dp_size - 1) == 0 and share % 128 == 0 and seq_size == 2
    )
    order = [1 << b for b in range(dp_size.bit_length() - 1)] if halving else None
    if halving:
        part_shapes = (shape((dp_size // 2, heads, share), BF16),) * 2
    else:
        part_shapes = (shape((heads, 3 * width), F32),)
    place = lax.axis_index("dp").astype(jnp.int32).reshape(1)
    d_logits, *parts = pl.pallas_call(
        functools.partial(logit_kernel, heads, order),
        out_shape=(shape((heads, tokens), BF16),) + part_shapes,
        in_specs=[spec()] * 8 + [smem()],
        out_specs=(spec(),) * (1 + len(part_shapes)),
        compiler_params=params(),
        name="logits",
    )(q, k, v, cum, logits, grads, terms, through, place)

    if halving:
        keep, send = parts
        for step, mask in enumerate(order):
            arrived = lax.ppermute(send, "dp", [(i, i ^ mask) for i in range(dp_size)])
            total = keep.astype(F32) + arrived.astype(F32)
            half = total.shape[0] // 2
            if half:
                keep, send = total[:half].astype(BF16), total[half:].astype(BF16)
        total = total[0]
        arrived = lax.ppermute(total.astype(BF16), "seq", [(0, 1), (1, 0)])
        total = total + arrived.astype(F32)
        piece = share // seq_size
        grad_gate = lax.dynamic_slice_in_dim(total, lax.axis_index("seq") * piece, piece, axis=1).T
    else:
        grad_gate = lax.psum_scatter(
            parts[0].T, ("dp", "seq"), scatter_dimension=0, tiled=True
        )

    def finish(kernel, arrays, index):
        return pl.pallas_call(
            kernel,
            grid=(1,),
            out_shape=shape((tokens, width), BF16),
            in_specs=[spec()] * (len(arrays) + 1) + [lanes(heads, width, index)],
            out_specs=spec(),
            compiler_params=params(),
            name="finish",
        )(*arrays, d_logits, gate)

    grad_q = finish(finish_q_kernel, (gq,), 0)
    grad_k = finish(functools.partial(finish_k_kernel, heads), (gk, v, grads, cum), 1)
    grad_v = finish(functools.partial(finish_v_kernel, heads), (gv, k, grads, cum), 2)
    return output[None], grad_q[None], grad_k[None], grad_v[None], grad_gate


def solution(mesh):
    rows = P("dp", "seq", None)
    return jax.shard_map(
        functools.partial(body, mesh.shape["dp"], mesh.shape["seq"]),
        mesh=mesh,
        in_specs=(rows, rows, rows, P("dp", None, "seq"), P(), P("dp", "seq"), rows),
        out_specs=(rows, rows, rows, rows, P(("dp", "seq"), None)),
        check_vma=False,
    )
```

time: 222 us -> 70.6 us (0.32)
  waiting for transfers between devices: 146 us -> 14.1 us
  matrix products: 22.8 us -> 0 us
  starting transfers between devices: 0.12 us -> 19.9 us
  Pallas kernels: 0 us -> 17.9 us
  between operations: 14.8 us -> 1.73 us
  other arithmetic: 11.3 us -> 2.42 us
  local copies, waits for them, and re-layouts: 20.9 us -> 13.9 us
  blocking collectives: 5.1 us -> 0 us
    unnamed x4 -> x0, waiting for transfers between devices: 96.7 us -> none
    all_gather x2 -> x0, waiting for transfers between devices: 49.7 us -> none  [the longest x1 28.4 us: body(): lax.all_gather(updates, 'seq', axis=0, tiled=True)]
    ppermute x0 -> x13, starting transfers between devices: none -> 19.9 us  [the longest x4 8.73 us: body(): arrived = lax.ppermute(own, 'seq', forward)]
    dot_general x14 -> x0, matrix products: 19.3 us -> none  [the longest x1 2.75 us: body(): jnp.einsum('nthf,nhef->nthe', value_blocks, state_grads_b, preferred_elem...]
    pallas_call x0 -> x10, Pallas kernels: none -> 17.9 us  [the longest x4 7.26 us: body(): pl.pallas_call(functools.partial(mix_kernel, g * count, count), grid=(1,)...]
    ppermute x0 -> x13, waiting for transfers between devices: none -> 14.1 us  [the longest x4 8.1 us: body(): arrived = lax.ppermute(send, 'dp', [(i, i ^ mask) for i in range(dp_size)])]
    reshape x4 -> x0, local copies, waits for them, and re-layouts: 7.94 us -> none  [the longest x1 2.64 us: body(): grad_v.reshape(token_count, model_width) + gate_back[:, 2 * model_width:]]
    reduce_sum x5 -> x0, other arithmetic: 5.69 us -> none  [the longest x2 3.79 us: weighted_states(): return jnp.sum(weights[:, :, None, None] * states, axis=0)]
  transfers between devices with their start and end apart: 3 -> 13, of which waited for: 3 -> 7; matrix products, arithmetic and copies ran while one was open for 7% -> 3% of each run, Pallas kernels for 0% -> 19%
where the time goes in v1:
time: 70.6 us; the launch traced here: 70 us
  starting transfers between devices  19.9 us (28%)
  Pallas kernels  17.9 us (25%)
  waiting for transfers between devices  14.1 us (20%)
  local copies, waits for them, and re-layouts  13.9 us (20%)
  other arithmetic  2.42 us (3%)
  between operations  1.73 us (2%)
    unnamed x55, local copies, waits for them, and re-layouts  10.7 us
    ppermute x4, starting transfers between devices, body(): arrived = lax.ppermute(own, 'seq', forward)  8.73 us
    ppermute x4, waiting for transfers between devices, body(): arrived = lax.ppermute(send, 'dp', [(i, i ^ mask) for i in range(dp_size)])  8.1 us
    pallas_call x4, Pallas kernels, body(): pl.pallas_call(functools.partial(mix_kernel, g * count, count), grid=(1,)...  7.26 us
    ppermute x4, waiting for transfers between devices, body(): arrived = lax.ppermute(pushed_g, 'seq', backward)  5.98 us
    ppermute x4, starting transfers between devices, body(): arrived = lax.ppermute(send, 'dp', [(i, i ^ mask) for i in range(dp_size)])  5.96 us
    ppermute x4, starting transfers between devices, body(): arrived = lax.ppermute(pushed_g, 'seq', backward)  5.16 us
    pallas_call x3, Pallas kernels, finish(): pl.pallas_call(kernel, grid=(1,), out_shape=shape((tokens, width), BF16),...  4.09 us
  transfers between devices with their start and end apart: 13, of which 7 were waited for; matrix products, arithmetic and copies ran while one was open for 3% of the time, Pallas kernels for 19%

profile of v1, /device:TPU:0, one launch (start us, length us, event | category | flops | bytes accessed | tf_op | source)
XLA Modules:
  0.0 70.0 jit_solution(17343603193809546346)
XLA Ops:
  0.6 0.7 copy-done.18
  1.3 1.0 %copy-done = bf16[1,128,2048]{2,1,0:T(8,128)(2,1)S(1)} copy-done((bf16[1,128,2048]{2,1,0:T(8,128)(2,1)S(1)}, bf16[1,128,2048]{2,1,0:T(8,128)(2,1)}, u32[]{:S(2)}) %copy-start) | copy-done | bytes 524312
  2.4 1.0 %copy-done.2 = bf16[1,128,2048]{2,1,0:T(8,128)(2,1)S(1)} copy-done((bf16[1,128,2048]{2,1,0:T(8,128)(2,1)S(1)}, bf16[1,128,2048]{2,1,0:T(8,128)(2,1)}, u32[]{:S(2)}) %copy-start.2) | copy-done | bytes 524312
  3.4 1.0 %copy-done.4 = bf16[1,128,2048]{2,1,0:T(8,128)(2,1)S(1)} copy-done((bf16[1,128,2048]{2,1,0:T(8,128)(2,1)S(1)}, bf16[1,128,2048]{2,1,0:T(8,128)(2,1)}, u32[]{:S(2)}) %copy-start.4) | copy-done | bytes 524312
  4.5 0.9 %copy-done.7 = bf16[6144,16]{0,1:T(8,128)(2,1)S(1)} copy-done((bf16[6144,16]{0,1:T(8,128)(2,1)S(1)}, bf16[6144,16]{0,1:T(8,128)(2,1)}, u32[]{:S(2)}) %copy-start.7) | copy-done | bytes 196632
  5.4 1.1 %gate.1 = (f32[16,128]{1,0:T(8,128)S(1)}, f32[16,128]{1,0:T(8,128)S(1)}, bf16[16,128,128]{2,1,0:T(8,128)(2,1)S(1)}) custom-call(bf16[128,2048]{1,0:T(8,128)(2,1)S(1)} %bitcast.34, bf16[128,2048]{1,0:T(8,128)(2,1)S(1)} %bitcast.18, bf16[128,2048]{1,0:T(8,128)(2,1)S(1)} %bitcast.26, f32[16,128]{1,0:T(8,128)S(1)} %bitcast.49, bf16[16,6144]{1,0:T(8,128)(2,1)S(1)} %bitcast.45), custom_call_target="tpu_custom_call" | custom-call | tf_op jit(solution)/shard_map/gate/pallas_call | solution.py:230
  6.5 0.0 copy-start.19
  6.5 0.0 copy-start.1
  6.5 0.0 copy-start.3
  6.5 0.7 fusion.2
  7.2 4.8 %collective-permute-start = (bf16[4,128,128]{2,1,0:T(8,128)(2,1)S(1)}, bf16[4,128,128]{2,1,0:T(8,128)(2,1)S(1)}, u32[]{:S(2)}, u32[]{:S(2)}) collective-permute-start(bf16[4,128,128]{2,1,0:T(8,128)(2,1)S(1)} %get-tuple-element.57), channel_id=1, source_target_pairs={{0,1},{2,3},{4,5},{6,7},{8,9},{10,11},{12,13},{14,15},{16,17},{18,... | collective-permute-start | bytes 393224 | tf_op jit(solution)/shard_map/ppermute | solution.py:248
  12.0 1.3 %collective-permute-start.1 = (bf16[4,128,128]{2,1,0:T(8,128)(2,1)S(1)}, bf16[4,128,128]{2,1,0:T(8,128)(2,1)S(1)}, u32[]{:S(2)}, u32[]{:S(2)}) collective-permute-start(bf16[4,128,128]{2,1,0:T(8,128)(2,1)S(1)} %get-tuple-element.60), channel_id=1, source_target_pairs={{0,1},{2,3},{4,5},{6,7},{8,9},{10,11},{12,13},{14,15},{16,17},{18,... | collective-permute-start | bytes 393224 | tf_op jit(solution)/shard_map/ppermute | solution.py:248
  13.4 1.3 %collective-permute-start.2 = (bf16[4,128,128]{2,1,0:T(8,128)(2,1)S(1)}, bf16[4,128,128]{2,1,0:T(8,128)(2,1)S(1)}, u32[]{:S(2)}, u32[]{:S(2)}) collective-permute-start(bf16[4,128,128]{2,1,0:T(8,128)(2,1)S(1)} %get-tuple-element.59), channel_id=1, source_target_pairs={{0,1},{2,3},{4,5},{6,7},{8,9},{10,11},{12,13},{14,15},{16,17},{18,... | collective-permute-start | bytes 393224 | tf_op jit(solution)/shard_map/ppermute | solution.py:248
  14.7 1.3 %collective-permute-start.3 = (bf16[4,128,128]{2,1,0:T(8,128)(2,1)}, bf16[4,128,128]{2,1,0:T(8,128)(2,1)S(1)}, u32[]{:S(2)}, u32[]{:S(2)}) collective-permute-start(bf16[4,128,128]{2,1,0:T(8,128)(2,1)} %get-tuple-element.58), channel_id=1, source_target_pairs={{0,1},{2,3},{4,5},{6,7},{8,9},{10,11},{12,13},{14,15},{16,17},{18,... | collective-permute-start | bytes 393224 | tf_op jit(solution)/shard_map/ppermute | solution.py:248
  16.6 0.0 collective-permute-done.state
  16.7 1.8 %mix.4 = (bf16[128,512]{1,0:T(8,128)(2,1)S(1)}, bf16[128,512]{1,0:T(8,128)(2,1)S(1)}, bf16[4,128,128]{2,1,0:T(8,128)(2,1)S(1)}, f32[128,4]{1,0:T(8,128)S(1)}) custom-call(bf16[128,2048]{1,0:T(8,128)(2,1)S(1)} %bitcast.35, bf16[128,2048]{1,0:T(8,128)(2,1)S(1)} %bitcast.19, bf16[128,2048]{1,0:T(8,128)(2,1)S(1)} %bitcast.27, bf16[128,2048]{1,0:T(8,128)(2,1)S(1)} %bitcast.41, ...), custom_call_target="tpu_custom_call" | custom-call | tf_op jit(solution)/shard_map/mix/pallas_call | solution.py:256
  18.5 0.0 copy-start.21
  18.5 0.7 copy-done.21
  19.1 0.1 copy.12
  19.2 1.8 %mix.5 = (bf16[128,512]{1,0:T(8,128)(2,1)S(1)}, bf16[128,512]{1,0:T(8,128)(2,1)S(1)}, bf16[4,128,128]{2,1,0:T(8,128)(2,1)S(1)}, f32[128,4]{1,0:T(8,128)S(1)}) custom-call(bf16[128,2048]{1,0:T(8,128)(2,1)S(1)} %bitcast.36, bf16[128,2048]{1,0:T(8,128)(2,1)S(1)} %bitcast.20, bf16[128,2048]{1,0:T(8,128)(2,1)S(1)} %bitcast.28, bf16[128,2048]{1,0:T(8,128)(2,1)S(1)} %bitcast.42, ...), custom_call_target="tpu_custom_call" | custom-call | tf_op jit(solution)/shard_map/mix/pallas_call | solution.py:256
  21.0 0.0 copy-start.22
  21.1 0.7 copy-done.22
  21.7 0.1 copy.13
  21.8 1.8 %mix.6 = (bf16[128,512]{1,0:T(8,128)(2,1)S(1)}, bf16[128,512]{1,0:T(8,128)(2,1)S(1)}, bf16[4,128,128]{2,1,0:T(8,128)(2,1)S(1)}, f32[128,4]{1,0:T(8,128)S(1)}) custom-call(bf16[128,2048]{1,0:T(8,128)(2,1)S(1)} %bitcast.37, bf16[128,2048]{1,0:T(8,128)(2,1)S(1)} %bitcast.21, bf16[128,2048]{1,0:T(8,128)(2,1)S(1)} %bitcast.29, bf16[128,2048]{1,0:T(8,128)(2,1)S(1)} %bitcast.43, ...), custom_call_target="tpu_custom_call" | custom-call | tf_op jit(solution)/shard_map/mix/pallas_call | solution.py:256
  23.6 0.6 copy-done.23
  24.2 0.6 copy.14
  24.9 1.8 %mix.7 = (bf16[128,512]{1,0:T(8,128)(2,1)S(1)}, bf16[128,512]{1,0:T(8,128)(2,1)S(1)}, bf16[4,128,128]{2,1,0:T(8,128)(2,1)S(1)}, f32[128,4]{1,0:T(8,128)S(1)}) custom-call(bf16[128,2048]{1,0:T(8,128)(2,1)S(1)} %bitcast.38, bf16[128,2048]{1,0:T(8,128)(2,1)S(1)} %bitcast.22, bf16[128,2048]{1,0:T(8,128)(2,1)S(1)} %bitcast.30, bf16[128,2048]{1,0:T(8,128)(2,1)S(1)} %bitcast.44, ...), custom_call_target="tpu_custom_call" | custom-call | tf_op jit(solution)/shard_map/mix/pallas_call | solution.py:256
  26.7 0.0 copy-start.15
  26.7 0.7 copy-done.15
  27.4 0.6 copy-done.17
  28.0 0.6 copy-done.24
  28.6 1.0 %copy.15 = f32[128,4]{0,1:T(4,128)S(1)} copy(f32[128,4]{1,0:T(8,128)} %copy-done.17) | data formatting | bytes 4096 | tf_op jit(solution)/shard_map/mix/pallas_call | solution.py:256
  29.6 0.7 pad_maximum_fusion.2
  30.3 0.7 %copy.16 = f32[128,16]{1,0:T(8,128)} copy(f32[128,16]{0,1:T(8,128)S(1)} %pad_maximum_fusion.2) | data formatting | bytes 16384 | tf_op jit(solution)/shard_map/concatenate | solution.py:297
  31.0 1.3 %collective-permute-start.4 = (bf16[4,128,128]{2,1,0:T(8,128)(2,1)}, bf16[4,128,128]{2,1,0:T(8,128)(2,1)S(1)}, u32[]{:S(2)}, u32[]{:S(2)}) collective-permute-start(bf16[4,128,128]{2,1,0:T(8,128)(2,1)} %copy-done.21), channel_id=1, source_target_pairs={{1,0},{3,2},{5,4},{7,6},{9,8},{11,10},{13,12},{15,14},{17,16},{19,... | collective-permute-start | bytes 393224 | tf_op jit(solution)/shard_map/ppermute | solution.py:273
  32.3 1.3 %collective-permute-start.5 = (bf16[4,128,128]{2,1,0:T(8,128)(2,1)}, bf16[4,128,128]{2,1,0:T(8,128)(2,1)S(1)}, u32[]{:S(2)}, u32[]{:S(2)}) collective-permute-start(bf16[4,128,128]{2,1,0:T(8,128)(2,1)} %copy-done.22), channel_id=1, source_target_pairs={{1,0},{3,2},{5,4},{7,6},{9,8},{11,10},{13,12},{15,14},{17,16},{19,... | collective-permute-start | bytes 393224 | tf_op jit(solution)/shard_map/ppermute | solution.py:273
  33.6 1.3 %collective-permute-start.6 = (bf16[4,128,128]{2,1,0:T(8,128)(2,1)}, bf16[4,128,128]{2,1,0:T(8,128)(2,1)S(1)}, u32[]{:S(2)}, u32[]{:S(2)}) collective-permute-start(bf16[4,128,128]{2,1,0:T(8,128)(2,1)} %copy-done.23), channel_id=1, source_target_pairs={{1,0},{3,2},{5,4},{7,6},{9,8},{11,10},{13,12},{15,14},{17,16},{19,... | collective-permute-start | bytes 393224 | tf_op jit(solution)/shard_map/ppermute | solution.py:273
  34.9 1.3 %collective-permute-start.7 = (bf16[4,128,128]{2,1,0:T(8,128)(2,1)}, bf16[4,128,128]{2,1,0:T(8,128)(2,1)S(1)}, u32[]{:S(2)}, u32[]{:S(2)}) collective-permute-start(bf16[4,128,128]{2,1,0:T(8,128)(2,1)} %copy-done.24), channel_id=1, source_target_pairs={{1,0},{3,2},{5,4},{7,6},{9,8},{11,10},{13,12},{15,14},{17,16},{19,... | collective-permute-start | bytes 393224 | tf_op jit(solution)/shard_map/ppermute | solution.py:273
  36.3 0.1 pad_maximum_fusion.1.state
  36.4 4.0 %back.1 = (f32[128,2048]{1,0:T(8,128)S(1)}, f32[128,2048]{1,0:T(8,128)S(1)}, f32[128,2048]{1,0:T(8,128)S(1)}, f32[128,16]{1,0:T(8,128)S(1)}) custom-call(bf16[128,2048]{1,0:T(8,128)(2,1)S(1)} %bitcast.39, bf16[128,2048]{1,0:T(8,128)(2,1)S(1)} %bitcast.23, bf16[128,2048]{1,0:T(8,128)(2,1)S(1)} %bitcast.31, bf16[128,2048]{1,0:T(8,128)(2,1)S(1)} %pad_maximum_fusion.d_mix, ...), custom_call_target="tpu_custom_call" | custom-call | tf_op jit(solution)/shard_map/back/pallas_call | solution.py:284
  40.5 1.9 %collective-permute-done.5 = bf16[4,128,128]{2,1,0:T(8,128)(2,1)S(1)} collective-permute-done((bf16[4,128,128]{2,1,0:T(8,128)(2,1)}, bf16[4,128,128]{2,1,0:T(8,128)(2,1)S(1)}, u32[]{:S(2)}, u32[]{:S(2)}) %collective-permute-start.5) | collective-permute-done | bytes 131104 | tf_op jit(solution)/shard_map/ppermute | solution.py:273
  42.4 2.7 %collective-permute-done.6 = bf16[4,128,128]{2,1,0:T(8,128)(2,1)S(1)} collective-permute-done((bf16[4,128,128]{2,1,0:T(8,128)(2,1)}, bf16[4,128,128]{2,1,0:T(8,128)(2,1)S(1)}, u32[]{:S(2)}, u32[]{:S(2)}) %collective-permute-start.6) | collective-permute-done | bytes 131104 | tf_op jit(solution)/shard_map/ppermute | solution.py:273
  45.1 1.4 %collective-permute-done.7 = bf16[4,128,128]{2,1,0:T(8,128)(2,1)S(1)} collective-permute-done((bf16[4,128,128]{2,1,0:T(8,128)(2,1)}, bf16[4,128,128]{2,1,0:T(8,128)(2,1)S(1)}, u32[]{:S(2)}, u32[]{:S(2)}) %collective-permute-start.7) | collective-permute-done | bytes 131104 | tf_op jit(solution)/shard_map/ppermute | solution.py:273
  46.5 0.0 copy-start.20
  46.5 0.7 copy-done.20
  47.2 1.5 %logits.1 = (bf16[16,128]{1,0:T(8,128)(2,1)S(1)}, bf16[8,16,384]{2,1,0:T(8,128)(2,1)S(1)}, bf16[8,16,384]{2,1,0:T(8,128)(2,1)S(1)}) custom-call(bf16[128,2048]{1,0:T(8,128)(2,1)S(1)} %bitcast.40, bf16[128,2048]{1,0:T(8,128)(2,1)S(1)} %bitcast.24, bf16[128,2048]{1,0:T(8,128)(2,1)S(1)} %bitcast.32, f32[16,128]{1,0:T(8,128)S(1)} %get-tuple-element.31.cum_ref, ...), custom_call_target="tpu_custom_call" | custom-call | tf_op jit(solution)/shard_map/logits/pallas_call | solution.py:313
  48.7 0.1 collective-permute-start.8
  48.8 1.3 %collective-permute-done.8 = bf16[8,16,384]{2,1,0:T(8,128)(2,1)S(1)} collective-permute-done((bf16[8,16,384]{2,1,0:T(8,128)(2,1)S(1)}, bf16[8,16,384]{2,1,0:T(8,128)(2,1)S(1)}, u32[]{:S(2)}, u32[]{:S(2)}) %collective-permute-start.8) | collective-permute-done | bytes 98336 | tf_op jit(solution)/shard_map/ppermute | solution.py:325
  50.1 1.6 %collective-permute-start.9 = (bf16[4,16,384]{2,1,0:T(8,128)(2,1)S(1)}, bf16[4,16,384]{2,1,0:T(8,128)(2,1)S(1)}, u32[]{:S(2)}, u32[]{:S(2)}) collective-permute-start(bf16[4,16,384]{2,1,0:T(8,128)(2,1)S(1)} %slice.47), channel_id=1, source_target_pairs={{0,4},{2,6},{4,0},{6,2},{8,12},{10,14},{12,8},{14,10},{16,20},{18,... | collective-permute-start | bytes 147464 | tf_op jit(solution)/shard_map/ppermute | solution.py:325
  51.7 2.6 %collective-permute-done.9 = bf16[4,16,384]{2,1,0:T(8,128)(2,1)S(1)} collective-permute-done((bf16[4,16,384]{2,1,0:T(8,128)(2,1)S(1)}, bf16[4,16,384]{2,1,0:T(8,128)(2,1)S(1)}, u32[]{:S(2)}, u32[]{:S(2)}) %collective-permute-start.9) | collective-permute-done | bytes 49184 | tf_op jit(solution)/shard_map/ppermute | solution.py:325
  54.3 0.0 copy-start.14
  54.3 1.6 %collective-permute-start.10 = (bf16[2,16,384]{2,1,0:T(8,128)(2,1)S(1)}, bf16[2,16,384]{2,1,0:T(8,128)(2,1)S(1)}, u32[]{:S(2)}, u32[]{:S(2)}) collective-permute-start(bf16[2,16,384]{2,1,0:T(8,128)(2,1)S(1)} %slice.49), channel_id=1, source_target_pairs={{0,8},{2,10},{4,12},{6,14},{8,0},{10,2},{12,4},{14,6},{16,24},{18,... | collective-permute-start | bytes 73736 | tf_op jit(solution)/shard_map/ppermute | solution.py:325
  56.0 2.2 %collective-permute-done.10 = bf16[2,16,384]{2,1,0:T(8,128)(2,1)S(1)} collective-permute-done((bf16[2,16,384]{2,1,0:T(8,128)(2,1)S(1)}, bf16[2,16,384]{2,1,0:T(8,128)(2,1)S(1)}, u32[]{:S(2)}, u32[]{:S(2)}) %collective-permute-start.10) | collective-permute-done | bytes 24608 | tf_op jit(solution)/shard_map/ppermute | solution.py:325
  58.3 2.7 %collective-permute-start.11 = (bf16[1,16,384]{2,1,0:T(8,128)(2,1)S(1)}, bf16[1,16,384]{2,1,0:T(8,128)(2,1)S(1)}, u32[]{:S(2)}, u32[]{:S(2)}) collective-permute-start(bf16[1,16,384]{2,1,0:T(8,128)(2,1)S(1)} %slice.51), channel_id=1, source_target_pairs={{0,16},{2,18},{4,20},{6,22},{8,24},{10,26},{12,28},{14,30},{16,0},... | collective-permute-start | bytes 36872 | tf_op jit(solution)/shard_map/ppermute | solution.py:325
  60.9 2.0 %collective-permute-done.11 = bf16[1,16,384]{2,1,0:T(8,128)(2,1)S(1)} collective-permute-done((bf16[1,16,384]{2,1,0:T(8,128)(2,1)S(1)}, bf16[1,16,384]{2,1,0:T(8,128)(2,1)S(1)}, u32[]{:S(2)}, u32[]{:S(2)}) %collective-permute-start.11) | collective-permute-done | bytes 12320 | tf_op jit(solution)/shard_map/ppermute | solution.py:325
  62.9 0.1 collective-permute-start.12
  63.0 0.0 copy-start.8
  63.0 0.8 %maximum_bitcast_fusion = bf16[1,128,2048]{2,1,0:T(8,128)(2,1)} fusion(bf16[128,512]{1,0:T(8,128)(2,1)S(1)} %copy-done.14, bf16[128,512]{1,0:T(8,128)(2,1)S(1)} %get-tuple-element.35, bf16[128,512]{1,0:T(8,128)(2,1)S(1)} %get-tuple-element.34, bf16[128,512]{1,0:T(8,128)(2,1)S(1)} %get-tuple-element.33), kind=kLoop, calls=%fused_computation | loop fusion | flops 2097152 | bytes 1048576 | tf_op jit(solution)/shard_map/broadcast_in_dim | solution.py:354
  63.9 0.1 copy-done.8
  64.0 1.2 %copy-done.12 = f32[128,2048]{1,0:T(8,128)S(1)} copy-done((f32[128,2048]{1,0:T(8,128)S(1)}, f32[128,2048]{1,0:T(8,128)}, u32[]{:S(2)}) %copy-start.12) | copy-done | bytes 1048600
  65.2 1.4 %finish.5 = bf16[128,2048]{1,0:T(8,128)(2,1)} custom-call(f32[128,2048]{1,0:T(8,128)S(1)} %copy-done.12, bf16[128,2048]{1,0:T(8,128)(2,1)S(1)} %bitcast.25, bf16[16,128,128]{2,1,0:T(8,128)(2,1)S(1)} %constant_dynamic-update-slice_fusion.grads, f32[16,128]{1,0:T(8,128)S(1)} %get-tuple-element.31.cum_ref, bf16[16,128]{1,0:T(8,128)(2,1)S(1)} %get-tuple-element.52.d_logits, ...), custom_call_target="tpu_custom_call" | custom-call | tf_op jit(solution)/shard_map/finish/pallas_call | solution.py:341
  66.6 1.5 %finish.4 = bf16[128,2048]{1,0:T(8,128)(2,1)} custom-call(f32[128,2048]{1,0:T(8,128)S(1)} %copy-done.10, bf16[128,2048]{1,0:T(8,128)(2,1)S(1)} %bitcast.33, bf16[16,128,128]{2,1,0:T(8,128)(2,1)S(1)} %constant_dynamic-update-slice_fusion.grads, f32[16,128]{1,0:T(8,128)S(1)} %get-tuple-element.31.cum_ref, bf16[16,128]{1,0:T(8,128)(2,1)S(1)} %get-tuple-element.52.d_logits, ...), custom_call_target="tpu_custom_call" | custom-call | tf_op jit(solution)/shard_map/finish/pallas_call | solution.py:341
  68.2 1.1 %finish.3 = bf16[128,2048]{1,0:T(8,128)(2,1)} custom-call(f32[128,2048]{1,0:T(8,128)S(1)} %get-tuple-element.41.gq, bf16[16,128]{1,0:T(8,128)(2,1)S(1)} %get-tuple-element.52.d_logits, bf16[16,6144]{1,0:T(8,128)(2,1)S(1)} %bitcast.48), custom_call_target="tpu_custom_call" | custom-call | tf_op jit(solution)/shard_map/finish/pallas_call | solution.py:341
  69.3 0.7 fusion
  (48 shorter events, 0.3 us)
Async XLA Ops:
  0.6 0.7 copy-start.18
  1.3 1.0 %copy-start = (bf16[1,128,2048]{2,1,0:T(8,128)(2,1)S(1)}, bf16[1,128,2048]{2,1,0:T(8,128)(2,1)}, u32[]{:S(2)}) copy-start(bf16[1,128,2048]{2,1,0:T(8,128)(2,1)} %param.8) | copy-start | bytes 1572868
  2.4 1.0 %copy-start.2 = (bf16[1,128,2048]{2,1,0:T(8,128)(2,1)S(1)}, bf16[1,128,2048]{2,1,0:T(8,128)(2,1)}, u32[]{:S(2)}) copy-start(bf16[1,128,2048]{2,1,0:T(8,128)(2,1)} %param.9) | copy-start | bytes 1572868
  3.4 1.0 %copy-start.4 = (bf16[1,128,2048]{2,1,0:T(8,128)(2,1)S(1)}, bf16[1,128,2048]{2,1,0:T(8,128)(2,1)}, u32[]{:S(2)}) copy-start(bf16[1,128,2048]{2,1,0:T(8,128)(2,1)} %param.7) | copy-start | bytes 1572868
  4.5 0.9 %copy-start.7 = (bf16[6144,16]{0,1:T(8,128)(2,1)S(1)}, bf16[6144,16]{0,1:T(8,128)(2,1)}, u32[]{:S(2)}) copy-start(bf16[6144,16]{0,1:T(8,128)(2,1)} %param.11) | copy-start | bytes 589828
  5.4 11.2 %copy-start.5 = (bf16[1,128,2048]{2,1,0:T(8,128)(2,1)S(1)}, bf16[1,128,2048]{2,1,0:T(8,128)(2,1)}, u32[]{:S(2)}) copy-start(bf16[1,128,2048]{2,1,0:T(8,128)(2,1)} %param.7) | copy-start | bytes 1572868
  5.4 11.3 %copy-start.6 = (bf16[1,128,2048]{2,1,0:T(8,128)(2,1)S(1)}, bf16[1,128,2048]{2,1,0:T(8,128)(2,1)}, u32[]{:S(2)}) copy-start(bf16[1,128,2048]{2,1,0:T(8,128)(2,1)} %param.13) | copy-start | bytes 1572868
  6.5 0.7 %copy-start.19 = (f32[16,128]{1,0:T(8,128)}, f32[16,128]{1,0:T(8,128)S(1)}, u32[]{:S(2)}) copy-start(f32[16,128]{1,0:T(8,128)S(1)} %get-tuple-element.42.logits_ref) | copy-start | bytes 24580
  6.5 10.2 %copy-start.1 = (bf16[1,128,2048]{2,1,0:T(8,128)(2,1)S(1)}, bf16[1,128,2048]{2,1,0:T(8,128)(2,1)}, u32[]{:S(2)}) copy-start(bf16[1,128,2048]{2,1,0:T(8,128)(2,1)} %param.8) | copy-start | bytes 1572868
  6.5 10.2 %copy-start.3 = (bf16[1,128,2048]{2,1,0:T(8,128)(2,1)S(1)}, bf16[1,128,2048]{2,1,0:T(8,128)(2,1)}, u32[]{:S(2)}) copy-start(bf16[1,128,2048]{2,1,0:T(8,128)(2,1)} %param.9) | copy-start | bytes 1572868
  7.2 9.4 %collective-permute-start = (bf16[4,128,128]{2,1,0:T(8,128)(2,1)S(1)}, bf16[4,128,128]{2,1,0:T(8,128)(2,1)S(1)}, u32[]{:S(2)}, u32[]{:S(2)}) collective-permute-start(bf16[4,128,128]{2,1,0:T(8,128)(2,1)S(1)} %get-tuple-element.57), channel_id=1, source_target_pairs={{0,1},{2,3},{4,5},{6,7},{8,9},{10,11},{12,13},{14,15},{16,17},{18,... | collective-permute-start | bytes 393224 | tf_op jit(solution)/shard_map/ppermute | solution.py:248
  12.0 7.2 %collective-permute-start.1 = (bf16[4,128,128]{2,1,0:T(8,128)(2,1)S(1)}, bf16[4,128,128]{2,1,0:T(8,128)(2,1)S(1)}, u32[]{:S(2)}, u32[]{:S(2)}) collective-permute-start(bf16[4,128,128]{2,1,0:T(8,128)(2,1)S(1)} %get-tuple-element.60), channel_id=1, source_target_pairs={{0,1},{2,3},{4,5},{6,7},{8,9},{10,11},{12,13},{14,15},{16,17},{18,... | collective-permute-start | bytes 393224 | tf_op jit(solution)/shard_map/ppermute | solution.py:248
  13.4 8.4 %collective-permute-start.2 = (bf16[4,128,128]{2,1,0:T(8,128)(2,1)S(1)}, bf16[4,128,128]{2,1,0:T(8,128)(2,1)S(1)}, u32[]{:S(2)}, u32[]{:S(2)}) collective-permute-start(bf16[4,128,128]{2,1,0:T(8,128)(2,1)S(1)} %get-tuple-element.59), channel_id=1, source_target_pairs={{0,1},{2,3},{4,5},{6,7},{8,9},{10,11},{12,13},{14,15},{16,17},{18,... | collective-permute-start | bytes 393224 | tf_op jit(solution)/shard_map/ppermute | solution.py:248
  14.7 10.2 %collective-permute-start.3 = (bf16[4,128,128]{2,1,0:T(8,128)(2,1)}, bf16[4,128,128]{2,1,0:T(8,128)(2,1)S(1)}, u32[]{:S(2)}, u32[]{:S(2)}) collective-permute-start(bf16[4,128,128]{2,1,0:T(8,128)(2,1)} %get-tuple-element.58), channel_id=1, source_target_pairs={{0,1},{2,3},{4,5},{6,7},{8,9},{10,11},{12,13},{14,15},{16,17},{18,... | collective-permute-start | bytes 393224 | tf_op jit(solution)/shard_map/ppermute | solution.py:248
  18.5 0.7 copy-start.21
  21.0 0.7 copy-start.22
  23.6 0.7 copy-start.23
  26.7 0.7 copy-start.15
  27.4 0.6 copy-start.17
  28.0 0.7 copy-start.24
  28.6 7.6 %copy-start.13 = (bf16[128,512]{1,0:T(8,128)(2,1)}, bf16[128,512]{1,0:T(8,128)(2,1)S(1)}, u32[]{:S(2)}) copy-start(bf16[128,512]{1,0:T(8,128)(2,1)S(1)} %get-tuple-element.36) | copy-start | bytes 393220
  28.6 7.6 %copy-start.16 = (bf16[128,512]{1,0:T(8,128)(2,1)S(1)}, bf16[128,512]{1,0:T(8,128)(2,1)}, u32[]{:S(2)}) copy-start(bf16[128,512]{1,0:T(8,128)(2,1)} %copy-done.15) | copy-start | bytes 393220
  31.0 9.4 %collective-permute-start.4 = (bf16[4,128,128]{2,1,0:T(8,128)(2,1)}, bf16[4,128,128]{2,1,0:T(8,128)(2,1)S(1)}, u32[]{:S(2)}, u32[]{:S(2)}) collective-permute-start(bf16[4,128,128]{2,1,0:T(8,128)(2,1)} %copy-done.21), channel_id=1, source_target_pairs={{1,0},{3,2},{5,4},{7,6},{9,8},{11,10},{13,12},{15,14},{17,16},{19,... | collective-permute-start | bytes 393224 | tf_op jit(solution)/shard_map/ppermute | solution.py:273
  32.3 10.0 %collective-permute-start.5 = (bf16[4,128,128]{2,1,0:T(8,128)(2,1)}, bf16[4,128,128]{2,1,0:T(8,128)(2,1)S(1)}, u32[]{:S(2)}, u32[]{:S(2)}) collective-permute-start(bf16[4,128,128]{2,1,0:T(8,128)(2,1)} %copy-done.22), channel_id=1, source_target_pairs={{1,0},{3,2},{5,4},{7,6},{9,8},{11,10},{13,12},{15,14},{17,16},{19,... | collective-permute-start | bytes 393224 | tf_op jit(solution)/shard_map/ppermute | solution.py:273
  33.6 11.5 %collective-permute-start.6 = (bf16[4,128,128]{2,1,0:T(8,128)(2,1)}, bf16[4,128,128]{2,1,0:T(8,128)(2,1)S(1)}, u32[]{:S(2)}, u32[]{:S(2)}) collective-permute-start(bf16[4,128,128]{2,1,0:T(8,128)(2,1)} %copy-done.23), channel_id=1, source_target_pairs={{1,0},{3,2},{5,4},{7,6},{9,8},{11,10},{13,12},{15,14},{17,16},{19,... | collective-permute-start | bytes 393224 | tf_op jit(solution)/shard_map/ppermute | solution.py:273
  34.9 11.6 %collective-permute-start.7 = (bf16[4,128,128]{2,1,0:T(8,128)(2,1)}, bf16[4,128,128]{2,1,0:T(8,128)(2,1)S(1)}, u32[]{:S(2)}, u32[]{:S(2)}) collective-permute-start(bf16[4,128,128]{2,1,0:T(8,128)(2,1)} %copy-done.24), channel_id=1, source_target_pairs={{1,0},{3,2},{5,4},{7,6},{9,8},{11,10},{13,12},{15,14},{17,16},{19,... | collective-permute-start | bytes 393224 | tf_op jit(solution)/shard_map/ppermute | solution.py:273
  36.4 4.1 %copy-start.25 = (f32[128,16]{1,0:T(8,128)S(1)}, f32[128,16]{1,0:T(8,128)}, u32[]{:S(2)}) copy-start(f32[128,16]{1,0:T(8,128)} %copy.16) | copy-start | bytes 24580
  40.4 8.3 %copy-start.9 = (f32[128,2048]{1,0:T(8,128)}, f32[128,2048]{1,0:T(8,128)S(1)}, u32[]{:S(2)}) copy-start(f32[128,2048]{1,0:T(8,128)S(1)} %get-tuple-element.53.gk) | copy-start | bytes 3145732
  40.4 8.3 %copy-start.11 = (f32[128,2048]{1,0:T(8,128)}, f32[128,2048]{1,0:T(8,128)S(1)}, u32[]{:S(2)}) copy-start(f32[128,2048]{1,0:T(8,128)S(1)} %get-tuple-element.54.gv) | copy-start | bytes 3145732
  46.5 0.7 %copy-start.20 = (f32[16,128]{1,0:T(8,128)S(1)}, f32[16,128]{1,0:T(8,128)}, u32[]{:S(2)}) copy-start(f32[16,128]{1,0:T(8,128)} %copy-done.19) | copy-start | bytes 24580
  48.7 1.4 %collective-permute-start.8 = (bf16[8,16,384]{2,1,0:T(8,128)(2,1)S(1)}, bf16[8,16,384]{2,1,0:T(8,128)(2,1)S(1)}, u32[]{:S(2)}, u32[]{:S(2)}) collective-permute-start(bf16[8,16,384]{2,1,0:T(8,128)(2,1)S(1)} %get-tuple-element.56), channel_id=1, source_target_pairs={{0,2},{2,0},{4,6},{6,4},{8,10},{10,8},{12,14},{14,12},{16,18},{18,... | collective-permute-start | bytes 294920 | tf_op jit(solution)/shard_map/ppermute | solution.py:325
  50.1 4.2 %collective-permute-start.9 = (bf16[4,16,384]{2,1,0:T(8,128)(2,1)S(1)}, bf16[4,16,384]{2,1,0:T(8,128)(2,1)S(1)}, u32[]{:S(2)}, u32[]{:S(2)}) collective-permute-start(bf16[4,16,384]{2,1,0:T(8,128)(2,1)S(1)} %slice.47), channel_id=1, source_target_pairs={{0,4},{2,6},{4,0},{6,2},{8,12},{10,14},{12,8},{14,10},{16,20},{18,... | collective-permute-start | bytes 147464 | tf_op jit(solution)/shard_map/ppermute | solution.py:325
  54.3 8.7 %copy-start.14 = (bf16[128,512]{1,0:T(8,128)(2,1)S(1)}, bf16[128,512]{1,0:T(8,128)(2,1)}, u32[]{:S(2)}) copy-start(bf16[128,512]{1,0:T(8,128)(2,1)} %copy-done.13) | copy-start | bytes 393220
  54.3 3.9 %collective-permute-start.10 = (bf16[2,16,384]{2,1,0:T(8,128)(2,1)S(1)}, bf16[2,16,384]{2,1,0:T(8,128)(2,1)S(1)}, u32[]{:S(2)}, u32[]{:S(2)}) collective-permute-start(bf16[2,16,384]{2,1,0:T(8,128)(2,1)S(1)} %slice.49), channel_id=1, source_target_pairs={{0,8},{2,10},{4,12},{6,14},{8,0},{10,2},{12,4},{14,6},{16,24},{18,... | collective-permute-start | bytes 73736 | tf_op jit(solution)/shard_map/ppermute | solution.py:325
  58.3 4.7 %collective-permute-start.11 = (bf16[1,16,384]{2,1,0:T(8,128)(2,1)S(1)}, bf16[1,16,384]{2,1,0:T(8,128)(2,1)S(1)}, u32[]{:S(2)}, u32[]{:S(2)}) collective-permute-start(bf16[1,16,384]{2,1,0:T(8,128)(2,1)S(1)} %slice.51), channel_id=1, source_target_pairs={{0,16},{2,18},{4,20},{6,22},{8,24},{10,26},{12,28},{14,30},{16,0},... | collective-permute-start | bytes 36872 | tf_op jit(solution)/shard_map/ppermute | solution.py:325
  62.9 6.4 %collective-permute-start.12 = (bf16[16,384]{1,0:T(8,128)(2,1)S(1)}, bf16[16,384]{1,0:T(8,128)(2,1)S(1)}, u32[]{:S(2)}, u32[]{:S(2)}) collective-permute-start(bf16[16,384]{1,0:T(8,128)(2,1)S(1)} %get-tuple-element.61), channel_id=1, source_target_pairs={{0,1},{1,0},{2,3},{3,2},{4,5},{5,4},{6,7},{7,6},{8,9},{9,8},{10,11... | collective-permute-start | bytes 36872 | tf_op jit(solution)/shard_map/ppermute | solution.py:331
  63.0 1.0 %copy-start.8 = (bf16[6144,16]{0,1:T(8,128)(2,1)S(1)}, bf16[6144,16]{0,1:T(8,128)(2,1)}, u32[]{:S(2)}) copy-start(bf16[6144,16]{0,1:T(8,128)(2,1)} %param.11) | copy-start | bytes 589828
  64.0 1.2 %copy-start.12 = (f32[128,2048]{1,0:T(8,128)S(1)}, f32[128,2048]{1,0:T(8,128)}, u32[]{:S(2)}) copy-start(f32[128,2048]{1,0:T(8,128)} %copy-done.11) | copy-start | bytes 3145732
  65.2 1.5 %copy-start.10 = (f32[128,2048]{1,0:T(8,128)S(1)}, f32[128,2048]{1,0:T(8,128)}, u32[]{:S(2)}) copy-start(f32[128,2048]{1,0:T(8,128)} %copy-done.9) | copy-start | bytes 3145732

commit v2 on v1

v2 whole, which is shorter than its diff:
```python
import functools

import jax
import jax.numpy as jnp
from jax import lax
from jax.experimental import pallas as pl
from jax.experimental.pallas import tpu as pltpu
from jax.sharding import PartitionSpec as P

EPSILON = 1e-06
F32 = jnp.float32
BF16 = jnp.bfloat16
SMALL = 16 * 1024 * 1024
LARGE = 60 * 1024 * 1024


def dot_nn(a, b):
    return lax.dot_general(a, b, (((1,), (0,)), ((), ())), preferred_element_type=F32)


def dot_nt(a, b):
    return lax.dot_general(a, b, (((1,), (1,)), ((), ())), preferred_element_type=F32)


def dot_tn(a, b):
    return lax.dot_general(a, b, (((0,), (0,)), ((), ())), preferred_element_type=F32)


def exact_dot(x, ones):
    rows = x.shape[0]
    high = x.astype(BF16)
    rest = x - high.astype(F32)
    middle = rest.astype(BF16)
    low = (rest - middle.astype(F32)).astype(BF16)
    parts = dot_nn(jnp.concatenate([high, middle, low], axis=0), ones)
    return parts[:rows] + parts[rows : 2 * rows] + parts[2 * rows :]


def triangle(size, upper):
    rows = lax.broadcasted_iota(jnp.int32, (size, size), 0)
    columns = lax.broadcasted_iota(jnp.int32, (size, size), 1)
    keep = rows <= columns if upper else rows >= columns
    return jnp.where(keep, 1.0, 0.0).astype(BF16)


def decay_matrix(cum_column, cum_row):
    size = cum_row.shape[1]
    rows = lax.broadcasted_iota(jnp.int32, (size, size), 0)
    columns = lax.broadcasted_iota(jnp.int32, (size, size), 1)
    return jnp.exp(jnp.where(columns <= rows, cum_column - cum_row, -jnp.inf))


def spec():
    return pl.BlockSpec(memory_space=pltpu.VMEM)


def smem():
    return pl.BlockSpec(memory_space=pltpu.SMEM)


def anywhere():
    return pl.BlockSpec(memory_space=pl.ANY)


def params(limit=SMALL):
    return pltpu.CompilerParams(vmem_limit_bytes=limit)


def cost():
    return pl.CostEstimate(flops=1000, bytes_accessed=1000, transcendentals=0)


def gate_kernel(heads, groups, q_in, k_in, v_in, bias_in, gate_in, *refs):
    logits_ref, cum_ref, *updates = refs[: 2 + len(groups)]
    q, k, v, bias, gate, sems = refs[2 + len(groups) :]
    copies = [
        pltpu.make_async_copy(source, target, sems.at[i])
        for i, (source, target) in enumerate(
            ((gate_in, gate), (bias_in, bias), (k_in, k), (q_in, q), (v_in, v))
        )
    ]
    for copy in copies:
        copy.start()
    width = q.shape[1]
    size = width // heads
    copies[0].wait()
    copies[1].wait()
    copies[2].wait()
    logits = bias[...] + dot_nt(gate[:, width : 2 * width], k[...])
    copies[3].wait()
    logits = logits + dot_nt(gate[:, :width], q[...])
    copies[4].wait()
    logits = logits + dot_nt(gate[:, 2 * width :], v[...])
    logits_ref[...] = logits
    soft = jnp.maximum(logits, 0.0) + jnp.log1p(jnp.exp(-jnp.abs(logits)))
    tokens = logits.shape[1]
    cum = exact_dot(-soft, triangle(tokens, True))
    cum_ref[...] = cum
    fading = jnp.exp(cum[:, tokens - 1 :] - cum)
    for (first, count), out in zip(groups, updates):
        for i in range(count):
            h = first + i
            part = slice(h * size, (h + 1) * size)
            faded = (k[:, part].astype(F32).T * fading[h : h + 1, :]).astype(BF16)
            out[i] = dot_nn(faded, v[:, part]).astype(BF16)


def mix_kernel(first, count, q, k, v, cot, cum_ref, state, resets, out, d_mix, pushed, row_ref):
    size = state.shape[1]
    kept = (1 - resets[0, 0]).astype(F32)
    cum_columns = cum_ref[...].T
    row_terms = []
    for i in range(count):
        h = first + i
        part = slice(h * size, (h + 1) * size)
        own = slice(i * size, (i + 1) * size)
        q_h, v_h = q[:, part], v[:, part]
        column, row = cum_columns[:, h : h + 1], cum_ref[h : h + 1, :]
        attn = (decay_matrix(column, row) * dot_nt(q_h, k[:, part])).astype(BF16)
        carried = (kept * jnp.exp(column)) * dot_nn(q_h, state[i])
        mixture = dot_nn(attn, v_h) + carried
        square = jnp.mean(mixture * mixture, axis=1, keepdims=True) + EPSILON
        inverse = lax.rsqrt(square)
        normed = mixture * inverse
        out[:, own] = normed.astype(BF16)
        upstream = cot[:, part].astype(F32)
        along = jnp.mean(upstream * normed, axis=1, keepdims=True)
        d_h = ((upstream - normed * along) * inverse).astype(BF16)
        d_mix[:, own] = d_h
        row_terms.append(jnp.sum(d_h.astype(F32) * mixture, axis=1, keepdims=True))
        faded = (q_h.astype(F32).T * (kept * jnp.exp(row))).astype(BF16)
        pushed[i] = dot_nn(faded, d_h).astype(BF16)
    row_ref[...] = jnp.concatenate(row_terms, axis=1).T


def back_kernel(heads, groups, *refs):
    q, k, v, cum_ref, resets = refs[:5]
    number = len(groups)
    outs, d_mixes, states, row_terms = [refs[5 + number * i : 5 + number * (i + 1)] for i in range(4)]
    output, gq, gk, gv, term_ref = refs[5 + 4 * number :]
    size = states[0].shape[1]
    kept = (1 - resets[0, 0]).astype(F32)
    cum_columns = cum_ref[...].T
    sums = []
    for g, (first, count) in enumerate(groups):
        output[:, first * size : (first + count) * size] = outs[g][...]
        for i in range(count):
            h = first + i
            part = slice(h * size, (h + 1) * size)
            q_h, k_h, v_h = q[:, part], k[:, part], v[:, part]
            d_h = d_mixes[g][:, i * size : (i + 1) * size]
            column, row = cum_columns[:, h : h + 1], cum_ref[h : h + 1, :]
            decays = decay_matrix(column, row)
            attn = (decays * dot_nt(q_h, k_h)).astype(BF16)
            d_attn = dot_nt(d_h, v_h)
            weighted = (decays * d_attn).astype(BF16)
            sums.append(jnp.sum(attn.astype(F32) * d_attn, axis=0, keepdims=True))
            gq[:, part] = dot_nn(weighted, k_h) + (kept * jnp.exp(column)) * dot_nt(
                d_h, states[g][i]
            )
            gk[:, part] = dot_tn(weighted, q_h)
            gv[:, part] = dot_tn(attn, d_h)
    term_ref[...] = jnp.concatenate([r[...] for r in row_terms], axis=0) - jnp.concatenate(
        sums, axis=0
    )


def logit_kernel(heads, groups, order, q, k, v, cum_ref, logits_ref, terms, through, place, *refs):
    grads = refs[: len(groups)]
    d_ref, *outs = refs[len(groups) :]
    size = grads[0].shape[1]
    width = q.shape[1]
    cum = cum_ref[...]
    tokens = cum.shape[1]
    totals = cum[:, tokens - 1 :]
    sums = []
    for g, (first, count) in enumerate(groups):
        for i in range(count):
            part = slice((first + i) * size, (first + i + 1) * size)
            moved = dot_nt(v[:, part], grads[g][i])
            sums.append(jnp.sum(k[:, part].astype(F32) * moved, axis=1, keepdims=True))
    from_state = jnp.concatenate(sums, axis=1).T * jnp.exp(totals - cum)
    ends = jnp.sum(from_state, axis=1, keepdims=True) + jnp.exp(totals) * through[...]
    last = lax.broadcasted_iota(jnp.int32, cum.shape, 1) == tokens - 1
    d_cum = terms[...] - from_state + jnp.where(last, ends, 0.0)
    d_decay = exact_dot(d_cum, triangle(tokens, False))
    d_logits = (-jax.nn.sigmoid(logits_ref[...]) * d_decay).astype(BF16)
    d_ref[...] = d_logits
    arrays = (q, k, v)
    if order is None:
        for i in range(3):
            outs[0][:, i * width : (i + 1) * width] = dot_nn(d_logits, arrays[i][...])
        return
    chunks = 2 * outs[0].shape[0]
    share = outs[0].shape[2]
    whole = [dot_nn(d_logits, arrays[i][...]).astype(BF16) for i in range(3)]
    joined = jnp.concatenate(whole, axis=1)
    mine = place[0]
    for j in range(chunks):
        relative = mine ^ j
        position = 0
        for bit, mask in enumerate(order):
            position = position + jnp.where((relative & mask) != 0, chunks >> (bit + 1), 0)
        piece = joined[:, j * share : (j + 1) * share]

        @pl.when(position < chunks // 2)
        def _():
            outs[0][position] = piece

        @pl.when(position >= chunks // 2)
        def _():
            outs[1][position - chunks // 2] = piece


def finish_q_kernel(gq, d_logits, gate, out):
    width = out.shape[1]
    out[...] = (gq[...] + dot_tn(d_logits[...], gate[:, :width])).astype(BF16)


def finish_k_kernel(groups, gk, v, cum_ref, d_logits, gate, *refs):
    *grads, out = refs
    size = grads[0].shape[1]
    width = out.shape[1]
    cum = cum_ref[...]
    fading = jnp.exp(cum[:, cum.shape[1] - 1 :] - cum).T
    back = dot_tn(d_logits[...], gate[:, width : 2 * width])
    for g, (first, count) in enumerate(groups):
        for i in range(count):
            h = first + i
            part = slice(h * size, (h + 1) * size)
            state_part = fading[:, h : h + 1] * dot_nt(v[:, part], grads[g][i])
            out[:, part] = (gk[:, part] + state_part + back[:, part]).astype(BF16)


def finish_v_kernel(groups, gv, k, cum_ref, d_logits, gate, *refs):
    *grads, out = refs
    size = grads[0].shape[1]
    width = out.shape[1]
    cum = cum_ref[...]
    fading = jnp.exp(cum[:, cum.shape[1] - 1 :] - cum).T
    back = dot_tn(d_logits[...], gate[:, 2 * width :])
    for g, (first, count) in enumerate(groups):
        for i in range(count):
            h = first + i
            part = slice(h * size, (h + 1) * size)
            state_part = fading[:, h : h + 1] * dot_nn(k[:, part], grads[g][i])
            out[:, part] = (gv[:, part] + state_part + back[:, part]).astype(BF16)


def shape(dims, dtype):
    return jax.ShapeDtypeStruct(dims, dtype)


def head_groups(heads):
    parts = 3 if heads >= 3 else 1
    sizes = [heads // parts + (1 if i < heads % parts else 0) for i in range(parts)]
    return [(sum(sizes[:i]), sizes[i]) for i in range(parts)]


def body(dp_size, seq_size, queries, keys, values, decay_bias, gate_matrix, resets, cotangent):
    q, k, v, cot = queries[0], keys[0], values[0], cotangent[0]
    tokens, width = q.shape
    heads = decay_bias.shape[1]
    size = width // heads
    gate = gate_matrix.T
    groups = head_groups(heads)
    forward = [(i, i + 1) for i in range(seq_size - 1)]
    backward = [(i + 1, i) for i in range(seq_size - 1)]
    kept = (1 - resets[0, 0]).astype(F32)

    logits, cum, *updates = pl.pallas_call(
        functools.partial(gate_kernel, heads, groups),
        out_shape=(shape((heads, tokens), F32),) * 2
        + tuple(shape((count, size, size), BF16) for _, count in groups),
        in_specs=[anywhere()] * 5,
        out_specs=(spec(),) * (2 + len(groups)),
        scratch_shapes=[
            pltpu.VMEM((tokens, width), BF16),
            pltpu.VMEM((tokens, width), BF16),
            pltpu.VMEM((tokens, width), BF16),
            pltpu.VMEM((heads, tokens), F32),
            pltpu.VMEM((heads, 3 * width), BF16),
            pltpu.SemaphoreType.DMA((5,)),
        ],
        compiler_params=params(LARGE),
        name="gate",
    )(q, k, v, decay_bias[0], gate)

    def chain(own, first, count, pairs):
        arrived = lax.ppermute(own, "seq", pairs)
        for _ in range(seq_size - 2):
            factor = kept * jnp.exp(cum[first : first + count, -1])[:, None, None]
            passed = factor * arrived.astype(F32) + own.astype(F32)
            arrived = lax.ppermute(passed.astype(BF16), "seq", pairs)
        return arrived

    entering = [chain(own, *group, forward) for own, group in zip(updates, groups)]
    outs, d_mixes, rows, grads = [], [], [], []
    for (first, count), state in zip(groups, entering):
        out_g, d_g, pushed, rows_g = pl.pallas_call(
            functools.partial(mix_kernel, first, count),
            out_shape=(
                shape((tokens, count * size), BF16),
                shape((tokens, count * size), BF16),
                shape((count, size, size), BF16),
                shape((count, tokens), F32),
            ),
            in_specs=[spec()] * 6 + [smem()],
            out_specs=(spec(),) * 4,
            compiler_params=params(),
            cost_estimate=cost(),
            name="mix",
        )(q, k, v, cot, cum, state, resets)
        outs.append(out_g)
        d_mixes.append(d_g)
        rows.append(rows_g)
        grads.append(chain(pushed, first, count, backward))

    output, gq, gk, gv, terms = pl.pallas_call(
        functools.partial(back_kernel, heads, groups),
        out_shape=(shape((tokens, width), BF16),)
        + (shape((tokens, width), F32),) * 3
        + (shape((heads, tokens), F32),),
        in_specs=[spec()] * 4 + [smem()] + [spec()] * (4 * len(groups)),
        out_specs=(spec(),) * 5,
        compiler_params=params(),
        cost_estimate=cost(),
        name="back",
    )(q, k, v, cum, resets, *outs, *d_mixes, *entering, *rows)
    if seq_size > 2:
        through = [
            kept * jnp.sum(g.astype(F32) * s.astype(F32), axis=(1, 2))[:, None]
            for g, s in zip(grads, entering)
        ]
        through = jnp.concatenate(through, axis=0)
    else:
        through = jnp.zeros((heads, 1), F32)

    share = 3 * width // dp_size
    halving = (
        dp_size > 1 and dp_size & (dp_size - 1) == 0 and share % 128 == 0 and seq_size == 2
    )
    order = [1 << b for b in range(dp_size.bit_length() - 1)] if halving else None
    if halving:
        part_shapes = (shape((dp_size // 2, heads, share), BF16),) * 2
    else:
        part_shapes = (shape((heads, 3 * width), F32),)
    place = lax.axis_index("dp").astype(jnp.int32).reshape(1)
    d_logits, *parts = pl.pallas_call(
        functools.partial(logit_kernel, heads, groups, order),
        out_shape=(shape((heads, tokens), BF16),) + part_shapes,
        in_specs=[spec()] * 7 + [smem()] + [spec()] * len(groups),
        out_specs=(spec(),) * (1 + len(part_shapes)),
        compiler_params=params(),
        cost_estimate=cost(),
        name="logits",
    )(q, k, v, cum, logits, terms, through, place, *grads)

    def finish(kernel, *arrays):
        return pl.pallas_call(
            kernel,
            out_shape=shape((tokens, width), BF16),
            in_specs=[spec()] * len(arrays),
            out_specs=spec(),
            compiler_params=params(),
            cost_estimate=cost(),
            name="finish",
        )(*arrays)

    grad_q = finish(finish_q_kernel, gq, d_logits, gate)
    grad_k = finish(
        functools.partial(finish_k_kernel, groups), gk, v, cum, d_logits, gate, *grads
    )
    grad_v = finish(
        functools.partial(finish_v_kernel, groups), gv, k, cum, d_logits, gate, *grads
    )

    if halving:
        keep, send = parts
        for step, mask in enumerate(order):
            arrived = lax.ppermute(send, "dp", [(i, i ^ mask) for i in range(dp_size)])
            total = keep.astype(F32) + arrived.astype(F32)
            half = total.shape[0] // 2
            if half:
                keep, send = total[:half].astype(BF16), total[half:].astype(BF16)
            if step == 0:
                send, grad_q = lax.optimization_barrier((send, grad_q))
            elif step == 1:
                send, grad_k = lax.optimization_barrier((send, grad_k))
            elif step == 2:
                send, grad_v = lax.optimization_barrier((send, grad_v))
        total = total[0]
        arrived = lax.ppermute(total.astype(BF16), "seq", [(0, 1), (1, 0)])
        total = total + arrived.astype(F32)
        piece = share // seq_size
        grad_gate = lax.dynamic_slice_in_dim(total, lax.axis_index("seq") * piece, piece, axis=1).T
    else:
        grad_gate = lax.psum_scatter(
            parts[0].T, ("dp", "seq"), scatter_dimension=0, tiled=True
        )
    return output[None], grad_q[None], grad_k[None], grad_v[None], grad_gate


def solution(mesh):
    rows = P("dp", "seq", None)
    return jax.shard_map(
        functools.partial(body, mesh.shape["dp"], mesh.shape["seq"]),
        mesh=mesh,
        in_specs=(rows, rows, rows, P("dp", None, "seq"), P(), P("dp", "seq"), rows),
        out_specs=(rows, rows, rows, rows, P(("dp", "seq"), None)),
        check_vma=False,
    )
```

time: 70.6 us -> 56.6 us (0.80)
  local copies, waits for them, and re-layouts: 13.9 us -> 2.66 us
  waiting for transfers between devices: 14.1 us -> 8.75 us
  Pallas kernels: 17.9 us -> 22.7 us
  other arithmetic: 2.42 us -> 0.75 us
    unnamed x55 -> x18, local copies, waits for them, and re-layouts: 10.7 us -> 2.64 us
    pallas_call x10 -> x9, Pallas kernels: 17.9 us -> 22.7 us  [the longest x3 9.03 us: body(): pl.pallas_call(functools.partial(mix_kernel, first, count), out_shape=(sh...]
    ppermute x4, waiting for transfers between devices: 8.1 us -> 4.01 us  [body(): arrived = lax.ppermute(send, 'dp', [(i, i ^ mask) for i in range(dp_size)])]
    ppermute x8 -> x6, waiting for transfers between devices: 5.99 us -> 3.07 us  [chain(): arrived = lax.ppermute(own, 'seq', pairs)]
    ppermute x1, starting transfers between devices: 0.07 us -> 2.66 us  [body(): arrived = lax.ppermute(total.astype(BF16), 'seq', [(0, 1), (1, 0)])]
    ppermute x8 -> x6, starting transfers between devices: 13.9 us -> 11.3 us  [chain(): arrived = lax.ppermute(own, 'seq', pairs)]
    pallas_call x4 -> x0, local copies, waits for them, and re-layouts: 1.73 us -> none  [body(): pl.pallas_call(functools.partial(mix_kernel, g * count, count), grid=(1,)...]
    ppermute x1, waiting for transfers between devices: 0.01 us -> 1.67 us  [body(): arrived = lax.ppermute(total.astype(BF16), 'seq', [(0, 1), (1, 0)])]
  transfers between devices with their start and end apart: 13 -> 11, of which waited for: 7 -> 7; matrix products, arithmetic and copies ran while one was open for 3% -> 0% of each run, Pallas kernels for 19% -> 31%
where the time goes in v2:
time: 56.6 us; the launch traced here: 56.3 us
  Pallas kernels  22.7 us (40%)
  starting transfers between devices  19.9 us (35%)
  waiting for transfers between devices  8.75 us (15%)
  local copies, waits for them, and re-layouts  2.66 us (5%)
  between operations  1.49 us (3%)
  other arithmetic  0.75 us (1%)
    ppermute x6, starting transfers between devices, chain(): arrived = lax.ppermute(own, 'seq', pairs)  11.3 us
    pallas_call x3, Pallas kernels, body(): pl.pallas_call(functools.partial(mix_kernel, first, count), out_shape=(sh...  9.03 us
    ppermute x4, starting transfers between devices, body(): arrived = lax.ppermute(send, 'dp', [(i, i ^ mask) for i in range(dp_size)])  5.95 us
    pallas_call x1, Pallas kernels, body(): pl.pallas_call(functools.partial(back_kernel, heads, groups), out_shape=(...  4.48 us
    pallas_call x3, Pallas kernels, finish(): pl.pallas_call(kernel, out_shape=shape((tokens, width), BF16), in_specs=[...  4.09 us
    ppermute x4, waiting for transfers between devices, body(): arrived = lax.ppermute(send, 'dp', [(i, i ^ mask) for i in range(dp_size)])  4.01 us
    pallas_call x1, Pallas kernels, body(): pl.pallas_call(functools.partial(gate_kernel, heads, groups), out_shape=(...  3.66 us
    ppermute x6, waiting for transfers between devices, chain(): arrived = lax.ppermute(own, 'seq', pairs)  3.07 us
  transfers between devices with their start and end apart: 11, of which 7 were waited for; matrix products, arithmetic and copies ran while one was open for 0% of the time, Pallas kernels for 31%

profile of v2, /device:TPU:0, one launch (start us, length us, event | category | flops | bytes accessed | tf_op | source)
XLA Modules:
  0.0 56.3 jit_solution(10544465175514465706)
XLA Ops:
  0.6 0.0 copy-start
  0.6 0.0 copy-start.1
  0.7 0.0 copy-start.2
  0.7 3.7 %gate.1 = (f32[16,128]{1,0:T(8,128)}, f32[16,128]{1,0:T(8,128)}, bf16[6,128,128]{2,1,0:T(8,128)(2,1)}, bf16[5,128,128]{2,1,0:T(8,128)(2,1)}, bf16[5,128,128]{2,1,0:T(8,128)(2,1)}) custom-call(bf16[128,2048]{1,0:T(8,128)(2,1)} %bitcast.31, bf16[128,2048]{1,0:T(8,128)(2,1)} %bitcast.24, bf16[128,2048]{1,0:T(8,128)(2,1)} %bitcast.17, f32[16,128]{1,0:T(8,128)} %bitcast.47, ...), custom_call_target="tpu_custom_call" | custom-call | tf_op jit(solution)/shard_map/gate/pallas_call | solution.py:271
  4.3 0.0 copy-start.5
  4.3 4.9 %collective-permute-start = (bf16[6,128,128]{2,1,0:T(8,128)(2,1)}, bf16[6,128,128]{2,1,0:T(8,128)(2,1)S(1)}, u32[]{:S(2)}, u32[]{:S(2)}) collective-permute-start(bf16[6,128,128]{2,1,0:T(8,128)(2,1)} %get-tuple-element.37), channel_id=1, source_target_pairs={{0,1},{2,3},{4,5},{6,7},{8,9},{10,11},{12,13},{14,15},{16,17},{18,... | collective-permute-start | bytes 589832 | tf_op jit(solution)/shard_map/ppermute | solution.py:290
  9.2 1.3 %collective-permute-start.1 = (bf16[5,128,128]{2,1,0:T(8,128)(2,1)}, bf16[5,128,128]{2,1,0:T(8,128)(2,1)S(1)}, u32[]{:S(2)}, u32[]{:S(2)}) collective-permute-start(bf16[5,128,128]{2,1,0:T(8,128)(2,1)} %get-tuple-element.39), channel_id=1, source_target_pairs={{0,1},{2,3},{4,5},{6,7},{8,9},{10,11},{12,13},{14,15},{16,17},{18,... | collective-permute-start | bytes 491528 | tf_op jit(solution)/shard_map/ppermute | solution.py:290
  10.5 1.3 %collective-permute-start.2 = (bf16[5,128,128]{2,1,0:T(8,128)(2,1)}, bf16[5,128,128]{2,1,0:T(8,128)(2,1)S(1)}, u32[]{:S(2)}, u32[]{:S(2)}) collective-permute-start(bf16[5,128,128]{2,1,0:T(8,128)(2,1)} %get-tuple-element.41), channel_id=1, source_target_pairs={{0,1},{2,3},{4,5},{6,7},{8,9},{10,11},{12,13},{14,15},{16,17},{18,... | collective-permute-start | bytes 491528 | tf_op jit(solution)/shard_map/ppermute | solution.py:290
  12.5 2.3 %collective-permute-done.state.refs_11_ = bf16[6,128,128]{2,1,0:T(8,128)(2,1)S(1)} collective-permute-done((bf16[6,128,128]{2,1,0:T(8,128)(2,1)}, bf16[6,128,128]{2,1,0:T(8,128)(2,1)S(1)}, u32[]{:S(2)}, u32[]{:S(2)}) %collective-permute-start) | collective-permute-done | bytes 196640 | tf_op jit(solution)/shard_map/ppermute | solution.py:290
  14.8 0.0 copy-done
  14.8 0.0 copy-done.1
  14.8 0.0 copy-done.2
  14.8 0.0 copy-done.5
  14.8 0.0 copy-start.3
  14.8 1.0 %copy-done.3 = bf16[1,128,2048]{2,1,0:T(8,128)(2,1)S(1)} copy-done((bf16[1,128,2048]{2,1,0:T(8,128)(2,1)S(1)}, bf16[1,128,2048]{2,1,0:T(8,128)(2,1)}, u32[]{:S(2)}) %copy-start.3) | copy-done | bytes 524312
  15.9 3.3 %mix.3 = (bf16[128,768]{1,0:T(8,128)(2,1)S(1)}, bf16[128,768]{1,0:T(8,128)(2,1)S(1)}, bf16[6,128,128]{2,1,0:T(8,128)(2,1)}, f32[6,128]{1,0:T(8,128)S(1)}) custom-call(bf16[128,2048]{1,0:T(8,128)(2,1)S(1)} %bitcast.32, bf16[128,2048]{1,0:T(8,128)(2,1)S(1)} %bitcast.25, bf16[128,2048]{1,0:T(8,128)(2,1)S(1)} %bitcast.18, bf16[128,2048]{1,0:T(8,128)(2,1)S(1)} %bitcast.37, ...), custom_call_target="tpu_custom_call" | custom-call | flops 1000 | bytes 1000 | tf_op jit(solution)/shard_map/mix/pallas_call | solution.py:300
  19.1 1.3 %collective-permute-start.3 = (bf16[6,128,128]{2,1,0:T(8,128)(2,1)}, bf16[6,128,128]{2,1,0:T(8,128)(2,1)S(1)}, u32[]{:S(2)}, u32[]{:S(2)}) collective-permute-start(bf16[6,128,128]{2,1,0:T(8,128)(2,1)} %get-tuple-element.52), channel_id=1, source_target_pairs={{1,0},{3,2},{5,4},{7,6},{9,8},{11,10},{13,12},{15,14},{17,16},{19,... | collective-permute-start | bytes 589832 | tf_op jit(solution)/shard_map/ppermute | solution.py:290
  20.4 0.0 collective-permute-done.1.state.refs_12_
  20.4 2.9 %mix.4 = (bf16[128,640]{1,0:T(8,128)(2,1)S(1)}, bf16[128,640]{1,0:T(8,128)(2,1)S(1)}, bf16[5,128,128]{2,1,0:T(8,128)(2,1)}, f32[5,128]{1,0:T(8,128)S(1)}) custom-call(bf16[128,2048]{1,0:T(8,128)(2,1)S(1)} %bitcast.33, bf16[128,2048]{1,0:T(8,128)(2,1)S(1)} %bitcast.26, bf16[128,2048]{1,0:T(8,128)(2,1)S(1)} %bitcast.19, bf16[128,2048]{1,0:T(8,128)(2,1)S(1)} %bitcast.38, ...), custom_call_target="tpu_custom_call" | custom-call | flops 1000 | bytes 1000 | tf_op jit(solution)/shard_map/mix/pallas_call | solution.py:300
  23.3 1.3 %collective-permute-start.4 = (bf16[5,128,128]{2,1,0:T(8,128)(2,1)}, bf16[5,128,128]{2,1,0:T(8,128)(2,1)S(1)}, u32[]{:S(2)}, u32[]{:S(2)}) collective-permute-start(bf16[5,128,128]{2,1,0:T(8,128)(2,1)} %get-tuple-element.53), channel_id=1, source_target_pairs={{1,0},{3,2},{5,4},{7,6},{9,8},{11,10},{13,12},{15,14},{17,16},{19,... | collective-permute-start | bytes 491528 | tf_op jit(solution)/shard_map/ppermute | solution.py:290
  24.6 0.0 collective-permute-done.2.state.refs_13_
  24.6 2.9 %mix.5 = (bf16[128,640]{1,0:T(8,128)(2,1)S(1)}, bf16[128,640]{1,0:T(8,128)(2,1)S(1)}, bf16[5,128,128]{2,1,0:T(8,128)(2,1)}, f32[5,128]{1,0:T(8,128)S(1)}) custom-call(bf16[128,2048]{1,0:T(8,128)(2,1)S(1)} %bitcast.34, bf16[128,2048]{1,0:T(8,128)(2,1)S(1)} %bitcast.27, bf16[128,2048]{1,0:T(8,128)(2,1)S(1)} %bitcast.20, bf16[128,2048]{1,0:T(8,128)(2,1)S(1)} %bitcast.39, ...), custom_call_target="tpu_custom_call" | custom-call | flops 1000 | bytes 1000 | tf_op jit(solution)/shard_map/mix/pallas_call | solution.py:300
  27.5 0.0 copy-start.6
  27.5 0.7 %copy-done.6 = bf16[128,640]{1,0:T(8,128)(2,1)} copy-done((bf16[128,640]{1,0:T(8,128)(2,1)}, bf16[128,640]{1,0:T(8,128)(2,1)S(1)}, u32[]{:S(2)}) %copy-start.6) | copy-done | bytes 163864
  28.2 1.3 %collective-permute-start.5 = (bf16[5,128,128]{2,1,0:T(8,128)(2,1)}, bf16[5,128,128]{2,1,0:T(8,128)(2,1)S(1)}, u32[]{:S(2)}, u32[]{:S(2)}) collective-permute-start(bf16[5,128,128]{2,1,0:T(8,128)(2,1)} %get-tuple-element.54), channel_id=1, source_target_pairs={{1,0},{3,2},{5,4},{7,6},{9,8},{11,10},{13,12},{15,14},{17,16},{19,... | collective-permute-start | bytes 491528 | tf_op jit(solution)/shard_map/ppermute | solution.py:290
  29.4 0.0 copy-start.7
  29.5 0.9 %copy-done.7 = bf16[128,640]{1,0:T(8,128)(2,1)S(1)} copy-done((bf16[128,640]{1,0:T(8,128)(2,1)S(1)}, bf16[128,640]{1,0:T(8,128)(2,1)}, u32[]{:S(2)}) %copy-start.7) | copy-done | bytes 163864
  30.4 4.5 %back.1 = (bf16[128,2048]{1,0:T(8,128)(2,1)}, f32[128,2048]{1,0:T(8,128)S(1)}, f32[128,2048]{1,0:T(8,128)S(1)}, f32[128,2048]{1,0:T(8,128)S(1)}, f32[16,128]{1,0:T(8,128)S(1)}) custom-call(bf16[128,2048]{1,0:T(8,128)(2,1)S(1)} %bitcast.35, bf16[128,2048]{1,0:T(8,128)(2,1)S(1)} %bitcast.28, bf16[128,2048]{1,0:T(8,128)(2,1)S(1)} %bitcast.21, ...), custom_call_target="tpu_custom_call" | custom-call | flops 1000 | bytes 1000 | tf_op jit(solution)/shard_map/back/pallas_call | solution.py:319
  34.9 0.0 copy-start.8
  34.9 0.0 collective-permute-done.4.refs_1_
  34.9 0.7 %collective-permute-done.5.refs_2_ = bf16[5,128,128]{2,1,0:T(8,128)(2,1)S(1)} collective-permute-done((bf16[5,128,128]{2,1,0:T(8,128)(2,1)}, bf16[5,128,128]{2,1,0:T(8,128)(2,1)S(1)}, u32[]{:S(2)}, u32[]{:S(2)}) %collective-permute-start.5) | collective-permute-done | bytes 163872 | tf_op jit(solution)/shard_map/ppermute | solution.py:290
  35.6 0.0 collective-permute-done.3.refs_0_
  35.6 0.0 copy-done.8
  35.6 0.0 copy-start.4
  35.6 1.5 %logits.1 = (bf16[16,128]{1,0:T(8,128)(2,1)S(1)}, bf16[8,16,384]{2,1,0:T(8,128)(2,1)S(1)}, bf16[8,16,384]{2,1,0:T(8,128)(2,1)S(1)}) custom-call(bf16[128,2048]{1,0:T(8,128)(2,1)S(1)} %bitcast.36, bf16[128,2048]{1,0:T(8,128)(2,1)S(1)} %bitcast.29, bf16[128,2048]{1,0:T(8,128)(2,1)S(1)} %bitcast.22, f32[16,128]{1,0:T(8,128)S(1)} %copy-done.5, ...), custom_call_target="tpu_custom_call" | custom-call | flops 1000 | bytes 1000 | tf_op jit(solution)/shard_map/logits/pallas_call | solution.py:349
  37.1 0.1 collective-permute-start.6
  37.2 0.0 copy-done.4
  37.2 1.1 %finish.3 = bf16[128,2048]{1,0:T(8,128)(2,1)} custom-call(f32[128,2048]{1,0:T(8,128)S(1)} %get-tuple-element.57.gq, bf16[16,128]{1,0:T(8,128)(2,1)S(1)} %get-tuple-element.58.d_logits, bf16[16,6144]{1,0:T(8,128)(2,1)S(1)} %bitcast.41), custom_call_target="tpu_custom_call" | custom-call | flops 1000 | bytes 1000 | tf_op jit(solution)/shard_map/finish/pallas_call | solution.py:360
  38.3 0.2 collective-permute-done.6
  38.5 1.6 %collective-permute-start.7 = (bf16[4,16,384]{2,1,0:T(8,128)(2,1)S(1)}, bf16[4,16,384]{2,1,0:T(8,128)(2,1)S(1)}, u32[]{:S(2)}, u32[]{:S(2)}) collective-permute-start(bf16[4,16,384]{2,1,0:T(8,128)(2,1)S(1)} %slice.30), channel_id=1, source_target_pairs={{0,4},{2,6},{4,0},{6,2},{8,12},{10,14},{12,8},{14,10},{16,20},{18,... | collective-permute-start | bytes 147464 | tf_op jit(solution)/shard_map/ppermute | solution.py:381
  40.1 1.5 %finish.4 = bf16[128,2048]{1,0:T(8,128)(2,1)} custom-call(f32[128,2048]{1,0:T(8,128)S(1)} %get-tuple-element.61.gk, bf16[128,2048]{1,0:T(8,128)(2,1)S(1)} %bitcast.23, f32[16,128]{1,0:T(8,128)S(1)} %copy-done.5, bf16[16,128]{1,0:T(8,128)(2,1)S(1)} %get-tuple-element.58.d_logits, bf16[16,6144]{1,0:T(8,128)(2,1)S(1)} %bitcast.42, ...), custom_call_target="tpu_custom_call" | custom-call | flops 1000 | bytes 1000 | tf_op jit(solution)/shard_map/finish/pallas_call | solution.py:360
  41.6 1.0 %collective-permute-done.7 = bf16[4,16,384]{2,1,0:T(8,128)(2,1)S(1)} collective-permute-done((bf16[4,16,384]{2,1,0:T(8,128)(2,1)S(1)}, bf16[4,16,384]{2,1,0:T(8,128)(2,1)S(1)}, u32[]{:S(2)}, u32[]{:S(2)}) %collective-permute-start.7) | collective-permute-done | bytes 49184 | tf_op jit(solution)/shard_map/ppermute | solution.py:381
  42.7 1.6 %collective-permute-start.8 = (bf16[2,16,384]{2,1,0:T(8,128)(2,1)S(1)}, bf16[2,16,384]{2,1,0:T(8,128)(2,1)S(1)}, u32[]{:S(2)}, u32[]{:S(2)}) collective-permute-start(bf16[2,16,384]{2,1,0:T(8,128)(2,1)S(1)} %slice.32), channel_id=1, source_target_pairs={{0,8},{2,10},{4,12},{6,14},{8,0},{10,2},{12,4},{14,6},{16,24},{18,... | collective-permute-start | bytes 73736 | tf_op jit(solution)/shard_map/ppermute | solution.py:381
  44.3 1.4 %finish.5 = bf16[128,2048]{1,0:T(8,128)(2,1)} custom-call(f32[128,2048]{1,0:T(8,128)S(1)} %get-tuple-element.64.gv, bf16[128,2048]{1,0:T(8,128)(2,1)S(1)} %bitcast.30, f32[16,128]{1,0:T(8,128)S(1)} %copy-done.5, bf16[16,128]{1,0:T(8,128)(2,1)S(1)} %get-tuple-element.58.d_logits, bf16[16,6144]{1,0:T(8,128)(2,1)S(1)} %bitcast.43, ...), custom_call_target="tpu_custom_call" | custom-call | flops 1000 | bytes 1000 | tf_op jit(solution)/shard_map/finish/pallas_call | solution.py:360
  45.8 0.8 %collective-permute-done.8 = bf16[2,16,384]{2,1,0:T(8,128)(2,1)S(1)} collective-permute-done((bf16[2,16,384]{2,1,0:T(8,128)(2,1)S(1)}, bf16[2,16,384]{2,1,0:T(8,128)(2,1)S(1)}, u32[]{:S(2)}, u32[]{:S(2)}) %collective-permute-start.8) | collective-permute-done | bytes 24608 | tf_op jit(solution)/shard_map/ppermute | solution.py:381
  46.6 2.7 %collective-permute-start.9 = (bf16[1,16,384]{2,1,0:T(8,128)(2,1)S(1)}, bf16[1,16,384]{2,1,0:T(8,128)(2,1)S(1)}, u32[]{:S(2)}, u32[]{:S(2)}) collective-permute-start(bf16[1,16,384]{2,1,0:T(8,128)(2,1)S(1)} %slice.34), channel_id=1, source_target_pairs={{0,16},{2,18},{4,20},{6,22},{8,24},{10,26},{12,28},{14,30},{16,0},... | collective-permute-start | bytes 36872 | tf_op jit(solution)/shard_map/ppermute | solution.py:381
  49.3 2.0 %collective-permute-done.9 = bf16[1,16,384]{2,1,0:T(8,128)(2,1)S(1)} collective-permute-done((bf16[1,16,384]{2,1,0:T(8,128)(2,1)S(1)}, bf16[1,16,384]{2,1,0:T(8,128)(2,1)S(1)}, u32[]{:S(2)}, u32[]{:S(2)}) %collective-permute-start.9) | collective-permute-done | bytes 12320 | tf_op jit(solution)/shard_map/ppermute | solution.py:381
  51.3 2.7 %collective-permute-start.10 = (bf16[16,384]{1,0:T(8,128)(2,1)S(1)}, bf16[16,384]{1,0:T(8,128)(2,1)S(1)}, u32[]{:S(2)}, u32[]{:S(2)}) collective-permute-start(bf16[16,384]{1,0:T(8,128)(2,1)S(1)} %get-tuple-element.67), channel_id=1, source_target_pairs={{0,1},{1,0},{2,3},{3,2},{4,5},{5,4},{6,7},{7,6},{8,9},{9,8},{10,11... | collective-permute-start | bytes 36872 | tf_op jit(solution)/shard_map/ppermute | solution.py:393
  53.9 1.7 %collective-permute-done.10 = bf16[16,384]{1,0:T(8,128)(2,1)S(1)} collective-permute-done((bf16[16,384]{1,0:T(8,128)(2,1)S(1)}, bf16[16,384]{1,0:T(8,128)(2,1)S(1)}, u32[]{:S(2)}, u32[]{:S(2)}) %collective-permute-start.10) | collective-permute-done | bytes 12320 | tf_op jit(solution)/shard_map/ppermute | solution.py:393
  55.6 0.7 %fusion = f32[192,16]{0,1:T(8,128)} fusion(f32[16,384]{1,0:T(8,128)S(1)} %get-tuple-element.68, s32[]{:T(128)S(6)} %select_n.3, bf16[16,384]{1,0:T(8,128)(2,1)S(1)} %collective-permute-done.10), kind=kLoop, calls=%fused_computation.5 | loop fusion | flops 6144 | bytes 30724 | tf_op jit(solution)/shard_map/transpose | solution.py:396
  (8 shorter events, 0.1 us)
Async XLA Ops:
  0.6 14.2 %copy-start = (bf16[1,128,2048]{2,1,0:T(8,128)(2,1)S(1)}, bf16[1,128,2048]{2,1,0:T(8,128)(2,1)}, u32[]{:S(2)}) copy-start(bf16[1,128,2048]{2,1,0:T(8,128)(2,1)} %param.9) | copy-start | bytes 1572868
  0.6 14.2 %copy-start.1 = (bf16[1,128,2048]{2,1,0:T(8,128)(2,1)S(1)}, bf16[1,128,2048]{2,1,0:T(8,128)(2,1)}, u32[]{:S(2)}) copy-start(bf16[1,128,2048]{2,1,0:T(8,128)(2,1)} %param.8) | copy-start | bytes 1572868
  0.7 14.2 %copy-start.2 = (bf16[1,128,2048]{2,1,0:T(8,128)(2,1)S(1)}, bf16[1,128,2048]{2,1,0:T(8,128)(2,1)}, u32[]{:S(2)}) copy-start(bf16[1,128,2048]{2,1,0:T(8,128)(2,1)} %param.7) | copy-start | bytes 1572868
  4.3 10.5 %copy-start.5 = (f32[16,128]{1,0:T(8,128)S(1)}, f32[16,128]{1,0:T(8,128)}, u32[]{:S(2)}) copy-start(f32[16,128]{1,0:T(8,128)} %get-tuple-element.36.cum_ref.refs_3_) | copy-start | bytes 24580
  4.3 10.5 %collective-permute-start = (bf16[6,128,128]{2,1,0:T(8,128)(2,1)}, bf16[6,128,128]{2,1,0:T(8,128)(2,1)S(1)}, u32[]{:S(2)}, u32[]{:S(2)}) collective-permute-start(bf16[6,128,128]{2,1,0:T(8,128)(2,1)} %get-tuple-element.37), channel_id=1, source_target_pairs={{0,1},{2,3},{4,5},{6,7},{8,9},{10,11},{12,13},{14,15},{16,17},{18,... | collective-permute-start | bytes 589832 | tf_op jit(solution)/shard_map/ppermute | solution.py:290
  9.2 11.2 %collective-permute-start.1 = (bf16[5,128,128]{2,1,0:T(8,128)(2,1)}, bf16[5,128,128]{2,1,0:T(8,128)(2,1)S(1)}, u32[]{:S(2)}, u32[]{:S(2)}) collective-permute-start(bf16[5,128,128]{2,1,0:T(8,128)(2,1)} %get-tuple-element.39), channel_id=1, source_target_pairs={{0,1},{2,3},{4,5},{6,7},{8,9},{10,11},{12,13},{14,15},{16,17},{18,... | collective-permute-start | bytes 491528 | tf_op jit(solution)/shard_map/ppermute | solution.py:290
  10.5 14.1 %collective-permute-start.2 = (bf16[5,128,128]{2,1,0:T(8,128)(2,1)}, bf16[5,128,128]{2,1,0:T(8,128)(2,1)S(1)}, u32[]{:S(2)}, u32[]{:S(2)}) collective-permute-start(bf16[5,128,128]{2,1,0:T(8,128)(2,1)} %get-tuple-element.41), channel_id=1, source_target_pairs={{0,1},{2,3},{4,5},{6,7},{8,9},{10,11},{12,13},{14,15},{16,17},{18,... | collective-permute-start | bytes 491528 | tf_op jit(solution)/shard_map/ppermute | solution.py:290
  14.8 1.0 %copy-start.3 = (bf16[1,128,2048]{2,1,0:T(8,128)(2,1)S(1)}, bf16[1,128,2048]{2,1,0:T(8,128)(2,1)}, u32[]{:S(2)}) copy-start(bf16[1,128,2048]{2,1,0:T(8,128)(2,1)} %param.13) | copy-start | bytes 1572868
  19.1 16.5 %collective-permute-start.3 = (bf16[6,128,128]{2,1,0:T(8,128)(2,1)}, bf16[6,128,128]{2,1,0:T(8,128)(2,1)S(1)}, u32[]{:S(2)}, u32[]{:S(2)}) collective-permute-start(bf16[6,128,128]{2,1,0:T(8,128)(2,1)} %get-tuple-element.52), channel_id=1, source_target_pairs={{1,0},{3,2},{5,4},{7,6},{9,8},{11,10},{13,12},{15,14},{17,16},{19,... | collective-permute-start | bytes 589832 | tf_op jit(solution)/shard_map/ppermute | solution.py:290
  23.3 11.5 %collective-permute-start.4 = (bf16[5,128,128]{2,1,0:T(8,128)(2,1)}, bf16[5,128,128]{2,1,0:T(8,128)(2,1)S(1)}, u32[]{:S(2)}, u32[]{:S(2)}) collective-permute-start(bf16[5,128,128]{2,1,0:T(8,128)(2,1)} %get-tuple-element.53), channel_id=1, source_target_pairs={{1,0},{3,2},{5,4},{7,6},{9,8},{11,10},{13,12},{15,14},{17,16},{19,... | collective-permute-start | bytes 491528 | tf_op jit(solution)/shard_map/ppermute | solution.py:290
  27.5 0.7 %copy-start.6 = (bf16[128,640]{1,0:T(8,128)(2,1)}, bf16[128,640]{1,0:T(8,128)(2,1)S(1)}, u32[]{:S(2)}) copy-start(bf16[128,640]{1,0:T(8,128)(2,1)S(1)} %get-tuple-element.45.refs_10_) | copy-start | bytes 491524
  28.2 7.4 %collective-permute-start.5 = (bf16[5,128,128]{2,1,0:T(8,128)(2,1)}, bf16[5,128,128]{2,1,0:T(8,128)(2,1)S(1)}, u32[]{:S(2)}, u32[]{:S(2)}) collective-permute-start(bf16[5,128,128]{2,1,0:T(8,128)(2,1)} %get-tuple-element.54), channel_id=1, source_target_pairs={{1,0},{3,2},{5,4},{7,6},{9,8},{11,10},{13,12},{15,14},{17,16},{19,... | collective-permute-start | bytes 491528 | tf_op jit(solution)/shard_map/ppermute | solution.py:290
  29.4 0.9 %copy-start.7 = (bf16[128,640]{1,0:T(8,128)(2,1)S(1)}, bf16[128,640]{1,0:T(8,128)(2,1)}, u32[]{:S(2)}) copy-start(bf16[128,640]{1,0:T(8,128)(2,1)} %copy-done.6) | copy-start | bytes 491524
  34.9 0.7 %copy-start.8 = (f32[16,128]{1,0:T(8,128)S(1)}, f32[16,128]{1,0:T(8,128)}, u32[]{:S(2)}) copy-start(f32[16,128]{1,0:T(8,128)} %get-tuple-element.50.logits_ref) | copy-start | bytes 24580
  35.6 1.6 %copy-start.4 = (bf16[6144,16]{0,1:T(8,128)(2,1)S(1)}, bf16[6144,16]{0,1:T(8,128)(2,1)}, u32[]{:S(2)}) copy-start(bf16[6144,16]{0,1:T(8,128)(2,1)} %param.11) | copy-start | bytes 589828
  37.1 1.4 %collective-permute-start.6 = (bf16[8,16,384]{2,1,0:T(8,128)(2,1)S(1)}, bf16[8,16,384]{2,1,0:T(8,128)(2,1)S(1)}, u32[]{:S(2)}, u32[]{:S(2)}) collective-permute-start(bf16[8,16,384]{2,1,0:T(8,128)(2,1)S(1)} %get-tuple-element.56), channel_id=1, source_target_pairs={{0,2},{2,0},{4,6},{6,4},{8,10},{10,8},{12,14},{14,12},{16,18},{18,... | collective-permute-start | bytes 294920 | tf_op jit(solution)/shard_map/ppermute | solution.py:381
  38.5 4.2 %collective-permute-start.7 = (bf16[4,16,384]{2,1,0:T(8,128)(2,1)S(1)}, bf16[4,16,384]{2,1,0:T(8,128)(2,1)S(1)}, u32[]{:S(2)}, u32[]{:S(2)}) collective-permute-start(bf16[4,16,384]{2,1,0:T(8,128)(2,1)S(1)} %slice.30), channel_id=1, source_target_pairs={{0,4},{2,6},{4,0},{6,2},{8,12},{10,14},{12,8},{14,10},{16,20},{18,... | collective-permute-start | bytes 147464 | tf_op jit(solution)/shard_map/ppermute | solution.py:381
  42.7 3.9 %collective-permute-start.8 = (bf16[2,16,384]{2,1,0:T(8,128)(2,1)S(1)}, bf16[2,16,384]{2,1,0:T(8,128)(2,1)S(1)}, u32[]{:S(2)}, u32[]{:S(2)}) collective-permute-start(bf16[2,16,384]{2,1,0:T(8,128)(2,1)S(1)} %slice.32), channel_id=1, source_target_pairs={{0,8},{2,10},{4,12},{6,14},{8,0},{10,2},{12,4},{14,6},{16,24},{18,... | collective-permute-start | bytes 73736 | tf_op jit(solution)/shard_map/ppermute | solution.py:381
  46.6 4.7 %collective-permute-start.9 = (bf16[1,16,384]{2,1,0:T(8,128)(2,1)S(1)}, bf16[1,16,384]{2,1,0:T(8,128)(2,1)S(1)}, u32[]{:S(2)}, u32[]{:S(2)}) collective-permute-start(bf16[1,16,384]{2,1,0:T(8,128)(2,1)S(1)} %slice.34), channel_id=1, source_target_pairs={{0,16},{2,18},{4,20},{6,22},{8,24},{10,26},{12,28},{14,30},{16,0},... | collective-permute-start | bytes 36872 | tf_op jit(solution)/shard_map/ppermute | solution.py:381
  51.3 4.3 %collective-permute-start.10 = (bf16[16,384]{1,0:T(8,128)(2,1)S(1)}, bf16[16,384]{1,0:T(8,128)(2,1)S(1)}, u32[]{:S(2)}, u32[]{:S(2)}) collective-permute-start(bf16[16,384]{1,0:T(8,128)(2,1)S(1)} %get-tuple-element.67), channel_id=1, source_target_pairs={{0,1},{1,0},{2,3},{3,2},{4,5},{5,4},{6,7},{7,6},{8,9},{9,8},{10,11... | collective-permute-start | bytes 36872 | tf_op jit(solution)/shard_map/ppermute | solution.py:393

commit v3 on v2

v3 whole, which is shorter than its diff:
```python
import functools

import jax
import jax.numpy as jnp
from jax import lax
from jax.experimental import pallas as pl
from jax.experimental.pallas import tpu as pltpu
from jax.sharding import PartitionSpec as P

EPSILON = 1e-06
F32 = jnp.float32
BF16 = jnp.bfloat16
STAGE = 8
VMEM_LIMIT = 16 * 1024 * 1024
VMEM_FULL = 51 * 1024 * 1024


def dot_nn(a, b):
    return lax.dot_general(a, b, (((1,), (0,)), ((), ())), preferred_element_type=F32)


def dot_nt(a, b):
    return lax.dot_general(a, b, (((1,), (1,)), ((), ())), preferred_element_type=F32)


def dot_tn(a, b):
    return lax.dot_general(a, b, (((0,), (0,)), ((), ())), preferred_element_type=F32)


def exact_dot(x, ones):
    rows = x.shape[0]
    high = x.astype(BF16)
    rest = x - high.astype(F32)
    middle = rest.astype(BF16)
    low = (rest - middle.astype(F32)).astype(BF16)
    parts = dot_nn(jnp.concatenate([high, middle, low], axis=0), ones)
    return parts[:rows] + parts[rows : 2 * rows] + parts[2 * rows :]


def triangle(size, upper):
    rows = lax.broadcasted_iota(jnp.int32, (size, size), 0)
    columns = lax.broadcasted_iota(jnp.int32, (size, size), 1)
    keep = rows <= columns if upper else rows >= columns
    return jnp.where(keep, 1.0, 0.0).astype(BF16)


def decay_matrix(cum_column, cum_row):
    size = cum_row.shape[1]
    rows = lax.broadcasted_iota(jnp.int32, (size, size), 0)
    columns = lax.broadcasted_iota(jnp.int32, (size, size), 1)
    return jnp.exp(jnp.where(columns <= rows, cum_column - cum_row, -jnp.inf))


def spec():
    return pl.BlockSpec(memory_space=pltpu.VMEM)


def smem():
    return pl.BlockSpec(memory_space=pltpu.SMEM)


def hbm():
    return pl.BlockSpec(memory_space=pltpu.HBM)


def params(limit=VMEM_LIMIT):
    return pltpu.CompilerParams(vmem_limit_bytes=limit)


def cost():
    return pl.CostEstimate(flops=1000, bytes_accessed=1000, transcendentals=0)


def head_lanes(size, first, count):
    return [slice(h * size, (h + 1) * size) for h in range(first, first + count)]


def add_updates(k, v, cum, groups, outs):
    size = outs[0].shape[1]
    fading = jnp.exp(cum[:, cum.shape[1] - 1 :] - cum)
    for (first, count), out in zip(groups, outs):
        parts = head_lanes(size, first, count)
        turned = [k[:, p].astype(F32).T for p in parts]
        faded = [(t * fading[first + i : first + i + 1, :]).astype(BF16) for i, t in enumerate(turned)]
        products = [dot_nn(f, v[:, p]) for f, p in zip(faded, parts)]
        for i, product in enumerate(products):
            out[i] = product.astype(BF16)


def gate_kernel(groups, q_in, k_in, v_in, cot_in, bias_in, gate_in, resets, *refs):
    logits_ref, cum_ref, rise_ref, *updates = refs[: 3 + len(groups)]
    q, k, v, cot, bias, gate, sems = refs[3 + len(groups) :]
    pairs = ((gate_in, gate), (bias_in, bias), (k_in, k), (q_in, q), (v_in, v), (cot_in, cot))
    copies = [
        pltpu.make_async_copy(source, target, sems.at[i])
        for i, (source, target) in enumerate(pairs)
    ]
    for copy in copies[:5]:
        copy.start()
    width = q.shape[1]
    for copy in copies[:3]:
        copy.wait()
    logits = bias[...] + dot_nt(gate[:, width : 2 * width], k[...])
    copies[3].wait()
    logits = logits + dot_nt(gate[:, :width], q[...])
    copies[4].wait()
    copies[5].start()
    logits = logits + dot_nt(gate[:, 2 * width :], v[...])
    logits_ref[...] = logits
    soft = jnp.maximum(logits, 0.0) + jnp.log1p(jnp.exp(-jnp.abs(logits)))
    cum = exact_dot(-soft, triangle(logits.shape[1], True))
    cum_ref[...] = cum
    rise_ref[...] = (1 - resets[0, 0]).astype(F32) * jnp.exp(cum)
    add_updates(k, v, cum, groups, updates)
    copies[5].wait()


def within_kernel(heads, q, k, v, cum_ref, attn_ref, within):
    size = q.shape[1] // heads
    cum_columns = cum_ref[...].T
    step = min(heads, STAGE)
    for first in range(0, heads, step):
        count = min(step, heads - first)
        parts = head_lanes(size, first, count)
        scores = [dot_nt(q[:, p], k[:, p]) for p in parts]
        attns = [
            (decay_matrix(cum_columns[:, h : h + 1], cum_ref[h : h + 1, :]) * s).astype(BF16)
            for h, s in enumerate(scores, first)
        ]
        for h, a in enumerate(attns, first):
            attn_ref[h] = a
        for a, p in zip(attns, parts):
            within[:, p] = dot_nn(a, v[:, p])


def mix_kernel(first, count, q, within, cot, rise_ref, state, *refs):
    *forwarded, out, d_mix, pushed, row_ref = refs
    size = state.shape[1]
    opening = lax.axis_index("seq") == 0
    parts, owns = head_lanes(size, first, count), head_lanes(size, 0, count)
    rise = rise_ref[...][first : first + count]
    decays = jnp.where(opening, 0.0, rise).T
    reads = [dot_nn(q[:, p], state[i]) for i, p in enumerate(parts)]
    mixtures = [
        within[:, p] + decays[:, i : i + 1] * x for i, (p, x) in enumerate(zip(parts, reads))
    ]
    upstream = [cot[:, p].astype(F32) for p in parts]
    squares = [jnp.mean(m * m, axis=1, keepdims=True) + EPSILON for m in mixtures]
    shared = [jnp.mean(u * m, axis=1, keepdims=True) for u, m in zip(upstream, mixtures)]
    inverses = [lax.rsqrt(s) for s in squares]
    normed = [m * i for m, i in zip(mixtures, inverses)]
    for n, o in zip(normed, owns):
        out[:, o] = n.astype(BF16)
    grads = [
        ((u - n * (s * i)) * i).astype(BF16)
        for u, n, s, i in zip(upstream, normed, shared, inverses)
    ]
    for g, o in zip(grads, owns):
        d_mix[:, o] = g
    faded = [
        (q[:, p].astype(F32).T * rise[i : i + 1, :]).astype(BF16) for i, p in enumerate(parts)
    ]
    products = [dot_nn(f, g) for f, g in zip(faded, grads)]
    for i, product in enumerate(products):
        product = product.astype(BF16)
        if forwarded:
            product = jnp.where(opening, forwarded[0][i], product)
        pushed[i] = product
    terms = [
        jnp.sum(g.astype(F32) * m, axis=1, keepdims=True) for g, m in zip(grads, mixtures)
    ]
    row_ref[...] = jnp.concatenate(terms, axis=1).T


def members(groups):
    return [(g, i) for g, (_, count) in enumerate(groups) for i in range(count)]


def back_kernel(groups, *refs):
    q, k, v, attn, cum_ref, rise_ref = refs[:6]
    number = len(groups)
    outs, d_mixes, states, row_terms = [refs[6 + number * i : 6 + number * (i + 1)] for i in range(4)]
    output, gq, gk, gv, term_ref, sems = refs[6 + 4 * number :]
    size = states[0].shape[1]
    copies = [
        pltpu.make_async_copy(
            out, output.at[:, pl.ds(first * size, count * size)], sems.at[i]
        )
        for i, ((first, count), out) in enumerate(zip(groups, outs))
    ]
    for copy in copies:
        copy.start()
    cum_columns = cum_ref[...].T
    rise_columns = jnp.where(lax.axis_index("seq") == 0, 0.0, rise_ref[...]).T
    sums = []
    places = members(groups)
    for start in range(0, len(places), STAGE):
        some = places[start : start + STAGE]
        heads = range(start, start + len(some))
        parts = head_lanes(size, start, len(some))
        grads = [d_mixes[g][:, i * size : (i + 1) * size] for g, i in some]
        columns = [cum_columns[:, h : h + 1] for h in heads]
        d_attns = [dot_nt(d, v[:, p]) for d, p in zip(grads, parts)]
        reads = [dot_nt(d, states[g][i]) for d, (g, i) in zip(grads, some)]
        weighted = [
            (decay_matrix(c, cum_ref[h : h + 1, :]) * d).astype(BF16)
            for h, c, d in zip(heads, columns, d_attns)
        ]
        for h, p, w, x in zip(heads, parts, weighted, reads):
            gq[:, p] = dot_nn(w, k[:, p]) + rise_columns[:, h : h + 1] * x
        for p, w in zip(parts, weighted):
            gk[:, p] = dot_tn(w, q[:, p])
        for h, p, d in zip(heads, parts, grads):
            gv[:, p] = dot_tn(attn[h], d)
        for h, d in zip(heads, d_attns):
            sums.append(jnp.sum(attn[h].astype(F32) * d, axis=0, keepdims=True))
    term_ref[...] = jnp.concatenate([r[...] for r in row_terms], axis=0) - jnp.concatenate(
        sums, axis=0
    )
    for copy in copies:
        copy.wait()


def logit_kernel(groups, order, slots, q, k, v, cum_ref, logits_ref, terms, through, *refs):
    grads = refs[: len(groups)]
    d_ref, *outs = refs[len(groups) :]
    size = grads[0].shape[1]
    width = q.shape[1]
    cum = cum_ref[...]
    tokens = cum.shape[1]
    totals = cum[:, tokens - 1 :]
    parts = head_lanes(size, 0, cum.shape[0])
    moved = [dot_nt(v[:, p], grads[g][i]) for p, (g, i) in zip(parts, members(groups))]
    sums = [jnp.sum(k[:, p].astype(F32) * m, axis=1, keepdims=True) for p, m in zip(parts, moved)]
    closing = lax.axis_index("seq") == slots - 1
    from_state = jnp.concatenate(sums, axis=1).T * jnp.where(closing, 0.0, jnp.exp(totals - cum))
    ends = jnp.sum(from_state, axis=1, keepdims=True) + jnp.exp(totals) * through[...]
    last = lax.broadcasted_iota(jnp.int32, cum.shape, 1) == tokens - 1
    d_cum = terms[...] - from_state + jnp.where(last, ends, 0.0)
    d_decay = exact_dot(d_cum, triangle(tokens, False))
    d_logits = (-jax.nn.sigmoid(logits_ref[...]) * d_decay).astype(BF16)
    d_ref[...] = d_logits
    whole = [dot_nn(d_logits, x[...]) for x in (q, k, v)]
    if order is None:
        for i in range(3):
            outs[0][:, i * width : (i + 1) * width] = whole[i]
        return
    keep, send, pieces = outs
    chunks, _, share = pieces.shape
    joined = jnp.concatenate([w.astype(BF16) for w in whole], axis=1)
    for j in range(chunks):
        pieces[j] = joined[:, j * share : (j + 1) * share]
    mine = lax.axis_index("dp")
    half = chunks // 2
    for position in range(chunks):
        relative = sum(mask for bit, mask in enumerate(order) if position & (chunks >> (bit + 1)))
        piece = pieces[mine ^ relative]
        if position < half:
            keep[position] = piece
        else:
            send[position - half] = piece


def finish_kernel(groups, index, rows, slots, partial, d_logits, gate, *refs):
    *refs, out, result, sems = refs
    width = partial.shape[1]
    places = members(groups)
    size = width // len(places)
    if rows is not None:
        operand, cum_ref, *grads = refs
        cum = cum_ref[...]
        closing = lax.axis_index("seq") == slots - 1
        fading = jnp.where(closing, 0.0, jnp.exp(cum[:, cum.shape[1] - 1 :] - cum)).T
    copies = []
    for start in range(0, len(places), STAGE):
        some = places[start : start + STAGE]
        lanes = slice(start * size, (start + len(some)) * size)
        at = index * width + start * size
        back = dot_tn(d_logits[...], gate[:, at : at + len(some) * size])
        if rows is None:
            result[:, lanes] = (partial[:, lanes] + back).astype(BF16)
        else:
            parts, owns = head_lanes(size, start, len(some)), head_lanes(size, 0, len(some))
            moved = [rows(operand[:, p], grads[g][i]) for p, (g, i) in zip(parts, some)]
            for i, (p, o, m) in enumerate(zip(parts, owns, moved)):
                h = start + i
                total = partial[:, p] + fading[:, h : h + 1] * m + back[:, o]
                result[:, p] = total.astype(BF16)
        at = pl.ds(start * size, len(some) * size)
        copies.append(
            pltpu.make_async_copy(result.at[:, at], out.at[:, at], sems.at[start // STAGE])
        )
        copies[-1].start()
    for copy in copies:
        copy.wait()


def shape(dims, dtype):
    return jax.ShapeDtypeStruct(dims, dtype)


def head_groups(heads):
    parts = 4 if heads >= 4 else 1
    sizes = [heads // parts + (1 if i < heads % parts else 0) for i in range(parts)]
    return [(sum(sizes[:i]), sizes[i]) for i in range(parts)]


def body(dp_size, seq_size, queries, keys, values, decay_bias, gate_matrix, resets, cotangent):
    q, k, v, cot = queries[0], keys[0], values[0], cotangent[0]
    tokens, width = q.shape
    heads = decay_bias.shape[1]
    size = width // heads
    gate = gate_matrix.T
    groups = head_groups(heads)
    forward = [(i, i + 1) for i in range(seq_size - 1)]
    backward = [(i + 1, i) for i in range(seq_size - 1)]
    slot = lax.axis_index("seq")
    kept = (1 - resets[0, 0]).astype(F32)

    def state_shapes(some):
        return tuple(shape((count, size, size), BF16) for _, count in some)

    logits, cum, rise, *made = pl.pallas_call(
        functools.partial(gate_kernel, groups),
        out_shape=(shape((heads, tokens), F32),) * 3
        + state_shapes(groups)
        + (shape((tokens, width), BF16),) * 4,
        in_specs=[hbm()] * 6 + [smem()],
        out_specs=(spec(),) * (7 + len(groups)),
        scratch_shapes=[
            pltpu.VMEM((heads, tokens), F32),
            pltpu.VMEM((heads, 3 * width), BF16),
            pltpu.SemaphoreType.DMA((6,)),
        ],
        compiler_params=params(VMEM_FULL),
        cost_estimate=cost(),
        name="gate",
    )(q, k, v, cot, decay_bias[0], gate, resets)
    *updates, q, k, v, cot = made

    def chain(own, first, count, pairs):
        if seq_size == 2:
            return lax.ppermute(own, "seq", [(0, 1), (1, 0)])
        arrived = lax.ppermute(own, "seq", pairs)
        for _ in range(seq_size - 2):
            factor = kept * jnp.exp(cum[first : first + count, -1])[:, None, None]
            passed = factor * arrived.astype(F32) + own.astype(F32)
            arrived = lax.ppermute(passed.astype(BF16), "seq", pairs)
        return arrived

    ahead = 2 if seq_size == 2 and len(groups) == 4 else len(groups)
    entering = [chain(updates[g], *groups[g], forward) for g in range(min(ahead, len(groups)))]
    attn, within = pl.pallas_call(
        functools.partial(within_kernel, heads),
        out_shape=(shape((heads, tokens, tokens), BF16), shape((tokens, width), F32)),
        in_specs=[spec()] * 4,
        out_specs=(spec(),) * 2,
        compiler_params=params(),
        cost_estimate=cost(),
        name="within",
    )(q, k, v, cum)
    outs, d_mixes, rows, grads = [], [], [], []
    for g, (first, count) in enumerate(groups):
        forwarded = [updates[g + ahead]] if g + ahead < len(groups) else []
        out_g, d_g, pushed, rows_g = pl.pallas_call(
            functools.partial(mix_kernel, first, count),
            out_shape=(
                shape((tokens, count * size), BF16),
                shape((tokens, count * size), BF16),
                shape((count, size, size), BF16),
                shape((count, tokens), F32),
            ),
            in_specs=[spec()] * (5 + len(forwarded)),
            out_specs=(spec(),) * 4,
            compiler_params=params(),
            cost_estimate=cost(),
            name="mix",
        )(q, within, cot, rise, entering[g], *forwarded)
        outs.append(out_g)
        d_mixes.append(d_g)
        rows.append(rows_g)
        if forwarded:
            arrived = lax.ppermute(pushed, "seq", [(0, 1), (1, 0)])
            entering.append(arrived)
            grads.append(arrived)
        else:
            grads.append(chain(pushed, first, count, backward))

    output, gq, gk, gv, terms = pl.pallas_call(
        functools.partial(back_kernel, groups),
        out_shape=(shape((tokens, width), BF16),)
        + (shape((tokens, width), F32),) * 3
        + (shape((heads, tokens), F32),),
        in_specs=[spec()] * (6 + 4 * len(groups)),
        out_specs=(hbm(),) + (spec(),) * 4,
        scratch_shapes=[pltpu.SemaphoreType.DMA((len(groups),))],
        compiler_params=params(),
        cost_estimate=cost(),
        name="back",
    )(q, k, v, attn, cum, rise, *outs, *d_mixes, *entering, *rows)
    if seq_size > 2:
        through = [
            kept * jnp.sum(g.astype(F32) * s.astype(F32), axis=(1, 2))[:, None]
            for g, s in zip(grads, entering)
        ]
        through = jnp.concatenate(through, axis=0)
    else:
        through = jnp.zeros((heads, 1), F32)

    share = 3 * width // dp_size
    halving = (
        dp_size > 1 and dp_size & (dp_size - 1) == 0 and share % 128 == 0 and seq_size == 2
    )
    order = [1 << b for b in range(dp_size.bit_length() - 1)] if halving else None
    if halving:
        part_shapes = (shape((dp_size // 2, heads, share), BF16),) * 2
        scratch = [pltpu.VMEM((dp_size, heads, share), BF16)]
    else:
        part_shapes = (shape((heads, 3 * width), F32),)
        scratch = []
    d_logits, *parts = pl.pallas_call(
        functools.partial(logit_kernel, groups, order, seq_size),
        out_shape=(shape((heads, tokens), BF16),) + part_shapes,
        in_specs=[spec()] * (7 + len(groups)),
        out_specs=(spec(),) * (1 + len(part_shapes)),
        scratch_shapes=scratch,
        compiler_params=params(),
        cost_estimate=cost(),
        name="logits",
    )(q, k, v, cum, logits, terms, through, *grads)

    def finish(index, rows, partial, *extra):
        return pl.pallas_call(
            functools.partial(finish_kernel, groups, index, rows, seq_size),
            out_shape=shape((tokens, width), BF16),
            in_specs=[spec()] * (3 + len(extra)),
            out_specs=hbm(),
            scratch_shapes=[
                pltpu.VMEM((tokens, width), BF16),
                pltpu.SemaphoreType.DMA((-(-heads // STAGE),)),
            ],
            compiler_params=params(),
            cost_estimate=cost(),
            name="finish",
        )(partial, d_logits, gate, *extra)

    grad_q = finish(0, None, gq)
    grad_k = finish(1, dot_nt, gk, v, cum, *grads)
    grad_v = finish(2, dot_nn, gv, k, cum, *grads)

    if halving:
        keep, send = parts
        for step, mask in enumerate(order):
            arrived = lax.ppermute(send, "dp", [(i, i ^ mask) for i in range(dp_size)])
            total = keep.astype(F32) + arrived.astype(F32)
            half = total.shape[0] // 2
            if half:
                keep, send = total[:half].astype(BF16), total[half:].astype(BF16)
            if step == 1:
                send, grad_q = lax.optimization_barrier((send, grad_q))
            elif step == 2:
                send, grad_k = lax.optimization_barrier((send, grad_k))
            elif step == 3:
                total, grad_v = lax.optimization_barrier((total, grad_v))
        total = total[0]
        arrived = lax.ppermute(total.astype(BF16), "seq", [(0, 1), (1, 0)])
        total = total + arrived.astype(F32)
        piece = share // seq_size
        grad_gate = lax.dynamic_slice_in_dim(total, slot * piece, piece, axis=1).T
    else:
        grad_gate = lax.psum_scatter(
            parts[0].T, ("dp", "seq"), scatter_dimension=0, tiled=True
        )
    return output[None], grad_q[None], grad_k[None], grad_v[None], grad_gate


def solution(mesh):
    rows = P("dp", "seq", None)
    return jax.shard_map(
        functools.partial(body, mesh.shape["dp"], mesh.shape["seq"]),
        mesh=mesh,
        in_specs=(rows, rows, rows, P("dp", None, "seq"), P(), P("dp", "seq"), rows),
        out_specs=(rows, rows, rows, rows, P(("dp", "seq"), None)),
        check_vma=False,
    )
```

time: 56.6 us -> 48.4 us (0.86)
  Pallas kernels: 22.7 us -> 13.7 us
  waiting for transfers between devices: 8.75 us -> 12.5 us
  local copies, waits for them, and re-layouts: 2.66 us -> 0.97 us
  starting transfers between devices: 19.9 us -> 18.9 us
    pallas_call x3 -> x4, Pallas kernels: 9.03 us -> 2.63 us  [body(): pl.pallas_call(functools.partial(mix_kernel, first, count), out_shape=(sh...]
    ppermute x6, waiting for transfers between devices: 3.07 us -> 6.7 us  [the longest x4 4.57 us: chain(): return lax.ppermute(own, 'seq', [(0, 1), (1, 0)])]
    pallas_call x6 -> x7, Pallas kernels: 13.7 us -> 11 us  [the longest x3 3.78 us: finish(): pl.pallas_call(functools.partial(finish_kernel, groups, index, rows, seq_...]
    unnamed x18 -> x4, local copies, waits for them, and re-layouts: 2.64 us -> 0.96 us
    ppermute x1, starting transfers between devices: 2.66 us -> 1.74 us  [body(): arrived = lax.ppermute(total.astype(BF16), 'seq', [(0, 1), (1, 0)])]
    ppermute x6, starting transfers between devices: 11.3 us -> 10.6 us  [the longest x4 7.06 us: chain(): return lax.ppermute(own, 'seq', [(0, 1), (1, 0)])]
  transfers between devices with their start and end apart: 11 -> 11, of which waited for: 7 -> 9; matrix products, arithmetic and copies ran while one was open for 0% -> 0% of each run, Pallas kernels for 31% -> 19%
where the time goes in v3:
time: 48.4 us; the launch traced here: 48.2 us
  starting transfers between devices  18.9 us (39%)
  Pallas kernels  13.7 us (28%)
  waiting for transfers between devices  12.5 us (26%)
  between operations  1.42 us (3%)
  local copies, waits for them, and re-layouts  0.97 us (2%)
  other arithmetic  0.75 us (2%)
    ppermute x4, starting transfers between devices, chain(): return lax.ppermute(own, 'seq', [(0, 1), (1, 0)])  7.06 us
    ppermute x4, starting transfers between devices, body(): arrived = lax.ppermute(send, 'dp', [(i, i ^ mask) for i in range(dp_size)])  6.5 us
    ppermute x4, waiting for transfers between devices, chain(): return lax.ppermute(own, 'seq', [(0, 1), (1, 0)])  4.57 us
    pallas_call x3, Pallas kernels, finish(): pl.pallas_call(functools.partial(finish_kernel, groups, index, rows, seq_...  3.78 us
    ppermute x4, waiting for transfers between devices, body(): arrived = lax.ppermute(send, 'dp', [(i, i ^ mask) for i in range(dp_size)])  3.76 us
    ppermute x2, starting transfers between devices, body(): arrived = lax.ppermute(pushed, 'seq', [(0, 1), (1, 0)])  3.58 us
    pallas_call x1, Pallas kernels, body(): pl.pallas_call(functools.partial(gate_kernel, groups), out_shape=(shape((...  3.03 us
    pallas_call x4, Pallas kernels, body(): pl.pallas_call(functools.partial(mix_kernel, first, count), out_shape=(sh...  2.63 us
  transfers between devices with their start and end apart: 11, of which 9 were waited for; matrix products, arithmetic and copies ran while one was open for 0% of the time, Pallas kernels for 19%

profile of v3, /device:TPU:0, one launch (start us, length us, event | category | flops | bytes accessed | tf_op | source)
XLA Modules:
  0.0 48.2 jit_solution(16589554848896763539)
XLA Ops:
  0.6 0.0 copy-start.1
  1.3 0.0 copy-done.1
  1.3 0.0 copy-start
  1.3 0.9 %copy-done = bf16[6144,16]{0,1:T(8,128)(2,1)S(1)} copy-done((bf16[6144,16]{0,1:T(8,128)(2,1)S(1)}, bf16[6144,16]{0,1:T(8,128)(2,1)}, u32[]{:S(2)}) %copy-start) | copy-done | bytes 196632
  2.3 3.0 %gate.1 = (f32[16,128]{1,0:T(8,128)S(1)}, f32[16,128]{1,0:T(8,128)S(1)}, f32[16,128]{1,0:T(8,128)S(1)}, bf16[4,128,128]{2,1,0:T(8,128)(2,1)S(1)}, bf16[4,128,128...) custom-call(bf16[128,2048]{1,0:T(8,128)(2,1)} %bitcast.19, ...), custom_call_target="tpu_custom_call" | custom-call | flops 1000 | bytes 1000 | tf_op jit(solution)/shard_map/gate/pallas_call | solution.py:323
  5.3 3.0 %collective-permute-start.1 = (bf16[4,128,128]{2,1,0:T(8,128)(2,1)S(1)}, bf16[4,128,128]{2,1,0:T(8,128)(2,1)S(1)}, u32[]{:S(2)}, u32[]{:S(2)}) collective-permute-start(bf16[4,128,128]{2,1,0:T(8,128)(2,1)S(1)} %get-tuple-element.59), channel_id=1, source_target_pairs={{0,1},{1,0},{2,3},{3,2},{4,5},{5,4},{6,7},{7,6},{8,9},{9,8},{10,11... | collective-permute-start | bytes 393224 | tf_op jit(solution)/shard_map/ppermute | solution.py:343
  8.3 0.1 collective-permute-start
  8.4 0.9 %within.1 = (bf16[16,128,128]{2,1,0:T(8,128)(2,1)S(1)}, f32[128,2048]{1,0:T(8,128)S(1)}) custom-call(bf16[128,2048]{1,0:T(8,128)(2,1)S(1)} %get-tuple-element.48.q.refs_0_, bf16[128,2048]{1,0:T(8,128)(2,1)S(1)} %get-tuple-element.49.k.refs_1_.refs_0_, bf16[128,2048]{1,0:T(8,128)(2,1)S(1)} %get-tuple-element.50.v.refs_2_.refs_0_, ...), custom_call_target="tpu_custom_call" | custom-call | flops 1000 | bytes 1000 | tf_op jit(solution)/shard_map/within/pallas_call | solution.py:353
  9.2 3.4 %collective-permute-done.1.state.refs_15_ = bf16[4,128,128]{2,1,0:T(8,128)(2,1)S(1)} collective-permute-done((bf16[4,128,128]{2,1,0:T(8,128)(2,1)S(1)}, bf16[4,128,128]{2,1,0:T(8,128)(2,1)S(1)}, u32[]{:S(2)}, u32[]{:S(2)}) %collective-permute-start.1) | collective-permute-done | bytes 131104 | tf_op jit(solution)/shard_map/ppermute | solution.py:343
  12.6 0.7 %mix.5 = (bf16[128,512]{1,0:T(8,128)(2,1)S(1)}, bf16[128,512]{1,0:T(8,128)(2,1)S(1)}, bf16[4,128,128]{2,1,0:T(8,128)(2,1)S(1)}, f32[4,128]{1,0:T(4,128)S(1)}) custom-call(bf16[128,2048]{1,0:T(8,128)(2,1)S(1)} %get-tuple-element.48.q.refs_0_, f32[128,2048]{1,0:T(8,128)S(1)} %get-tuple-element.54.within, bf16[128,2048]{1,0:T(8,128)(2,1)S(1)} %get-tuple-element.55.cot, ...), custom_call_target="tpu_custom_call" | custom-call | flops 1000 | bytes 1000 | tf_op jit(solution)/shard_map/mix/pallas_call | solution.py:365
  13.3 2.1 %collective-permute-start.3 = (bf16[4,128,128]{2,1,0:T(8,128)(2,1)S(1)}, bf16[4,128,128]{2,1,0:T(8,128)(2,1)S(1)}, u32[]{:S(2)}, u32[]{:S(2)}) collective-permute-start(bf16[4,128,128]{2,1,0:T(8,128)(2,1)S(1)} %get-tuple-element.64), channel_id=1, source_target_pairs={{0,1},{1,0},{2,3},{3,2},{4,5},{5,4},{6,7},{7,6},{8,9},{9,8},{10,11... | collective-permute-start | bytes 393224 | tf_op jit(solution)/shard_map/ppermute | solution.py:383
  15.4 0.0 collective-permute-done.state.refs_14_
  15.4 0.7 %mix.4 = (bf16[128,512]{1,0:T(8,128)(2,1)S(1)}, bf16[128,512]{1,0:T(8,128)(2,1)S(1)}, bf16[4,128,128]{2,1,0:T(8,128)(2,1)S(1)}, f32[4,128]{1,0:T(4,128)S(1)}) custom-call(bf16[128,2048]{1,0:T(8,128)(2,1)S(1)} %get-tuple-element.48.q.refs_0_, f32[128,2048]{1,0:T(8,128)S(1)} %get-tuple-element.54.within, bf16[128,2048]{1,0:T(8,128)(2,1)S(1)} %get-tuple-element.55.cot, ...), custom_call_target="tpu_custom_call" | custom-call | flops 1000 | bytes 1000 | tf_op jit(solution)/shard_map/mix/pallas_call | solution.py:365
  16.1 1.5 %collective-permute-start.2 = (bf16[4,128,128]{2,1,0:T(8,128)(2,1)S(1)}, bf16[4,128,128]{2,1,0:T(8,128)(2,1)S(1)}, u32[]{:S(2)}, u32[]{:S(2)}) collective-permute-start(bf16[4,128,128]{2,1,0:T(8,128)(2,1)S(1)} %get-tuple-element.62), channel_id=1, source_target_pairs={{0,1},{1,0},{2,3},{3,2},{4,5},{5,4},{6,7},{7,6},{8,9},{9,8},{10,11... | collective-permute-start | bytes 393224 | tf_op jit(solution)/shard_map/ppermute | solution.py:383
  17.5 2.0 %collective-permute-done.3.state.refs_17_.refs_1_.refs_3_ = bf16[4,128,128]{2,1,0:T(8,128)(2,1)S(1)} collective-permute-done((bf16[4,128,128]{2,1,0:T(8,128)(2,1)S(1)}, bf16[4,128,128]{2,1,0:T(8,128)(2,1)S(1)}, u32[]{:S(2)}, u32[]{:S(2)}) %collective-permute-start.3) | collective-permute-done | bytes 131104 | tf_op jit(solution)/shard_map/ppermute | solution.py:383
  19.5 0.7 %mix.7 = (bf16[128,512]{1,0:T(8,128)(2,1)S(1)}, bf16[128,512]{1,0:T(8,128)(2,1)S(1)}, bf16[4,128,128]{2,1,0:T(8,128)(2,1)S(1)}, f32[4,128]{1,0:T(4,128)S(1)}) custom-call(bf16[128,2048]{1,0:T(8,128)(2,1)S(1)} %get-tuple-element.48.q.refs_0_, f32[128,2048]{1,0:T(8,128)S(1)} %get-tuple-element.54.within, bf16[128,2048]{1,0:T(8,128)(2,1)S(1)} %get-tuple-element.55.cot, ...), custom_call_target="tpu_custom_call" | custom-call | flops 1000 | bytes 1000 | tf_op jit(solution)/shard_map/mix/pallas_call | solution.py:365
  20.2 2.2 %collective-permute-start.5 = (bf16[4,128,128]{2,1,0:T(8,128)(2,1)S(1)}, bf16[4,128,128]{2,1,0:T(8,128)(2,1)S(1)}, u32[]{:S(2)}, u32[]{:S(2)}) collective-permute-start(bf16[4,128,128]{2,1,0:T(8,128)(2,1)S(1)} %get-tuple-element.78), channel_id=1, source_target_pairs={{0,1},{1,0},{2,3},{3,2},{4,5},{5,4},{6,7},{7,6},{8,9},{9,8},{10,11... | collective-permute-start | bytes 393224 | tf_op jit(solution)/shard_map/ppermute | solution.py:343
  22.4 0.2 collective-permute-done.2.state.refs_16_.refs_0_.refs_2_
  22.6 0.7 %mix.6 = (bf16[128,512]{1,0:T(8,128)(2,1)S(1)}, bf16[128,512]{1,0:T(8,128)(2,1)S(1)}, bf16[4,128,128]{2,1,0:T(8,128)(2,1)S(1)}, f32[4,128]{1,0:T(4,128)S(1)}) custom-call(bf16[128,2048]{1,0:T(8,128)(2,1)S(1)} %get-tuple-element.48.q.refs_0_, f32[128,2048]{1,0:T(8,128)S(1)} %get-tuple-element.54.within, bf16[128,2048]{1,0:T(8,128)(2,1)S(1)} %get-tuple-element.55.cot, ...), custom_call_target="tpu_custom_call" | custom-call | flops 1000 | bytes 1000 | tf_op jit(solution)/shard_map/mix/pallas_call | solution.py:365
  23.2 1.7 %collective-permute-start.4 = (bf16[4,128,128]{2,1,0:T(8,128)(2,1)S(1)}, bf16[4,128,128]{2,1,0:T(8,128)(2,1)S(1)}, u32[]{:S(2)}, u32[]{:S(2)}) collective-permute-start(bf16[4,128,128]{2,1,0:T(8,128)(2,1)S(1)} %get-tuple-element.77), channel_id=1, source_target_pairs={{0,1},{1,0},{2,3},{3,2},{4,5},{5,4},{6,7},{7,6},{8,9},{9,8},{10,11... | collective-permute-start | bytes 393224 | tf_op jit(solution)/shard_map/ppermute | solution.py:343
  25.0 2.1 %back.1 = (bf16[128,2048]{1,0:T(8,128)(2,1)}, f32[128,2048]{1,0:T(8,128)S(1)}, f32[128,2048]{1,0:T(8,128)S(1)}, f32[128,2048]{1,0:T(8,128)S(1)}, f32[16,128]{1,0:T(8,128)S(1)}) custom-call(bf16[128,2048]{1,0:T(8,128)(2,1)S(1)} %get-tuple-element.48.q.refs_0_, bf16[128,2048]{1,0:T(8,128)(2,1)S(1)} %get-tuple-element.49.k.refs_1_.refs_0_, ...), custom_call_target="tpu_custom_call" | custom-call | flops 1000 | bytes 1000 | tf_op jit(solution)/shard_map/back/pallas_call | solution.py:389
  27.1 0.0 collective-permute-done.5.refs_3_.refs_5_
  27.1 1.2 %collective-permute-done.4.refs_2_.refs_4_ = bf16[4,128,128]{2,1,0:T(8,128)(2,1)S(1)} collective-permute-done((bf16[4,128,128]{2,1,0:T(8,128)(2,1)S(1)}, bf16[4,128,128]{2,1,0:T(8,128)(2,1)S(1)}, u32[]{:S(2)}, u32[]{:S(2)}) %collective-permute-start.4) | collective-permute-done | bytes 131104 | tf_op jit(solution)/shard_map/ppermute | solution.py:343
  28.3 1.3 %logits.1 = (bf16[16,128]{1,0:T(8,128)(2,1)S(1)}, bf16[8,16,384]{2,1,0:T(8,128)(2,1)S(1)}, bf16[8,16,384]{2,1,0:T(8,128)(2,1)S(1)}) custom-call(bf16[128,2048]{1,0:T(8,128)(2,1)S(1)} %get-tuple-element.48.q.refs_0_, bf16[128,2048]{1,0:T(8,128)(2,1)S(1)} %get-tuple-element.49.k.refs_1_.refs_0_, bf16[128,2048]{1,0:T(8,128)(2,1)S(1)} %get-tuple-element.50.v.refs_2_.refs_0_, ...), custom_call_target="tpu_custom_call" | custom-call | flops 1000 | bytes 1000 | tf_op jit(solution)/shard_map/logits/pallas_call | solution.py:421
  29.6 0.1 collective-permute-start.6
  29.6 1.3 %collective-permute-done.6 = bf16[8,16,384]{2,1,0:T(8,128)(2,1)S(1)} collective-permute-done((bf16[8,16,384]{2,1,0:T(8,128)(2,1)S(1)}, bf16[8,16,384]{2,1,0:T(8,128)(2,1)S(1)}, u32[]{:S(2)}, u32[]{:S(2)}) %collective-permute-start.6) | collective-permute-done | bytes 98336 | tf_op jit(solution)/shard_map/ppermute | solution.py:454
  31.0 1.8 %collective-permute-start.7 = (bf16[4,16,384]{2,1,0:T(8,128)(2,1)S(1)}, bf16[4,16,384]{2,1,0:T(8,128)(2,1)S(1)}, u32[]{:S(2)}, u32[]{:S(2)}) collective-permute-start(bf16[4,16,384]{2,1,0:T(8,128)(2,1)S(1)} %slice.31), channel_id=1, source_target_pairs={{0,4},{2,6},{4,0},{6,2},{8,12},{10,14},{12,8},{14,10},{16,20},{18,... | collective-permute-start | bytes 147464 | tf_op jit(solution)/shard_map/ppermute | solution.py:454
  32.7 1.1 %finish.3 = bf16[128,2048]{1,0:T(8,128)(2,1)} custom-call(f32[128,2048]{1,0:T(8,128)S(1)} %get-tuple-element.81.partial, bf16[16,128]{1,0:T(8,128)(2,1)S(1)} %get-tuple-element.82.d_logits, bf16[16,6144]{1,0:T(8,128)(2,1)S(1)} %bitcast.15), custom_call_target="tpu_custom_call" | custom-call | flops 1000 | bytes 1000 | tf_op jit(solution)/shard_map/finish/pallas_call | solution.py:433
  33.8 1.3 %collective-permute-done.7 = bf16[4,16,384]{2,1,0:T(8,128)(2,1)S(1)} collective-permute-done((bf16[4,16,384]{2,1,0:T(8,128)(2,1)S(1)}, bf16[4,16,384]{2,1,0:T(8,128)(2,1)S(1)}, u32[]{:S(2)}, u32[]{:S(2)}) %collective-permute-start.7) | collective-permute-done | bytes 49184 | tf_op jit(solution)/shard_map/ppermute | solution.py:454
  35.2 1.8 %collective-permute-start.8 = (bf16[2,16,384]{2,1,0:T(8,128)(2,1)S(1)}, bf16[2,16,384]{2,1,0:T(8,128)(2,1)S(1)}, u32[]{:S(2)}, u32[]{:S(2)}) collective-permute-start(bf16[2,16,384]{2,1,0:T(8,128)(2,1)S(1)} %slice.32), channel_id=1, source_target_pairs={{0,8},{2,10},{4,12},{6,14},{8,0},{10,2},{12,4},{14,6},{16,24},{18,... | collective-permute-start | bytes 73736 | tf_op jit(solution)/shard_map/ppermute | solution.py:454
  37.0 1.4 %finish.4 = bf16[128,2048]{1,0:T(8,128)(2,1)} custom-call(f32[128,2048]{1,0:T(8,128)S(1)} %get-tuple-element.85.partial, bf16[16,128]{1,0:T(8,128)(2,1)S(1)} %get-tuple-element.82.d_logits, bf16[16,6144]{1,0:T(8,128)(2,1)S(1)} %bitcast.16, bf16[128,2048]{1,0:T(8,128)(2,1)S(1)} %get-tuple-element.50.v.refs_2_.refs_0_, ...), custom_call_target="tpu_custom_call" | custom-call | flops 1000 | bytes 1000 | tf_op jit(solution)/shard_map/finish/pallas_call | solution.py:433
  38.4 0.7 %collective-permute-done.8 = bf16[2,16,384]{2,1,0:T(8,128)(2,1)S(1)} collective-permute-done((bf16[2,16,384]{2,1,0:T(8,128)(2,1)S(1)}, bf16[2,16,384]{2,1,0:T(8,128)(2,1)S(1)}, u32[]{:S(2)}, u32[]{:S(2)}) %collective-permute-start.8) | collective-permute-done | bytes 24608 | tf_op jit(solution)/shard_map/ppermute | solution.py:454
  39.1 2.8 %collective-permute-start.9 = (bf16[1,16,384]{2,1,0:T(8,128)(2,1)S(1)}, bf16[1,16,384]{2,1,0:T(8,128)(2,1)S(1)}, u32[]{:S(2)}, u32[]{:S(2)}) collective-permute-start(bf16[1,16,384]{2,1,0:T(8,128)(2,1)S(1)} %slice.34), channel_id=1, source_target_pairs={{0,16},{2,18},{4,20},{6,22},{8,24},{10,26},{12,28},{14,30},{16,0},... | collective-permute-start | bytes 36872 | tf_op jit(solution)/shard_map/ppermute | solution.py:454
  41.9 1.3 %finish.5 = bf16[128,2048]{1,0:T(8,128)(2,1)} custom-call(f32[128,2048]{1,0:T(8,128)S(1)} %get-tuple-element.88.partial, bf16[16,128]{1,0:T(8,128)(2,1)S(1)} %get-tuple-element.82.d_logits, bf16[16,6144]{1,0:T(8,128)(2,1)S(1)} %bitcast.17, bf16[128,2048]{1,0:T(8,128)(2,1)S(1)} %get-tuple-element.49.k.refs_1_.refs_0_, ...), custom_call_target="tpu_custom_call" | custom-call | flops 1000 | bytes 1000 | tf_op jit(solution)/shard_map/finish/pallas_call | solution.py:433
  43.3 0.5 collective-permute-done.9
  43.7 1.7 %collective-permute-start.10 = (bf16[16,384]{1,0:T(8,128)(2,1)S(1)}, bf16[16,384]{1,0:T(8,128)(2,1)S(1)}, u32[]{:S(2)}, u32[]{:S(2)}) collective-permute-start(bf16[16,384]{1,0:T(8,128)(2,1)S(1)} %bitcast_convert_fusion), channel_id=1, source_target_pairs={{0,1},{1,0},{2,3},{3,2},{4,5},{5,4},{6,7},{7,6},{8,9},{9,8},{10,11... | collective-permute-start | bytes 36872 | tf_op jit(solution)/shard_map/ppermute | solution.py:466
  45.5 2.0 %collective-permute-done.10 = bf16[16,384]{1,0:T(8,128)(2,1)S(1)} collective-permute-done((bf16[16,384]{1,0:T(8,128)(2,1)S(1)}, bf16[16,384]{1,0:T(8,128)(2,1)S(1)}, u32[]{:S(2)}, u32[]{:S(2)}) %collective-permute-start.10) | collective-permute-done | bytes 12320 | tf_op jit(solution)/shard_map/ppermute | solution.py:466
  47.5 0.7 %fusion = f32[192,16]{0,1:T(8,128)} fusion(f32[16,384]{1,0:T(8,128)S(1)} %bitcast.26, s32[]{:T(128)S(6)} %select_n.3, bf16[16,384]{1,0:T(8,128)(2,1)S(1)} %collective-permute-done.10), kind=kLoop, calls=%fused_computation.5 | loop fusion | flops 6144 | bytes 30724 | tf_op jit(solution)/shard_map/transpose | solution.py:469
  (9 shorter events, 0.1 us)
Async XLA Ops:
  0.6 0.7 %copy-start.1 = (f32[1,16,128]{2,1,0:T(8,128)S(1)}, f32[1,16,128]{2,1,0:T(8,128)}, u32[]{:S(2)}) copy-start(f32[1,16,128]{2,1,0:T(8,128)} %param.10) | copy-start | bytes 24580
  1.3 0.9 %copy-start = (bf16[6144,16]{0,1:T(8,128)(2,1)S(1)}, bf16[6144,16]{0,1:T(8,128)(2,1)}, u32[]{:S(2)}) copy-start(bf16[6144,16]{0,1:T(8,128)(2,1)} %param.11) | copy-start | bytes 589828
  5.3 7.3 %collective-permute-start.1 = (bf16[4,128,128]{2,1,0:T(8,128)(2,1)S(1)}, bf16[4,128,128]{2,1,0:T(8,128)(2,1)S(1)}, u32[]{:S(2)}, u32[]{:S(2)}) collective-permute-start(bf16[4,128,128]{2,1,0:T(8,128)(2,1)S(1)} %get-tuple-element.59), channel_id=1, source_target_pairs={{0,1},{1,0},{2,3},{3,2},{4,5},{5,4},{6,7},{7,6},{8,9},{9,8},{10,11... | collective-permute-start | bytes 393224 | tf_op jit(solution)/shard_map/ppermute | solution.py:343
  8.3 7.1 %collective-permute-start = (bf16[4,128,128]{2,1,0:T(8,128)(2,1)S(1)}, bf16[4,128,128]{2,1,0:T(8,128)(2,1)S(1)}, u32[]{:S(2)}, u32[]{:S(2)}) collective-permute-start(bf16[4,128,128]{2,1,0:T(8,128)(2,1)S(1)} %get-tuple-element.56), channel_id=1, source_target_pairs={{0,1},{1,0},{2,3},{3,2},{4,5},{5,4},{6,7},{7,6},{8,9},{9,8},{10,11... | collective-permute-start | bytes 393224 | tf_op jit(solution)/shard_map/ppermute | solution.py:343
  13.3 6.2 %collective-permute-start.3 = (bf16[4,128,128]{2,1,0:T(8,128)(2,1)S(1)}, bf16[4,128,128]{2,1,0:T(8,128)(2,1)S(1)}, u32[]{:S(2)}, u32[]{:S(2)}) collective-permute-start(bf16[4,128,128]{2,1,0:T(8,128)(2,1)S(1)} %get-tuple-element.64), channel_id=1, source_target_pairs={{0,1},{1,0},{2,3},{3,2},{4,5},{5,4},{6,7},{7,6},{8,9},{9,8},{10,11... | collective-permute-start | bytes 393224 | tf_op jit(solution)/shard_map/ppermute | solution.py:383
  16.1 6.5 %collective-permute-start.2 = (bf16[4,128,128]{2,1,0:T(8,128)(2,1)S(1)}, bf16[4,128,128]{2,1,0:T(8,128)(2,1)S(1)}, u32[]{:S(2)}, u32[]{:S(2)}) collective-permute-start(bf16[4,128,128]{2,1,0:T(8,128)(2,1)S(1)} %get-tuple-element.62), channel_id=1, source_target_pairs={{0,1},{1,0},{2,3},{3,2},{4,5},{5,4},{6,7},{7,6},{8,9},{9,8},{10,11... | collective-permute-start | bytes 393224 | tf_op jit(solution)/shard_map/ppermute | solution.py:383
  20.2 6.9 %collective-permute-start.5 = (bf16[4,128,128]{2,1,0:T(8,128)(2,1)S(1)}, bf16[4,128,128]{2,1,0:T(8,128)(2,1)S(1)}, u32[]{:S(2)}, u32[]{:S(2)}) collective-permute-start(bf16[4,128,128]{2,1,0:T(8,128)(2,1)S(1)} %get-tuple-element.78), channel_id=1, source_target_pairs={{0,1},{1,0},{2,3},{3,2},{4,5},{5,4},{6,7},{7,6},{8,9},{9,8},{10,11... | collective-permute-start | bytes 393224 | tf_op jit(solution)/shard_map/ppermute | solution.py:343
  23.2 5.0 %collective-permute-start.4 = (bf16[4,128,128]{2,1,0:T(8,128)(2,1)S(1)}, bf16[4,128,128]{2,1,0:T(8,128)(2,1)S(1)}, u32[]{:S(2)}, u32[]{:S(2)}) collective-permute-start(bf16[4,128,128]{2,1,0:T(8,128)(2,1)S(1)} %get-tuple-element.77), channel_id=1, source_target_pairs={{0,1},{1,0},{2,3},{3,2},{4,5},{5,4},{6,7},{7,6},{8,9},{9,8},{10,11... | collective-permute-start | bytes 393224 | tf_op jit(solution)/shard_map/ppermute | solution.py:343
  29.6 1.4 %collective-permute-start.6 = (bf16[8,16,384]{2,1,0:T(8,128)(2,1)S(1)}, bf16[8,16,384]{2,1,0:T(8,128)(2,1)S(1)}, u32[]{:S(2)}, u32[]{:S(2)}) collective-permute-start(bf16[8,16,384]{2,1,0:T(8,128)(2,1)S(1)} %get-tuple-element.80), channel_id=1, source_target_pairs={{0,2},{2,0},{4,6},{6,4},{8,10},{10,8},{12,14},{14,12},{16,18},{18,... | collective-permute-start | bytes 294920 | tf_op jit(solution)/shard_map/ppermute | solution.py:454
  31.0 4.2 %collective-permute-start.7 = (bf16[4,16,384]{2,1,0:T(8,128)(2,1)S(1)}, bf16[4,16,384]{2,1,0:T(8,128)(2,1)S(1)}, u32[]{:S(2)}, u32[]{:S(2)}) collective-permute-start(bf16[4,16,384]{2,1,0:T(8,128)(2,1)S(1)} %slice.31), channel_id=1, source_target_pairs={{0,4},{2,6},{4,0},{6,2},{8,12},{10,14},{12,8},{14,10},{16,20},{18,... | collective-permute-start | bytes 147464 | tf_op jit(solution)/shard_map/ppermute | solution.py:454
  35.2 3.9 %collective-permute-start.8 = (bf16[2,16,384]{2,1,0:T(8,128)(2,1)S(1)}, bf16[2,16,384]{2,1,0:T(8,128)(2,1)S(1)}, u32[]{:S(2)}, u32[]{:S(2)}) collective-permute-start(bf16[2,16,384]{2,1,0:T(8,128)(2,1)S(1)} %slice.32), channel_id=1, source_target_pairs={{0,8},{2,10},{4,12},{6,14},{8,0},{10,2},{12,4},{14,6},{16,24},{18,... | collective-permute-start | bytes 73736 | tf_op jit(solution)/shard_map/ppermute | solution.py:454
  39.1 4.7 %collective-permute-start.9 = (bf16[1,16,384]{2,1,0:T(8,128)(2,1)S(1)}, bf16[1,16,384]{2,1,0:T(8,128)(2,1)S(1)}, u32[]{:S(2)}, u32[]{:S(2)}) collective-permute-start(bf16[1,16,384]{2,1,0:T(8,128)(2,1)S(1)} %slice.34), channel_id=1, source_target_pairs={{0,16},{2,18},{4,20},{6,22},{8,24},{10,26},{12,28},{14,30},{16,0},... | collective-permute-start | bytes 36872 | tf_op jit(solution)/shard_map/ppermute | solution.py:454
  43.7 3.8 %collective-permute-start.10 = (bf16[16,384]{1,0:T(8,128)(2,1)S(1)}, bf16[16,384]{1,0:T(8,128)(2,1)S(1)}, u32[]{:S(2)}, u32[]{:S(2)}) collective-permute-start(bf16[16,384]{1,0:T(8,128)(2,1)S(1)} %bitcast_convert_fusion), channel_id=1, source_target_pairs={{0,1},{1,0},{2,3},{3,2},{4,5},{5,4},{6,7},{7,6},{8,9},{9,8},{10,11... | collective-permute-start | bytes 36872 | tf_op jit(solution)/shard_map/ppermute | solution.py:466

commit v4 on v3

v4 whole, which is shorter than its diff:
```python
import functools

import jax
import jax.numpy as jnp
from jax import lax
from jax.experimental import pallas as pl
from jax.experimental.pallas import tpu as pltpu
from jax.sharding import PartitionSpec as P

EPSILON = 1e-06
F32 = jnp.float32
BF16 = jnp.bfloat16
STAGE = 8
CORES = 2
VMEM_LIMIT = 16 * 1024 * 1024
VMEM_FULL = 58 * 1024 * 1024


def dot_nn(a, b):
    return lax.dot_general(a, b, (((1,), (0,)), ((), ())), preferred_element_type=F32)


def dot_nt(a, b):
    return lax.dot_general(a, b, (((1,), (1,)), ((), ())), preferred_element_type=F32)


def dot_tn(a, b):
    return lax.dot_general(a, b, (((0,), (0,)), ((), ())), preferred_element_type=F32)


def exact_dot(x, ones):
    rows = x.shape[0]
    high = x.astype(BF16)
    rest = x - high.astype(F32)
    middle = rest.astype(BF16)
    low = (rest - middle.astype(F32)).astype(BF16)
    parts = dot_nn(jnp.concatenate([high, middle, low], axis=0), ones)
    return parts[:rows] + parts[rows : 2 * rows] + parts[2 * rows :]


def triangle(size, upper):
    rows = lax.broadcasted_iota(jnp.int32, (size, size), 0)
    columns = lax.broadcasted_iota(jnp.int32, (size, size), 1)
    keep = rows <= columns if upper else rows >= columns
    return jnp.where(keep, 1.0, 0.0).astype(BF16)


def decay_matrix(cum_column, cum_row):
    size = cum_row.shape[1]
    rows = lax.broadcasted_iota(jnp.int32, (size, size), 0)
    columns = lax.broadcasted_iota(jnp.int32, (size, size), 1)
    return jnp.exp(jnp.where(columns <= rows, cum_column - cum_row, -jnp.inf))


def spec():
    return pl.BlockSpec(memory_space=pltpu.VMEM)


def smem():
    return pl.BlockSpec(memory_space=pltpu.SMEM)


def hbm():
    return pl.BlockSpec(memory_space=pltpu.HBM)


def params(limit=VMEM_LIMIT):
    return pltpu.CompilerParams(vmem_limit_bytes=limit)


def cost():
    return pl.CostEstimate(flops=1000, bytes_accessed=1000, transcendentals=0)


def head_lanes(size, first, count):
    return [slice(h * size, (h + 1) * size) for h in range(first, first + count)]


def turn(k, size, groups):
    return [
        [k[:, p].astype(F32).T for p in head_lanes(size, first, count)] for first, count in groups
    ]


def add_updates(turned, v, cum, groups, outs):
    size = outs[0].shape[1]
    fading = jnp.exp(cum[:, cum.shape[1] - 1 :] - cum)
    faded = [
        [(t * fading[first + i : first + i + 1, :]).astype(BF16) for i, t in enumerate(some)]
        for (first, _), some in zip(groups, turned)
    ]
    for (first, count), some, out in zip(groups, faded, outs):
        parts = head_lanes(size, first, count)
        for i, product in enumerate([dot_nn(f, v[:, p]) for f, p in zip(some, parts)]):
            out[i] = product.astype(BF16)


def gate_kernel(groups, q_in, k_in, v_in, bias_in, gate_in, *refs):
    logits_ref, cum_ref, *updates = refs[: 2 + len(groups)]
    q, k, v, bias, gate, sems = refs[2 + len(groups) :]
    pairs = ((gate_in, gate), (bias_in, bias), (k_in, k), (q_in, q), (v_in, v))
    copies = [
        pltpu.make_async_copy(source, target, sems.at[i])
        for i, (source, target) in enumerate(pairs)
    ]
    for copy in copies:
        copy.start()
    width = q.shape[1]
    for copy in copies[:3]:
        copy.wait()
    logits = bias[...] + dot_nt(gate[:, width : 2 * width], k[...])
    turned = turn(k, updates[0].shape[1], groups)
    copies[3].wait()
    logits = logits + dot_nt(gate[:, :width], q[...])
    copies[4].wait()
    logits = logits + dot_nt(gate[:, 2 * width :], v[...])
    logits_ref[...] = logits
    soft = jnp.maximum(logits, 0.0) + jnp.log1p(jnp.exp(-jnp.abs(logits)))
    cum = exact_dot(-soft, triangle(logits.shape[1], True))
    cum_ref[...] = cum
    add_updates(turned, v, cum, groups, updates)


def within_kernel(heads, groups, q, k, v, cum_ref, cot, resets, attn_ref, within, rise_ref, *updates):
    del cot
    rise_ref[...] = (1 - resets[0, 0]).astype(F32) * jnp.exp(cum_ref[...])
    size = q.shape[1] // heads
    if groups:
        add_updates(turn(k, size, groups), v, cum_ref[...], groups, updates)
    cum_columns = cum_ref[...].T
    step = min(heads, STAGE)
    for first in range(0, heads, step):
        count = min(step, heads - first)
        parts = head_lanes(size, first, count)
        scores = [dot_nt(q[:, p], k[:, p]) for p in parts]
        attns = [
            (decay_matrix(cum_columns[:, h : h + 1], cum_ref[h : h + 1, :]) * s).astype(BF16)
            for h, s in enumerate(scores, first)
        ]
        for h, a in enumerate(attns, first):
            attn_ref[h] = a
        for a, p in zip(attns, parts):
            within[:, p] = dot_nn(a, v[:, p])


def mix_kernel(first, count, q, within, cot, rise_ref, state, *refs):
    *forwarded, out, d_mix, pushed, row_ref = refs
    size = state.shape[1]
    opening = lax.axis_index("seq") == 0
    parts, owns = head_lanes(size, first, count), head_lanes(size, 0, count)
    rise = rise_ref[...][first : first + count]
    decays = jnp.where(opening, 0.0, rise).T
    reads = [dot_nn(q[:, p], state[i]) for i, p in enumerate(parts)]
    mixtures = [
        within[:, p] + decays[:, i : i + 1] * x for i, (p, x) in enumerate(zip(parts, reads))
    ]
    upstream = [cot[:, p].astype(F32) for p in parts]
    squares = [jnp.mean(m * m, axis=1, keepdims=True) + EPSILON for m in mixtures]
    shared = [jnp.mean(u * m, axis=1, keepdims=True) for u, m in zip(upstream, mixtures)]
    inverses = [lax.rsqrt(s) for s in squares]
    normed = [m * i for m, i in zip(mixtures, inverses)]
    for n, o in zip(normed, owns):
        out[:, o] = n.astype(BF16)
    grads = [
        ((u - n * (s * i)) * i).astype(BF16)
        for u, n, s, i in zip(upstream, normed, shared, inverses)
    ]
    for g, o in zip(grads, owns):
        d_mix[:, o] = g
    faded = [
        (q[:, p].astype(F32).T * rise[i : i + 1, :]).astype(BF16) for i, p in enumerate(parts)
    ]
    products = [dot_nn(f, g) for f, g in zip(faded, grads)]
    for i, product in enumerate(products):
        product = product.astype(BF16)
        if forwarded:
            product = jnp.where(opening, forwarded[0][i], product)
        pushed[i] = product
    terms = [
        jnp.sum(g.astype(F32) * m, axis=1, keepdims=True) for g, m in zip(grads, mixtures)
    ]
    row_ref[...] = jnp.concatenate(terms, axis=1).T


def members(groups):
    return [(g, i) for g, (_, count) in enumerate(groups) for i in range(count)]


def fading_rows(cum, slots):
    closing = lax.axis_index("seq") == slots - 1
    return jnp.where(closing, 0.0, jnp.exp(cum[:, cum.shape[1] - 1 :] - cum))


def state_terms(keys, moved, fading):
    sums = [jnp.sum(x.astype(F32) * m, axis=1, keepdims=True) for x, m in zip(keys, moved)]
    from_state = jnp.concatenate(sums, axis=1).T * fading
    last = lax.broadcasted_iota(jnp.int32, fading.shape, 1) == fading.shape[1] - 1
    total = jnp.sum(from_state, axis=1, keepdims=True)
    return jnp.where(last, total, 0.0) - from_state


def back_kernel(groups, early, slots, *refs):
    q, k, v, attn, cum_ref, rise_ref = refs[:6]
    number = len(groups)
    outs, d_mixes, states, row_terms = [refs[6 + number * i : 6 + number * (i + 1)] for i in range(4)]
    *grads, output, gq, gk, gv, term_ref, sems = refs[6 + 4 * number :]
    size = states[0].shape[1]
    copies = [
        pltpu.make_async_copy(
            out, output.at[:, pl.ds(first * size, count * size)], sems.at[i]
        )
        for i, ((first, count), out) in enumerate(zip(groups, outs))
    ]
    for copy in copies:
        copy.start()
    cum = cum_ref[...]
    cum_columns = cum.T
    rise_columns = jnp.where(lax.axis_index("seq") == 0, 0.0, rise_ref[...]).T
    fading = fading_rows(cum, slots)
    fading_columns = fading.T
    sums, added = [], []
    places = members(groups)
    for start in range(0, len(places), STAGE):
        some = places[start : start + STAGE]
        heads = range(start, start + len(some))
        parts = head_lanes(size, start, len(some))
        d_outs = [d_mixes[g][:, i * size : (i + 1) * size] for g, i in some]
        columns = [cum_columns[:, h : h + 1] for h in heads]
        d_attns = [dot_nt(d, v[:, p]) for d, p in zip(d_outs, parts)]
        reads = [dot_nt(d, states[g][i]) for d, (g, i) in zip(d_outs, some)]
        weighted = [
            (decay_matrix(c, cum_ref[h : h + 1, :]) * d).astype(BF16)
            for h, c, d in zip(heads, columns, d_attns)
        ]
        ready = [(h, p, g, i) for h, p, (g, i) in zip(heads, parts, some) if g < early]
        moved_k = {h: dot_nt(v[:, p], grads[g][i]) for h, p, g, i in ready}
        moved_v = {h: dot_nn(k[:, p], grads[g][i]) for h, p, g, i in ready}
        for h, p, w, x in zip(heads, parts, weighted, reads):
            gq[:, p] = dot_nn(w, k[:, p]) + rise_columns[:, h : h + 1] * x
        for h, p, w in zip(heads, parts, weighted):
            total = dot_tn(w, q[:, p])
            gk[:, p] = total + fading_columns[:, h : h + 1] * moved_k[h] if h in moved_k else total
        for h, p, d in zip(heads, parts, d_outs):
            total = dot_tn(attn[h], d)
            gv[:, p] = total + fading_columns[:, h : h + 1] * moved_v[h] if h in moved_v else total
        for h, d in zip(heads, d_attns):
            sums.append(jnp.sum(attn[h].astype(F32) * d, axis=0, keepdims=True))
        if ready:
            first = ready[0][0]
            keys = [k[:, p] for _, p, _, _ in ready]
            some_fading = fading[first : first + len(ready)]
            added.append(state_terms(keys, [moved_k[h] for h, *_ in ready], some_fading))
    terms = jnp.concatenate([r[...] for r in row_terms], axis=0) - jnp.concatenate(sums, axis=0)
    if added:
        early_terms = jnp.concatenate(added, axis=0)
        count = early_terms.shape[0]
        term_ref[:count, :] = terms[:count] + early_terms
        term_ref[count:, :] = terms[count:]
    else:
        term_ref[...] = terms
    for copy in copies:
        copy.wait()


def logit_kernel(groups, early, slots, q, k, v, cum_ref, logits_ref, terms, through, *refs):
    late = len(groups) - early
    grads, (d_ref, *outs) = refs[:late], refs[late:]
    size = grads[0].shape[1]
    width = q.shape[1]
    cum = cum_ref[...]
    tokens = cum.shape[1]
    first = groups[early][0]
    parts = head_lanes(size, first, cum.shape[0] - first)
    moved = [dot_nt(v[:, p], grads[g][i]) for p, (g, i) in zip(parts, members(groups[early:]))]
    added = state_terms([k[:, p] for p in parts], moved, fading_rows(cum, slots)[first:])
    d_cum = terms[...] + through[...]
    d_cum = jnp.concatenate([d_cum[:first], d_cum[first:] + added], axis=0) if first else d_cum + added
    d_decay = exact_dot(d_cum, triangle(tokens, False))
    d_logits = (-jax.nn.sigmoid(logits_ref[...]) * d_decay).astype(BF16)
    d_ref[...] = d_logits
    whole = [dot_nn(d_logits, x[...]) for x in (q, k, v)]
    if len(outs) == 1:
        for i in range(3):
            outs[0][:, i * width : (i + 1) * width] = whole[i]
        return
    keep, send, pieces = outs
    joined = jnp.concatenate(whole, axis=1)
    cores, others = pieces.shape[:2]
    piece = 3 * width // (cores * others)
    for j in range(others):
        for c in range(cores):
            row, slot = j // slots * cores + c, j % slots
            pieces[c, j] = pack(joined, (row * slots + slot) * piece, piece).astype(BF16)
    core = lax.axis_index("core")
    keep[...] = pieces[core]
    send[...] = pieces[1 - core]


def pack(joined, first, piece):
    tiles = [joined[:, first + i : first + i + 128] for i in range(0, piece - 127, 128)]
    if piece % 128:
        rest = joined[:, first + piece // 128 * 128 : first + piece]
        half = rest.shape[0] // 2
        tiles.append(jnp.concatenate([rest[:half], rest[half:]], axis=1))
    return jnp.concatenate(tiles, axis=0)


def sum_kernel(arrived, out):
    heads, piece = out.shape
    total = jnp.sum(arrived[...].astype(F32), axis=0)
    tiles = piece // 128
    for i in range(tiles):
        out[:, i * 128 : (i + 1) * 128] = total[i * heads : (i + 1) * heads]
    if piece % 128:
        rest = total[tiles * heads :]
        out[: heads // 2, tiles * 128 :] = rest[:, :64]
        out[heads // 2 :, tiles * 128 :] = rest[:, 64:]


def finish_kernel(groups, early, slots, gq, gk, gv, k, v, cum_ref, d_logits, gate, *refs):
    late = len(groups) - early
    grads, outs, (result, sems) = refs[:late], refs[late : late + 3], refs[late + 3 :]
    width = gq.shape[1]
    places = members(groups)
    size = width // len(places)
    fading = fading_rows(cum_ref[...], slots).T
    copies = []
    for index, (partial, operand) in enumerate(((gq, None), (gk, v), (gv, k))):
        for start in range(0, len(places), STAGE):
            some = places[start : start + STAGE]
            at = index * width + start * size
            back = dot_tn(d_logits[...], gate[:, at : at + len(some) * size])
            parts, owns = head_lanes(size, start, len(some)), head_lanes(size, 0, len(some))
            moved = {}
            for h, (p, (g, i)) in enumerate(zip(parts, some), start):
                if operand is not None and g >= early:
                    dot = dot_nt if index == 1 else dot_nn
                    moved[h] = dot(operand[:, p], grads[g - early][i])
            for h, (p, o) in enumerate(zip(parts, owns), start):
                total = partial[:, p] + back[:, o]
                if h in moved:
                    total = total + fading[:, h : h + 1] * moved[h]
                result[index, :, p] = total.astype(BF16)
            lanes = pl.ds(start * size, len(some) * size)
            copies.append(
                pltpu.make_async_copy(
                    result.at[index, :, lanes], outs[index].at[:, lanes], sems.at[len(copies)]
                )
            )
            copies[-1].start()
    for copy in copies:
        copy.wait()


def shape(dims, dtype):
    return jax.ShapeDtypeStruct(dims, dtype)


def head_groups(heads):
    parts = 4 if heads >= 4 else 1
    sizes = [heads // parts + (1 if i < heads % parts else 0) for i in range(parts)]
    return [(sum(sizes[:i]), sizes[i]) for i in range(parts)]


def body(
    pairs, cores, seq_size, queries, keys, values, decay_bias, gate_matrix, resets, cotangent
):
    q, k, v, cot = queries[0], keys[0], values[0], cotangent[0]
    tokens, width = q.shape
    heads = decay_bias.shape[1]
    size = width // heads
    gate = gate_matrix.T
    groups = head_groups(heads)
    forward = [(i, i + 1) for i in range(seq_size - 1)]
    backward = [(i + 1, i) for i in range(seq_size - 1)]
    kept = (1 - resets[0, 0]).astype(F32)

    def state_shapes(some):
        return tuple(shape((count, size, size), BF16) for _, count in some)

    ahead = 2 if seq_size == 2 and len(groups) > 2 else len(groups)
    logits, cum, *updates = pl.pallas_call(
        functools.partial(gate_kernel, groups[:ahead]),
        out_shape=(shape((heads, tokens), F32),) * 2
        + state_shapes(groups[:ahead]),
        in_specs=[hbm()] * 5,
        out_specs=(spec(),) * (2 + ahead),
        scratch_shapes=[
            pltpu.VMEM((tokens, width), BF16),
            pltpu.VMEM((tokens, width), BF16),
            pltpu.VMEM((tokens, width), BF16),
            pltpu.VMEM((heads, tokens), F32),
            pltpu.VMEM((heads, 3 * width), BF16),
            pltpu.SemaphoreType.DMA((5,)),
        ],
        compiler_params=params(VMEM_FULL),
        cost_estimate=cost(),
        name="gate",
    )(q, k, v, decay_bias[0], gate)
    attn, within, rise, *made = pl.pallas_call(
        functools.partial(within_kernel, heads, groups[ahead:]),
        out_shape=(
            shape((heads, tokens, tokens), BF16),
            shape((tokens, width), F32),
            shape((heads, tokens), F32),
        )
        + state_shapes(groups[ahead:]),
        in_specs=[spec()] * 5 + [smem()],
        out_specs=(spec(),) * (3 + len(groups) - ahead),
        compiler_params=params(),
        cost_estimate=cost(),
        name="within",
    )(q, k, v, cum, cot, resets)
    updates += made

    def chain(own, first, count, pairs):
        if seq_size == 2:
            return lax.ppermute(own, "seq", [(0, 1), (1, 0)])
        arrived = lax.ppermute(own, "seq", pairs)
        for _ in range(seq_size - 2):
            factor = kept * jnp.exp(cum[first : first + count, -1])[:, None, None]
            passed = factor * arrived.astype(F32) + own.astype(F32)
            arrived = lax.ppermute(passed.astype(BF16), "seq", pairs)
        return arrived

    entering = [chain(updates[g], *groups[g], forward) for g in range(ahead)]
    outs, d_mixes, rows, grads = [], [], [], []
    for g, (first, count) in enumerate(groups):
        forwarded = [updates[g + ahead]] if g + ahead < len(groups) else []
        out_g, d_g, pushed, rows_g = pl.pallas_call(
            functools.partial(mix_kernel, first, count),
            out_shape=(
                shape((tokens, count * size), BF16),
                shape((tokens, count * size), BF16),
                shape((count, size, size), BF16),
                shape((count, tokens), F32),
            ),
            in_specs=[spec()] * (5 + len(forwarded)),
            out_specs=(spec(),) * 4,
            compiler_params=params(),
            cost_estimate=cost(),
            name="mix",
        )(q, within, cot, rise, entering[g], *forwarded)
        outs.append(out_g)
        d_mixes.append(d_g)
        rows.append(rows_g)
        if forwarded:
            arrived = lax.ppermute(pushed, "seq", [(0, 1), (1, 0)])
            entering.append(arrived)
            grads.append(arrived)
        else:
            grads.append(chain(pushed, first, count, backward))

    early = min(ahead, len(groups) // 2)
    output, gq, gk, gv, terms = pl.pallas_call(
        functools.partial(back_kernel, groups, early, seq_size),
        out_shape=(shape((tokens, width), BF16),)
        + (shape((tokens, width), F32),) * 3
        + (shape((heads, tokens), F32),),
        in_specs=[spec()] * (6 + 4 * len(groups) + early),
        out_specs=(hbm(),) + (spec(),) * 4,
        scratch_shapes=[pltpu.SemaphoreType.DMA((len(groups),))],
        compiler_params=params(),
        cost_estimate=cost(),
        name="back",
    )(q, k, v, attn, cum, rise, *outs, *d_mixes, *entering, *rows, *grads[:early])
    if seq_size > 2:
        through = [
            kept * jnp.sum(g.astype(F32) * s.astype(F32), axis=(1, 2))[:, None]
            for g, s in zip(grads, entering)
        ]
        through = jnp.concatenate(through, axis=0) * jnp.exp(cum[:, -1:])
        through = through * (jnp.arange(tokens) == tokens - 1).astype(F32)
    else:
        through = jnp.zeros((heads, tokens), F32)

    piece = 3 * width // (pairs * CORES * seq_size)
    exchanged = cores == CORES and piece >= 128 and piece % 64 == 0 and heads % 16 == 0
    others = pairs * seq_size
    packed = piece * heads // 128
    if exchanged:
        part_shapes = (shape((others, packed, 128), BF16),) * 2
        scratch = [pltpu.VMEM((CORES, others, packed, 128), BF16)]
    else:
        part_shapes = (shape((heads, 3 * width), F32),)
        scratch = []
    d_logits, *parts = pl.pallas_call(
        functools.partial(logit_kernel, groups, early, seq_size),
        out_shape=(shape((heads, tokens), BF16),) + part_shapes,
        in_specs=[spec()] * (7 + len(groups) - early),
        out_specs=(spec(),) * (1 + len(part_shapes)),
        scratch_shapes=scratch,
        compiler_params=params(),
        cost_estimate=cost(),
        name="logits",
    )(q, k, v, cum, logits, terms, through, *grads[early:])

    input_grads = pl.pallas_call(
        functools.partial(finish_kernel, groups, early, seq_size),
        out_shape=(shape((tokens, width), BF16),) * 3,
        in_specs=[spec()] * (8 + len(groups) - early),
        out_specs=(hbm(),) * 3,
        scratch_shapes=[
            pltpu.VMEM((3, tokens, width), BF16),
            pltpu.SemaphoreType.DMA((3 * -(-heads // STAGE),)),
        ],
        compiler_params=params(),
        cost_estimate=cost(),
        name="finish",
    )(gq, gk, gv, k, v, cum, d_logits, gate, *grads[early:])

    if exchanged:
        keep, send = parts
        arrived = lax.ppermute(send, "core", [(0, 1), (1, 0)])
        total = (keep.astype(F32) + arrived.astype(F32)).astype(BF16)
        total, *input_grads = lax.optimization_barrier((total, *input_grads))
        arrived = lax.all_to_all(total, ("pair", "seq"), 0, 0, tiled=True)
        grad_gate = pl.pallas_call(
            sum_kernel,
            out_shape=shape((heads, piece), F32),
            in_specs=[spec()],
            out_specs=spec(),
            compiler_params=params(),
            name="sum",
        )(arrived).T
    else:
        grad_gate = lax.psum_scatter(
            parts[0].T, ("pair", "core", "seq"), scatter_dimension=0, tiled=True
        )
    return output[None], *[g[None] for g in input_grads], grad_gate


def solution(mesh):
    rows, slots = mesh.devices.shape
    cores = CORES if rows % CORES == 0 else 1
    devices = mesh.devices.reshape(rows // cores, cores, slots)
    mesh = jax.sharding.Mesh(devices, ("pair", "core", "seq"))
    row = ("pair", "core")
    tokens = P(row, "seq", None)
    return jax.shard_map(
        functools.partial(body, rows // cores, cores, slots),
        mesh=mesh,
        in_specs=(tokens, tokens, tokens, P(row, None, "seq"), P(), P(row, "seq"), tokens),
        out_specs=(tokens, tokens, tokens, tokens, P((*row, "seq"), None)),
        check_vma=False,
    )
```

time: 48.4 us -> 45.8 us (0.946)
  blocking collectives: 0 us -> 14.5 us
  starting transfers between devices: 18.9 us -> 10.7 us
  waiting for transfers between devices: 12.5 us -> 4.47 us
  other arithmetic: 0.75 us -> 0.03 us
  Pallas kernels: 13.7 us -> 13.2 us
    all_to_all x0 -> x1, blocking collectives: none -> 14.5 us  [body(): arrived = lax.all_to_all(total, ('pair', 'seq'), 0, 0, tiled=True)]
    ppermute x5 -> x1, starting transfers between devices: 8.24 us -> 0.07 us  [body(): arrived = lax.ppermute(send, 'core', [(0, 1), (1, 0)])]
    ppermute x5 -> x1, waiting for transfers between devices: 5.78 us -> 0.01 us  [body(): arrived = lax.ppermute(send, 'core', [(0, 1), (1, 0)])]
    ppermute x4, waiting for transfers between devices: 4.57 us -> 2.33 us  [chain(): return lax.ppermute(own, 'seq', [(0, 1), (1, 0)])]
    transpose x1 -> x0, other arithmetic: 0.69 us -> none  [body(): grad_gate = lax.dynamic_slice_in_dim(total, slot * piece, piece, axis=1).T]
    pallas_call x7 -> x6, Pallas kernels: 11 us -> 10.6 us  [the longest x1 3.31 us: body(): pl.pallas_call(functools.partial(gate_kernel, groups[:ahead]), out_shape=...]
    unnamed x4 -> x16, local copies, waits for them, and re-layouts: 0.96 us -> 1.11 us
  transfers between devices with their start and end apart: 11 -> 7, of which waited for: 9 -> 4; matrix products, arithmetic and copies ran while one was open for 0% -> 0% of each run, Pallas kernels for 19% -> 17%
where the time goes in v4:
time: 45.8 us; the launch traced here: 45.5 us
  blocking collectives  14.5 us (32%)
  Pallas kernels  13.2 us (29%)
  starting transfers between devices  10.7 us (23%)
  waiting for transfers between devices  4.47 us (10%)
  between operations  1.45 us (3%)
  local copies, waits for them, and re-layouts  1.11 us (2%)
    all_to_all x1, blocking collectives, body(): arrived = lax.all_to_all(total, ('pair', 'seq'), 0, 0, tiled=True)  14.5 us
    ppermute x4, starting transfers between devices, chain(): return lax.ppermute(own, 'seq', [(0, 1), (1, 0)])  7.05 us
    ppermute x2, starting transfers between devices, body(): arrived = lax.ppermute(pushed, 'seq', [(0, 1), (1, 0)])  3.58 us
    pallas_call x1, Pallas kernels, body(): pl.pallas_call(functools.partial(gate_kernel, groups[:ahead]), out_shape=...  3.31 us
    pallas_call x1, Pallas kernels, body(): pl.pallas_call(functools.partial(back_kernel, groups, early, seq_size), o...  2.63 us
    pallas_call x4, Pallas kernels, body(): pl.pallas_call(functools.partial(mix_kernel, first, count), out_shape=(sh...  2.62 us
    ppermute x4, waiting for transfers between devices, chain(): return lax.ppermute(own, 'seq', [(0, 1), (1, 0)])  2.33 us
    ppermute x2, waiting for transfers between devices, body(): arrived = lax.ppermute(pushed, 'seq', [(0, 1), (1, 0)])  2.14 us
  transfers between devices with their start and end apart: 7, of which 4 were waited for; matrix products, arithmetic and copies ran while one was open for 0% of the time, Pallas kernels for 17%

profile of v4, /device:TPU:0, one launch (start us, length us, event | category | flops | bytes accessed | tf_op | source)
XLA Modules:
  0.0 45.5 jit_solution(16199994447637551402)
XLA Ops:
  0.6 0.0 copy-start
  0.6 0.0 copy-start.1
  0.7 0.0 copy-start.2
  0.7 3.3 %gate.1 = (f32[16,128]{1,0:T(8,128)}, f32[16,128]{1,0:T(8,128)}, bf16[4,128,128]{2,1,0:T(8,128)(2,1)}, bf16[4,128,128]{2,1,0:T(8,128)(2,1)}) custom-call(bf16[128,2048]{1,0:T(8,128)(2,1)} %bitcast.11, bf16[128,2048]{1,0:T(8,128)(2,1)} %bitcast.24, bf16[128,2048]{1,0:T(8,128)(2,1)} %bitcast.29, f32[16,128]{1,0:T(8,128)} %bitcast.37, bf16[16,6144]{1,0:T(8,128)(2,1)} %bitcast.34), custom_call_target="tpu_custom_call" | custom-call | flops 1000 | bytes 1000 | tf_op jit(solution)/shard_map/gate/pallas_call | solution.py:382
  4.0 0.0 copy-start.6
  4.0 3.0 %collective-permute-start.1 = (bf16[4,128,128]{2,1,0:T(8,128)(2,1)}, bf16[4,128,128]{2,1,0:T(8,128)(2,1)S(1)}, u32[]{:S(2)}, u32[]{:S(2)}) collective-permute-start(bf16[4,128,128]{2,1,0:T(8,128)(2,1)} %get-tuple-element.52), channel_id=1, source_target_pairs={{0,1},{1,0},{2,3},{3,2},{4,5},{5,4},{6,7},{7,6},{8,9},{9,8},{10,11... | collective-permute-start | bytes 393224 | tf_op jit(solution)/shard_map/ppermute | solution.py:418
  7.0 0.1 collective-permute-start
  7.7 0.0 copy-done
  7.7 0.0 copy-done.1
  7.7 0.0 copy-done.2
  7.8 0.0 copy-done.6
  7.8 0.0 copy-start.3
  7.8 1.0 %copy-done.3 = bf16[1,128,2048]{2,1,0:T(8,128)(2,1)S(1)} copy-done((bf16[1,128,2048]{2,1,0:T(8,128)(2,1)S(1)}, bf16[1,128,2048]{2,1,0:T(8,128)(2,1)}, u32[]{:S(2)}) %copy-start.3) | copy-done | bytes 524312
  8.8 1.0 %within.1 = (bf16[16,128,128]{2,1,0:T(8,128)(2,1)S(1)}, f32[128,2048]{1,0:T(8,128)S(1)}, f32[16,128]{1,0:T(8,128)S(1)}, bf16[4,128,128]{2,1,0:T(8,128)(2,1)S(1)}, bf16[4,128,128]{2,1,0:T(8,128)(2,1)S(1)}) custom-call(bf16[128,2048]{1,0:T(8,128)(2,1)S(1)} %bitcast.12, bf16[128,2048]{1,0:T(8,128)(2,1)S(1)} %bitcast.25, bf16[128,2048]{1,0:T(8,128)(2,1)S(1)} %bitcast.30, ...), custom_call_target="tpu_custom_call" | custom-call | flops 1000 | bytes 1000 | tf_op jit(solution)/shard_map/within/pallas_call | solution.py:400
  9.8 1.7 %collective-permute-done.1.state.refs_15_ = bf16[4,128,128]{2,1,0:T(8,128)(2,1)S(1)} collective-permute-done((bf16[4,128,128]{2,1,0:T(8,128)(2,1)}, bf16[4,128,128]{2,1,0:T(8,128)(2,1)S(1)}, u32[]{:S(2)}, u32[]{:S(2)}) %collective-permute-start.1) | collective-permute-done | bytes 131104 | tf_op jit(solution)/shard_map/ppermute | solution.py:418
  11.5 0.7 %mix.5 = (bf16[128,512]{1,0:T(8,128)(2,1)S(1)}, bf16[128,512]{1,0:T(8,128)(2,1)S(1)}, bf16[4,128,128]{2,1,0:T(8,128)(2,1)S(1)}, f32[4,128]{1,0:T(4,128)S(1)}) custom-call(bf16[128,2048]{1,0:T(8,128)(2,1)S(1)} %bitcast.13, f32[128,2048]{1,0:T(8,128)S(1)} %get-tuple-element.48.within, bf16[128,2048]{1,0:T(8,128)(2,1)S(1)} %bitcast.20, ...), custom_call_target="tpu_custom_call" | custom-call | flops 1000 | bytes 1000 | tf_op jit(solution)/shard_map/mix/pallas_call | solution.py:430
  12.2 2.1 %collective-permute-start.3 = (bf16[4,128,128]{2,1,0:T(8,128)(2,1)S(1)}, bf16[4,128,128]{2,1,0:T(8,128)(2,1)S(1)}, u32[]{:S(2)}, u32[]{:S(2)}) collective-permute-start(bf16[4,128,128]{2,1,0:T(8,128)(2,1)S(1)} %get-tuple-element.57), channel_id=1, source_target_pairs={{0,1},{1,0},{2,3},{3,2},{4,5},{5,4},{6,7},{7,6},{8,9},{9,8},{10,11... | collective-permute-start | bytes 393224 | tf_op jit(solution)/shard_map/ppermute | solution.py:448
  14.3 0.0 collective-permute-done.state.refs_14_
  14.3 0.7 %mix.4 = (bf16[128,512]{1,0:T(8,128)(2,1)S(1)}, bf16[128,512]{1,0:T(8,128)(2,1)S(1)}, bf16[4,128,128]{2,1,0:T(8,128)(2,1)S(1)}, f32[4,128]{1,0:T(4,128)S(1)}) custom-call(bf16[128,2048]{1,0:T(8,128)(2,1)S(1)} %bitcast.14, f32[128,2048]{1,0:T(8,128)S(1)} %get-tuple-element.48.within, bf16[128,2048]{1,0:T(8,128)(2,1)S(1)} %bitcast.21, ...), custom_call_target="tpu_custom_call" | custom-call | flops 1000 | bytes 1000 | tf_op jit(solution)/shard_map/mix/pallas_call | solution.py:430
  15.0 1.5 %collective-permute-start.2 = (bf16[4,128,128]{2,1,0:T(8,128)(2,1)S(1)}, bf16[4,128,128]{2,1,0:T(8,128)(2,1)S(1)}, u32[]{:S(2)}, u32[]{:S(2)}) collective-permute-start(bf16[4,128,128]{2,1,0:T(8,128)(2,1)S(1)} %get-tuple-element.55), channel_id=1, source_target_pairs={{0,1},{1,0},{2,3},{3,2},{4,5},{5,4},{6,7},{7,6},{8,9},{9,8},{10,11... | collective-permute-start | bytes 393224 | tf_op jit(solution)/shard_map/ppermute | solution.py:448
  16.4 2.0 %collective-permute-done.3.state.refs_17_.refs_23_ = bf16[4,128,128]{2,1,0:T(8,128)(2,1)S(1)} collective-permute-done((bf16[4,128,128]{2,1,0:T(8,128)(2,1)S(1)}, bf16[4,128,128]{2,1,0:T(8,128)(2,1)S(1)}, u32[]{:S(2)}, u32[]{:S(2)}) %collective-permute-start.3) | collective-permute-done | bytes 131104 | tf_op jit(solution)/shard_map/ppermute | solution.py:448
  18.4 0.7 %mix.7 = (bf16[128,512]{1,0:T(8,128)(2,1)S(1)}, bf16[128,512]{1,0:T(8,128)(2,1)S(1)}, bf16[4,128,128]{2,1,0:T(8,128)(2,1)S(1)}, f32[4,128]{1,0:T(4,128)S(1)}) custom-call(bf16[128,2048]{1,0:T(8,128)(2,1)S(1)} %bitcast.15, f32[128,2048]{1,0:T(8,128)S(1)} %get-tuple-element.48.within, bf16[128,2048]{1,0:T(8,128)(2,1)S(1)} %bitcast.22, ...), custom_call_target="tpu_custom_call" | custom-call | flops 1000 | bytes 1000 | tf_op jit(solution)/shard_map/mix/pallas_call | solution.py:430
  19.1 0.0 copy-start.4
  19.1 2.2 %collective-permute-start.5 = (bf16[4,128,128]{2,1,0:T(8,128)(2,1)S(1)}, bf16[4,128,128]{2,1,0:T(8,128)(2,1)S(1)}, u32[]{:S(2)}, u32[]{:S(2)}) collective-permute-start(bf16[4,128,128]{2,1,0:T(8,128)(2,1)S(1)} %get-tuple-element.71), channel_id=1, source_target_pairs={{0,1},{1,0},{2,3},{3,2},{4,5},{5,4},{6,7},{7,6},{8,9},{9,8},{10,11... | collective-permute-start | bytes 393224 | tf_op jit(solution)/shard_map/ppermute | solution.py:418
  21.3 0.1 collective-permute-done.2.state.refs_16_.refs_22_
  21.5 0.7 %mix.6 = (bf16[128,512]{1,0:T(8,128)(2,1)S(1)}, bf16[128,512]{1,0:T(8,128)(2,1)S(1)}, bf16[4,128,128]{2,1,0:T(8,128)(2,1)S(1)}, f32[4,128]{1,0:T(4,128)S(1)}) custom-call(bf16[128,2048]{1,0:T(8,128)(2,1)S(1)} %bitcast.16, f32[128,2048]{1,0:T(8,128)S(1)} %get-tuple-element.48.within, bf16[128,2048]{1,0:T(8,128)(2,1)S(1)} %bitcast.23, ...), custom_call_target="tpu_custom_call" | custom-call | flops 1000 | bytes 1000 | tf_op jit(solution)/shard_map/mix/pallas_call | solution.py:430
  22.1 1.7 %collective-permute-start.4 = (bf16[4,128,128]{2,1,0:T(8,128)(2,1)S(1)}, bf16[4,128,128]{2,1,0:T(8,128)(2,1)S(1)}, u32[]{:S(2)}, u32[]{:S(2)}) collective-permute-start(bf16[4,128,128]{2,1,0:T(8,128)(2,1)S(1)} %get-tuple-element.70), channel_id=1, source_target_pairs={{0,1},{1,0},{2,3},{3,2},{4,5},{5,4},{6,7},{7,6},{8,9},{9,8},{10,11... | collective-permute-start | bytes 393224 | tf_op jit(solution)/shard_map/ppermute | solution.py:418
  23.9 0.0 copy-done.4
  23.9 2.6 %back.1 = (bf16[128,2048]{1,0:T(8,128)(2,1)}, f32[128,2048]{1,0:T(8,128)S(1)}, f32[128,2048]{1,0:T(8,128)S(1)}, f32[128,2048]{1,0:T(8,128)S(1)}, f32[16,128]{1,0:T(8,128)S(1)}) custom-call(bf16[128,2048]{1,0:T(8,128)(2,1)S(1)} %bitcast.17, bf16[128,2048]{1,0:T(8,128)(2,1)S(1)} %bitcast.26, bf16[128,2048]{1,0:T(8,128)(2,1)S(1)} %bitcast.31, ...), custom_call_target="tpu_custom_call" | custom-call | flops 1000 | bytes 1000 | tf_op jit(solution)/shard_map/back/pallas_call | solution.py:455
  26.5 0.0 copy-start.7
  26.5 0.0 collective-permute-done.5.refs_1_
  26.5 0.6 %collective-permute-done.4.refs_0_ = bf16[4,128,128]{2,1,0:T(8,128)(2,1)S(1)} collective-permute-done((bf16[4,128,128]{2,1,0:T(8,128)(2,1)S(1)}, bf16[4,128,128]{2,1,0:T(8,128)(2,1)S(1)}, u32[]{:S(2)}, u32[]{:S(2)}) %collective-permute-start.4) | collective-permute-done | bytes 131104 | tf_op jit(solution)/shard_map/ppermute | solution.py:418
  27.2 0.0 copy-done.7
  27.2 0.0 copy-start.5
  27.2 1.3 %logits.1 = (bf16[16,128]{1,0:T(8,128)(2,1)S(1)}, bf16[16,24,128]{2,1,0:T(8,128)(2,1)S(1)}, bf16[16,24,128]{2,1,0:T(8,128)(2,1)S(1)}) custom-call(bf16[128,2048]{1,0:T(8,128)(2,1)S(1)} %bitcast.18, bf16[128,2048]{1,0:T(8,128)(2,1)S(1)} %bitcast.27, bf16[128,2048]{1,0:T(8,128)(2,1)S(1)} %bitcast.32, f32[16,128]{1,0:T(8,128)S(1)} %copy-done.6, ...), custom_call_target="tpu_custom_call" | custom-call | flops 1000 | bytes 1000 | tf_op jit(solution)/shard_map/logits/pallas_call | solution.py:487
  28.5 0.1 collective-permute-start.6
  28.6 0.0 copy-done.5
  28.6 1.7 %finish.1 = (bf16[128,2048]{1,0:T(8,128)(2,1)}, bf16[128,2048]{1,0:T(8,128)(2,1)}, bf16[128,2048]{1,0:T(8,128)(2,1)}) custom-call(f32[128,2048]{1,0:T(8,128)S(1)} %get-tuple-element.74.gq, f32[128,2048]{1,0:T(8,128)S(1)} %get-tuple-element.75.gk, f32[128,2048]{1,0:T(8,128)S(1)} %get-tuple-element.76.gv, bf16[128,2048]{1,0:T(8,128)(2,1)S(1)} %bitcast.28, ...), custom_call_target="tpu_custom_call" | custom-call | flops 1000 | bytes 1000 | tf_op jit(solution)/shard_map/finish/pallas_call | solution.py:498
  30.3 0.0 collective-permute-done.6
  30.3 14.5 %all_to_all.5.arrived = bf16[16,24,128]{2,1,0:T(8,128)(2,1)S(1)} all-to-all(bf16[16,24,128]{2,1,0:T(8,128)(2,1)S(1)} %add_convert_fusion), channel_id=1, replica_groups=mesh['pair'=8,'core'=2,'seq'=2] {'pair','seq'}, dimensions={0} | all-to-all | bytes 196608 | tf_op jit(solution)/shard_map/all_to_all | solution.py:517
  44.8 0.7 %sum.1 = f32[16,192]{1,0:T(8,128)} custom-call(bf16[16,24,128]{2,1,0:T(8,128)(2,1)S(1)} %all_to_all.5.arrived), custom_call_target="tpu_custom_call" | custom-call | tf_op jit(solution)/shard_map/sum/pallas_call | solution.py:518
  (2 shorter events, 0.0 us)
Async XLA Ops:
  0.6 7.1 %copy-start = (bf16[1,128,2048]{2,1,0:T(8,128)(2,1)S(1)}, bf16[1,128,2048]{2,1,0:T(8,128)(2,1)}, u32[]{:S(2)}) copy-start(bf16[1,128,2048]{2,1,0:T(8,128)(2,1)} %param.7) | copy-start | bytes 1572868
  0.6 7.1 %copy-start.1 = (bf16[1,128,2048]{2,1,0:T(8,128)(2,1)S(1)}, bf16[1,128,2048]{2,1,0:T(8,128)(2,1)}, u32[]{:S(2)}) copy-start(bf16[1,128,2048]{2,1,0:T(8,128)(2,1)} %param.13) | copy-start | bytes 1572868
  0.7 7.1 %copy-start.2 = (bf16[1,128,2048]{2,1,0:T(8,128)(2,1)S(1)}, bf16[1,128,2048]{2,1,0:T(8,128)(2,1)}, u32[]{:S(2)}) copy-start(bf16[1,128,2048]{2,1,0:T(8,128)(2,1)} %param.8) | copy-start | bytes 1572868
  4.0 3.8 %copy-start.6 = (f32[16,128]{1,0:T(8,128)S(1)}, f32[16,128]{1,0:T(8,128)}, u32[]{:S(2)}) copy-start(f32[16,128]{1,0:T(8,128)} %get-tuple-element.45.cum_ref.refs_4_) | copy-start | bytes 24580
  4.0 7.5 %collective-permute-start.1 = (bf16[4,128,128]{2,1,0:T(8,128)(2,1)}, bf16[4,128,128]{2,1,0:T(8,128)(2,1)S(1)}, u32[]{:S(2)}, u32[]{:S(2)}) collective-permute-start(bf16[4,128,128]{2,1,0:T(8,128)(2,1)} %get-tuple-element.52), channel_id=1, source_target_pairs={{0,1},{1,0},{2,3},{3,2},{4,5},{5,4},{6,7},{7,6},{8,9},{9,8},{10,11... | collective-permute-start | bytes 393224 | tf_op jit(solution)/shard_map/ppermute | solution.py:418
  7.0 7.3 %collective-permute-start = (bf16[4,128,128]{2,1,0:T(8,128)(2,1)}, bf16[4,128,128]{2,1,0:T(8,128)(2,1)S(1)}, u32[]{:S(2)}, u32[]{:S(2)}) collective-permute-start(bf16[4,128,128]{2,1,0:T(8,128)(2,1)} %get-tuple-element.49), channel_id=1, source_target_pairs={{0,1},{1,0},{2,3},{3,2},{4,5},{5,4},{6,7},{7,6},{8,9},{9,8},{10,11... | collective-permute-start | bytes 393224 | tf_op jit(solution)/shard_map/ppermute | solution.py:418
  7.8 1.0 %copy-start.3 = (bf16[1,128,2048]{2,1,0:T(8,128)(2,1)S(1)}, bf16[1,128,2048]{2,1,0:T(8,128)(2,1)}, u32[]{:S(2)}) copy-start(bf16[1,128,2048]{2,1,0:T(8,128)(2,1)} %param.9) | copy-start | bytes 1572868
  12.2 6.2 %collective-permute-start.3 = (bf16[4,128,128]{2,1,0:T(8,128)(2,1)S(1)}, bf16[4,128,128]{2,1,0:T(8,128)(2,1)S(1)}, u32[]{:S(2)}, u32[]{:S(2)}) collective-permute-start(bf16[4,128,128]{2,1,0:T(8,128)(2,1)S(1)} %get-tuple-element.57), channel_id=1, source_target_pairs={{0,1},{1,0},{2,3},{3,2},{4,5},{5,4},{6,7},{7,6},{8,9},{9,8},{10,11... | collective-permute-start | bytes 393224 | tf_op jit(solution)/shard_map/ppermute | solution.py:448
  15.0 6.5 %collective-permute-start.2 = (bf16[4,128,128]{2,1,0:T(8,128)(2,1)S(1)}, bf16[4,128,128]{2,1,0:T(8,128)(2,1)S(1)}, u32[]{:S(2)}, u32[]{:S(2)}) collective-permute-start(bf16[4,128,128]{2,1,0:T(8,128)(2,1)S(1)} %get-tuple-element.55), channel_id=1, source_target_pairs={{0,1},{1,0},{2,3},{3,2},{4,5},{5,4},{6,7},{7,6},{8,9},{9,8},{10,11... | collective-permute-start | bytes 393224 | tf_op jit(solution)/shard_map/ppermute | solution.py:448
  19.1 4.8 %copy-start.4 = (bf16[1,128,2048]{2,1,0:T(8,128)(2,1)S(1)}, bf16[1,128,2048]{2,1,0:T(8,128)(2,1)}, u32[]{:S(2)}) copy-start(bf16[1,128,2048]{2,1,0:T(8,128)(2,1)} %param.9) | copy-start | bytes 1572868
  19.1 7.4 %collective-permute-start.5 = (bf16[4,128,128]{2,1,0:T(8,128)(2,1)S(1)}, bf16[4,128,128]{2,1,0:T(8,128)(2,1)S(1)}, u32[]{:S(2)}, u32[]{:S(2)}) collective-permute-start(bf16[4,128,128]{2,1,0:T(8,128)(2,1)S(1)} %get-tuple-element.71), channel_id=1, source_target_pairs={{0,1},{1,0},{2,3},{3,2},{4,5},{5,4},{6,7},{7,6},{8,9},{9,8},{10,11... | collective-permute-start | bytes 393224 | tf_op jit(solution)/shard_map/ppermute | solution.py:418
  22.1 5.0 %collective-permute-start.4 = (bf16[4,128,128]{2,1,0:T(8,128)(2,1)S(1)}, bf16[4,128,128]{2,1,0:T(8,128)(2,1)S(1)}, u32[]{:S(2)}, u32[]{:S(2)}) collective-permute-start(bf16[4,128,128]{2,1,0:T(8,128)(2,1)S(1)} %get-tuple-element.70), channel_id=1, source_target_pairs={{0,1},{1,0},{2,3},{3,2},{4,5},{5,4},{6,7},{7,6},{8,9},{9,8},{10,11... | collective-permute-start | bytes 393224 | tf_op jit(solution)/shard_map/ppermute | solution.py:418
  26.5 0.7 %copy-start.7 = (f32[16,128]{1,0:T(8,128)S(1)}, f32[16,128]{1,0:T(8,128)}, u32[]{:S(2)}) copy-start(f32[16,128]{1,0:T(8,128)} %get-tuple-element.68.logits_ref) | copy-start | bytes 24580
  27.2 1.4 %copy-start.5 = (bf16[6144,16]{0,1:T(8,128)(2,1)S(1)}, bf16[6144,16]{0,1:T(8,128)(2,1)}, u32[]{:S(2)}) copy-start(bf16[6144,16]{0,1:T(8,128)(2,1)} %param.11) | copy-start | bytes 589828
  28.5 1.8 %collective-permute-start.6 = (bf16[16,24,128]{2,1,0:T(8,128)(2,1)S(1)}, bf16[16,24,128]{2,1,0:T(8,128)(2,1)S(1)}, u32[]{:S(2)}, u32[]{:S(2)}) collective-permute-start(bf16[16,24,128]{2,1,0:T(8,128)(2,1)S(1)} %get-tuple-element.73), channel_id=1, source_target_pairs={{0,2},{2,0},{1,3},{3,1},{4,6},{6,4},{5,7},{7,5},{8,10},{10,8},{9,1... | collective-permute-start | bytes 294920 | tf_op jit(solution)/shard_map/ppermute | solution.py:514

commit v5 on v4

--- a/solution.py
+++ b/solution.py
@@ -95,7 +95,7 @@
             out[i] = product.astype(BF16)
 
 
-def gate_kernel(groups, q_in, k_in, v_in, bias_in, gate_in, *refs):
+def gate_kernel(groups, slots, q_in, k_in, v_in, bias_in, gate_in, *refs):
     logits_ref, cum_ref, *updates = refs[: 2 + len(groups)]
     q, k, v, bias, gate, sems = refs[2 + len(groups) :]
     pairs = ((gate_in, gate), (bias_in, bias), (k_in, k), (q_in, q), (v_in, v))
@@ -109,7 +109,6 @@
     for copy in copies[:3]:
         copy.wait()
     logits = bias[...] + dot_nt(gate[:, width : 2 * width], k[...])
-    turned = turn(k, updates[0].shape[1], groups)
     copies[3].wait()
     logits = logits + dot_nt(gate[:, :width], q[...])
     copies[4].wait()
@@ -118,12 +117,23 @@
     soft = jnp.maximum(logits, 0.0) + jnp.log1p(jnp.exp(-jnp.abs(logits)))
     cum = exact_dot(-soft, triangle(logits.shape[1], True))
     cum_ref[...] = cum
-    add_updates(turned, v, cum, groups, updates)
-
-
-def within_kernel(heads, groups, q, k, v, cum_ref, cot, resets, attn_ref, within, rise_ref, *updates):
-    del cot
-    rise_ref[...] = (1 - resets[0, 0]).astype(F32) * jnp.exp(cum_ref[...])
+    if slots > 2:
+        add_updates(turn(k, updates[0].shape[1], groups), v, cum, groups, updates)
+        return
+    opening = lax.axis_index("seq") == 0
+
+    @pl.when(opening)
+    def _():
+        add_updates(turn(k, updates[0].shape[1], groups), v, cum, groups, updates)
+
+    @pl.when(jnp.logical_not(opening))
+    def _():
+        for update in updates:
+            update[...] = jnp.zeros(update.shape, update.dtype)
+
+
+def within_kernel(heads, groups, q, k, v, cum_ref, resets, attn_ref, within, rise_ref, *updates):
+    rise_ref[...] = (1 - resets[...]).astype(F32) * jnp.exp(cum_ref[...])
     size = q.shape[1] // heads
     if groups:
         add_updates(turn(k, size, groups), v, cum_ref[...], groups, updates)
@@ -357,8 +367,8 @@
 
 
 def head_groups(heads):
-    parts = 4 if heads >= 4 else 1
-    sizes = [heads // parts + (1 if i < heads % parts else 0) for i in range(parts)]
+    sizes=[3, 3, 2, 3, 3, 2]
+    parts=len(sizes)
     return [(sum(sizes[:i]), sizes[i]) for i in range(parts)]
 
 
@@ -378,9 +388,9 @@
     def state_shapes(some):
         return tuple(shape((count, size, size), BF16) for _, count in some)
 
-    ahead = 2 if seq_size == 2 and len(groups) > 2 else len(groups)
+    ahead = 3 if seq_size == 2 and len(groups) > 2 else len(groups)
     logits, cum, *updates = pl.pallas_call(
-        functools.partial(gate_kernel, groups[:ahead]),
+        functools.partial(gate_kernel, groups[:ahead], seq_size),
         out_shape=(shape((heads, tokens), F32),) * 2
         + state_shapes(groups[:ahead]),
         in_specs=[hbm()] * 5,
@@ -405,12 +415,12 @@
             shape((heads, tokens), F32),
         )
         + state_shapes(groups[ahead:]),
-        in_specs=[spec()] * 5 + [smem()],
+        in_specs=[spec()] * 5,
         out_specs=(spec(),) * (3 + len(groups) - ahead),
         compiler_params=params(),
         cost_estimate=cost(),
         name="within",
-    )(q, k, v, cum, cot, resets)
+    )(q, k, v, cum, resets)
     updates += made
 
     def chain(own, first, count, pairs):

time: 45.8 us -> 44.4 us (0.969)
  waiting for transfers between devices: 4.47 us -> 0.99 us
  starting transfers between devices: 10.7 us -> 13.5 us
  local copies, waits for them, and re-layouts: 1.11 us -> 0.06 us
  Pallas kernels: 13.2 us -> 14.1 us
  blocking collectives: 14.5 us -> 14 us
    ppermute x4 -> x6, starting transfers between devices: 7.05 us -> 8.96 us  [chain(): return lax.ppermute(own, 'seq', [(0, 1), (1, 0)])]
    ppermute x2 -> x3, waiting for transfers between devices: 2.14 us -> 0.25 us  [body(): arrived = lax.ppermute(pushed, 'seq', [(0, 1), (1, 0)])]
    ppermute x4 -> x6, waiting for transfers between devices: 2.33 us -> 0.74 us  [chain(): return lax.ppermute(own, 'seq', [(0, 1), (1, 0)])]
    unnamed x16 -> x14, local copies, waits for them, and re-layouts: 1.11 us -> 0.06 us
    ppermute x2 -> x3, starting transfers between devices: 3.58 us -> 4.49 us  [body(): arrived = lax.ppermute(pushed, 'seq', [(0, 1), (1, 0)])]
    pallas_call x4 -> x6, Pallas kernels: 2.62 us -> 3.35 us  [body(): pl.pallas_call(functools.partial(mix_kernel, first, count), out_shape=(sh...]
    all_to_all x1, blocking collectives: 14.5 us -> 14 us  [body(): arrived = lax.all_to_all(total, ('pair', 'seq'), 0, 0, tiled=True)]
  transfers between devices with their start and end apart: 7 -> 10, of which waited for: 4 -> 3; matrix products, arithmetic and copies ran while one was open for 0% -> 0% of each run, Pallas kernels for 17% -> 20%
where the time goes in v5:
time: 44.4 us; the launch traced here: 44.2 us
  Pallas kernels  14.1 us (32%)
  blocking collectives  14 us (32%)
  starting transfers between devices  13.5 us (30%)
  between operations  1.49 us (3%)
  waiting for transfers between devices  0.99 us (2%)
    all_to_all x1, blocking collectives, body(): arrived = lax.all_to_all(total, ('pair', 'seq'), 0, 0, tiled=True)  14 us
    ppermute x6, starting transfers between devices, chain(): return lax.ppermute(own, 'seq', [(0, 1), (1, 0)])  8.96 us
    ppermute x3, starting transfers between devices, body(): arrived = lax.ppermute(pushed, 'seq', [(0, 1), (1, 0)])  4.49 us
    pallas_call x1, Pallas kernels, body(): pl.pallas_call(functools.partial(gate_kernel, groups[:ahead], seq_size),...  3.38 us
    pallas_call x6, Pallas kernels, body(): pl.pallas_call(functools.partial(mix_kernel, first, count), out_shape=(sh...  3.35 us
    pallas_call x1, Pallas kernels, body(): pl.pallas_call(functools.partial(back_kernel, groups, early, seq_size), o...  2.71 us
    pallas_call x1, Pallas kernels, body(): pl.pallas_call(functools.partial(finish_kernel, groups, early, seq_size),...  1.68 us
    pallas_call x1, Pallas kernels, body(): pl.pallas_call(functools.partial(logit_kernel, groups, early, seq_size),...  1.29 us
  transfers between devices with their start and end apart: 10, of which 3 were waited for; matrix products, arithmetic and copies ran while one was open for 0% of the time, Pallas kernels for 20%

profile of v5, /device:TPU:0, one launch (start us, length us, event | category | flops | bytes accessed | tf_op | source)
XLA Modules:
  0.0 44.2 jit_solution(15264922888492432830)
XLA Ops:
  0.6 0.0 copy-start
  0.6 0.0 copy-start.2
  0.7 0.0 copy-start.3
  0.7 3.4 %gate.1 = (f32[16,128]{1,0:T(8,128)}, f32[16,128]{1,0:T(8,128)}, bf16[3,128,128]{2,1,0:T(8,128)(2,1)}, bf16[3,128,128]{2,1,0:T(8,128)(2,1)}, bf16[2,128,128]{2,1,0:T(8,128)(2,1)}) custom-call(bf16[128,2048]{1,0:T(8,128)(2,1)} %bitcast.11, bf16[128,2048]{1,0:T(8,128)(2,1)} %bitcast.27, bf16[128,2048]{1,0:T(8,128)(2,1)} %bitcast.32, f32[16,128]{1,0:T(8,128)} %bitcast.40, ...), custom_call_target="tpu_custom_call" | custom-call | flops 1000 | bytes 1000 | tf_op jit(solution)/shard_map/gate/pallas_call | solution.py:392
  4.0 0.0 copy-start.5
  4.1 2.7 %collective-permute-start.1 = (bf16[3,128,128]{2,1,0:T(8,128)(2,1)}, bf16[3,128,128]{2,1,0:T(8,128)(2,1)S(1)}, u32[]{:S(2)}, u32[]{:S(2)}) collective-permute-start(bf16[3,128,128]{2,1,0:T(8,128)(2,1)} %get-tuple-element.62), channel_id=1, source_target_pairs={{0,1},{1,0},{2,3},{3,2},{4,5},{5,4},{6,7},{7,6},{8,9},{9,8},{10,11... | collective-permute-start | bytes 294920 | tf_op jit(solution)/shard_map/ppermute | solution.py:428
  6.8 0.1 collective-permute-start
  6.9 1.9 %collective-permute-start.2 = (bf16[2,128,128]{2,1,0:T(8,128)(2,1)}, bf16[2,128,128]{2,1,0:T(8,128)(2,1)S(1)}, u32[]{:S(2)}, u32[]{:S(2)}) collective-permute-start(bf16[2,128,128]{2,1,0:T(8,128)(2,1)} %get-tuple-element.65), channel_id=1, source_target_pairs={{0,1},{1,0},{2,3},{3,2},{4,5},{5,4},{6,7},{7,6},{8,9},{9,8},{10,11... | collective-permute-start | bytes 196616 | tf_op jit(solution)/shard_map/ppermute | solution.py:428
  9.5 0.0 copy-done
  9.5 0.0 copy-done.2
  9.5 0.0 copy-done.3
  9.5 0.0 copy-done.5
  9.5 0.0 copy-start.1
  9.5 1.0 %within.1 = (bf16[16,128,128]{2,1,0:T(8,128)(2,1)S(1)}, f32[128,2048]{1,0:T(8,128)S(1)}, f32[16,128]{1,0:T(8,128)S(1)}, bf16[3,128,128]{2,1,0:T(8,128)(2,1)S(1)}...) custom-call(bf16[128,2048]{1,0:T(8,128)(2,1)S(1)} %bitcast.12, bf16[128,2048]{1,0:T(8,128)(2,1)S(1)} %bitcast.28, ...), custom_call_target="tpu_custom_call" | custom-call | flops 1000 | bytes 1000 | tf_op jit(solution)/shard_map/within/pallas_call | solution.py:410
  10.5 0.0 collective-permute-done.1.state.refs_19_
  10.5 0.0 copy-done.1
  10.6 0.6 %mix.7 = (bf16[128,384]{1,0:T(8,128)(2,1)S(1)}, bf16[128,384]{1,0:T(8,128)(2,1)S(1)}, bf16[3,128,128]{2,1,0:T(8,128)(2,1)S(1)}, f32[3,128]{1,0:T(4,128)S(1)}) custom-call(bf16[128,2048]{1,0:T(8,128)(2,1)S(1)} %bitcast.13, f32[128,2048]{1,0:T(8,128)S(1)} %get-tuple-element.58.within, bf16[128,2048]{1,0:T(8,128)(2,1)S(1)} %bitcast.21, ...), custom_call_target="tpu_custom_call" | custom-call | flops 1000 | bytes 1000 | tf_op jit(solution)/shard_map/mix/pallas_call | solution.py:440
  11.2 2.2 %collective-permute-start.4 = (bf16[3,128,128]{2,1,0:T(8,128)(2,1)S(1)}, bf16[3,128,128]{2,1,0:T(8,128)(2,1)S(1)}, u32[]{:S(2)}, u32[]{:S(2)}) collective-permute-start(bf16[3,128,128]{2,1,0:T(8,128)(2,1)S(1)} %get-tuple-element.70), channel_id=1, source_target_pairs={{0,1},{1,0},{2,3},{3,2},{4,5},{5,4},{6,7},{7,6},{8,9},{9,8},{10,11... | collective-permute-start | bytes 294920 | tf_op jit(solution)/shard_map/ppermute | solution.py:458
  13.4 0.0 collective-permute-done.state.refs_18_
  13.4 0.6 %mix.6 = (bf16[128,384]{1,0:T(8,128)(2,1)S(1)}, bf16[128,384]{1,0:T(8,128)(2,1)S(1)}, bf16[3,128,128]{2,1,0:T(8,128)(2,1)S(1)}, f32[3,128]{1,0:T(4,128)S(1)}) custom-call(bf16[128,2048]{1,0:T(8,128)(2,1)S(1)} %bitcast.14, f32[128,2048]{1,0:T(8,128)S(1)} %get-tuple-element.58.within, bf16[128,2048]{1,0:T(8,128)(2,1)S(1)} %bitcast.22, ...), custom_call_target="tpu_custom_call" | custom-call | flops 1000 | bytes 1000 | tf_op jit(solution)/shard_map/mix/pallas_call | solution.py:440
  14.0 1.5 %collective-permute-start.3 = (bf16[3,128,128]{2,1,0:T(8,128)(2,1)S(1)}, bf16[3,128,128]{2,1,0:T(8,128)(2,1)S(1)}, u32[]{:S(2)}, u32[]{:S(2)}) collective-permute-start(bf16[3,128,128]{2,1,0:T(8,128)(2,1)S(1)} %get-tuple-element.68), channel_id=1, source_target_pairs={{0,1},{1,0},{2,3},{3,2},{4,5},{5,4},{6,7},{7,6},{8,9},{9,8},{10,11... | collective-permute-start | bytes 294920 | tf_op jit(solution)/shard_map/ppermute | solution.py:458
  15.5 0.0 collective-permute-done.2.state.refs_20_
  15.5 0.5 %mix.8 = (bf16[128,256]{1,0:T(8,128)(2,1)S(1)}, bf16[128,256]{1,0:T(8,128)(2,1)S(1)}, bf16[2,128,128]{2,1,0:T(8,128)(2,1)S(1)}, f32[2,128]{1,0:T(2,128)S(1)}) custom-call(bf16[128,2048]{1,0:T(8,128)(2,1)S(1)} %bitcast.15, f32[128,2048]{1,0:T(8,128)S(1)} %get-tuple-element.58.within, bf16[128,2048]{1,0:T(8,128)(2,1)S(1)} %bitcast.23, ...), custom_call_target="tpu_custom_call" | custom-call | flops 1000 | bytes 1000 | tf_op jit(solution)/shard_map/mix/pallas_call | solution.py:440
  16.0 0.8 %collective-permute-start.5 = (bf16[2,128,128]{2,1,0:T(8,128)(2,1)S(1)}, bf16[2,128,128]{2,1,0:T(8,128)(2,1)S(1)}, u32[]{:S(2)}, u32[]{:S(2)}) collective-permute-start(bf16[2,128,128]{2,1,0:T(8,128)(2,1)S(1)} %get-tuple-element.72), channel_id=1, source_target_pairs={{0,1},{1,0},{2,3},{3,2},{4,5},{5,4},{6,7},{7,6},{8,9},{9,8},{10,11... | collective-permute-start | bytes 196616 | tf_op jit(solution)/shard_map/ppermute | solution.py:458
  16.8 0.2 collective-permute-done.4.state.refs_22_.refs_31_
  16.9 0.6 %mix.10 = (bf16[128,384]{1,0:T(8,128)(2,1)S(1)}, bf16[128,384]{1,0:T(8,128)(2,1)S(1)}, bf16[3,128,128]{2,1,0:T(8,128)(2,1)S(1)}, f32[3,128]{1,0:T(4,128)S(1)}) custom-call(bf16[128,2048]{1,0:T(8,128)(2,1)S(1)} %bitcast.16, f32[128,2048]{1,0:T(8,128)S(1)} %get-tuple-element.58.within, bf16[128,2048]{1,0:T(8,128)(2,1)S(1)} %bitcast.24, ...), custom_call_target="tpu_custom_call" | custom-call | flops 1000 | bytes 1000 | tf_op jit(solution)/shard_map/mix/pallas_call | solution.py:440
  17.5 2.1 %collective-permute-start.7 = (bf16[3,128,128]{2,1,0:T(8,128)(2,1)S(1)}, bf16[3,128,128]{2,1,0:T(8,128)(2,1)S(1)}, u32[]{:S(2)}, u32[]{:S(2)}) collective-permute-start(bf16[3,128,128]{2,1,0:T(8,128)(2,1)S(1)} %get-tuple-element.90), channel_id=1, source_target_pairs={{0,1},{1,0},{2,3},{3,2},{4,5},{5,4},{6,7},{7,6},{8,9},{9,8},{10,11... | collective-permute-start | bytes 294920 | tf_op jit(solution)/shard_map/ppermute | solution.py:428
  19.6 0.1 collective-permute-done.3.state.refs_21_.refs_30_
  19.7 0.6 %mix.9 = (bf16[128,384]{1,0:T(8,128)(2,1)S(1)}, bf16[128,384]{1,0:T(8,128)(2,1)S(1)}, bf16[3,128,128]{2,1,0:T(8,128)(2,1)S(1)}, f32[3,128]{1,0:T(4,128)S(1)}) custom-call(bf16[128,2048]{1,0:T(8,128)(2,1)S(1)} %bitcast.17, f32[128,2048]{1,0:T(8,128)S(1)} %get-tuple-element.58.within, bf16[128,2048]{1,0:T(8,128)(2,1)S(1)} %bitcast.25, ...), custom_call_target="tpu_custom_call" | custom-call | flops 1000 | bytes 1000 | tf_op jit(solution)/shard_map/mix/pallas_call | solution.py:440
  20.2 1.3 %collective-permute-start.6 = (bf16[3,128,128]{2,1,0:T(8,128)(2,1)S(1)}, bf16[3,128,128]{2,1,0:T(8,128)(2,1)S(1)}, u32[]{:S(2)}, u32[]{:S(2)}) collective-permute-start(bf16[3,128,128]{2,1,0:T(8,128)(2,1)S(1)} %get-tuple-element.89), channel_id=1, source_target_pairs={{0,1},{1,0},{2,3},{3,2},{4,5},{5,4},{6,7},{7,6},{8,9},{9,8},{10,11... | collective-permute-start | bytes 294920 | tf_op jit(solution)/shard_map/ppermute | solution.py:428
  21.5 0.0 collective-permute-done.5.state.refs_23_.refs_32_
  21.5 0.5 %mix.11 = (bf16[128,256]{1,0:T(8,128)(2,1)S(1)}, bf16[128,256]{1,0:T(8,128)(2,1)S(1)}, bf16[2,128,128]{2,1,0:T(8,128)(2,1)S(1)}, f32[2,128]{1,0:T(2,128)S(1)}) custom-call(bf16[128,2048]{1,0:T(8,128)(2,1)S(1)} %bitcast.18, f32[128,2048]{1,0:T(8,128)S(1)} %get-tuple-element.58.within, bf16[128,2048]{1,0:T(8,128)(2,1)S(1)} %bitcast.26, ...), custom_call_target="tpu_custom_call" | custom-call | flops 1000 | bytes 1000 | tf_op jit(solution)/shard_map/mix/pallas_call | solution.py:440
  22.0 0.9 %collective-permute-start.8 = (bf16[2,128,128]{2,1,0:T(8,128)(2,1)S(1)}, bf16[2,128,128]{2,1,0:T(8,128)(2,1)S(1)}, u32[]{:S(2)}, u32[]{:S(2)}) collective-permute-start(bf16[2,128,128]{2,1,0:T(8,128)(2,1)S(1)} %get-tuple-element.91), channel_id=1, source_target_pairs={{0,1},{1,0},{2,3},{3,2},{4,5},{5,4},{6,7},{7,6},{8,9},{9,8},{10,11... | collective-permute-start | bytes 196616 | tf_op jit(solution)/shard_map/ppermute | solution.py:428
  22.9 2.7 %back.1 = (bf16[128,2048]{1,0:T(8,128)(2,1)}, f32[128,2048]{1,0:T(8,128)S(1)}, f32[128,2048]{1,0:T(8,128)S(1)}, f32[128,2048]{1,0:T(8,128)S(1)}, f32[16,128]{1,0:T(8,128)S(1)}) custom-call(bf16[128,2048]{1,0:T(8,128)(2,1)S(1)} %bitcast.19, bf16[128,2048]{1,0:T(8,128)(2,1)S(1)} %bitcast.29, bf16[128,2048]{1,0:T(8,128)(2,1)S(1)} %bitcast.34, ...), custom_call_target="tpu_custom_call" | custom-call | flops 1000 | bytes 1000 | tf_op jit(solution)/shard_map/back/pallas_call | solution.py:465
  25.6 0.0 copy-start.6
  25.6 0.7 %collective-permute-done.8.refs_2_ = bf16[2,128,128]{2,1,0:T(8,128)(2,1)S(1)} collective-permute-done((bf16[2,128,128]{2,1,0:T(8,128)(2,1)S(1)}, bf16[2,128,128]{2,1,0:T(8,128)(2,1)S(1)}, u32[]{:S(2)}, u32[]{:S(2)}) %collective-permute-start.8) | collective-permute-done | bytes 65568 | tf_op jit(solution)/shard_map/ppermute | solution.py:428
  26.3 0.0 collective-permute-done.7.refs_1_
  26.4 0.0 collective-permute-done.6.refs_0_
  26.4 0.0 copy-done.6
  26.4 0.0 copy-start.4
  26.4 1.3 %logits.1 = (bf16[16,128]{1,0:T(8,128)(2,1)S(1)}, bf16[16,24,128]{2,1,0:T(8,128)(2,1)S(1)}, bf16[16,24,128]{2,1,0:T(8,128)(2,1)S(1)}) custom-call(bf16[128,2048]{1,0:T(8,128)(2,1)S(1)} %bitcast.20, bf16[128,2048]{1,0:T(8,128)(2,1)S(1)} %bitcast.30, bf16[128,2048]{1,0:T(8,128)(2,1)S(1)} %bitcast.35, f32[16,128]{1,0:T(8,128)S(1)} %copy-done.5, ...), custom_call_target="tpu_custom_call" | custom-call | flops 1000 | bytes 1000 | tf_op jit(solution)/shard_map/logits/pallas_call | solution.py:497
  27.7 0.1 collective-permute-start.9
  27.7 0.0 copy-done.4
  27.8 1.7 %finish.1 = (bf16[128,2048]{1,0:T(8,128)(2,1)}, bf16[128,2048]{1,0:T(8,128)(2,1)}, bf16[128,2048]{1,0:T(8,128)(2,1)}) custom-call(f32[128,2048]{1,0:T(8,128)S(1)} %get-tuple-element.94.gq, f32[128,2048]{1,0:T(8,128)S(1)} %get-tuple-element.95.gk, f32[128,2048]{1,0:T(8,128)S(1)} %get-tuple-element.96.gv, bf16[128,2048]{1,0:T(8,128)(2,1)S(1)} %bitcast.31, ...), custom_call_target="tpu_custom_call" | custom-call | flops 1000 | bytes 1000 | tf_op jit(solution)/shard_map/finish/pallas_call | solution.py:508
  29.4 0.0 collective-permute-done.9
  29.5 14.0 %all_to_all.5.arrived = bf16[16,24,128]{2,1,0:T(8,128)(2,1)S(1)} all-to-all(bf16[16,24,128]{2,1,0:T(8,128)(2,1)S(1)} %add_convert_fusion), channel_id=1, replica_groups=mesh['pair'=8,'core'=2,'seq'=2] {'pair','seq'}, dimensions={0} | all-to-all | bytes 196608 | tf_op jit(solution)/shard_map/all_to_all | solution.py:527
  43.5 0.7 %sum.1 = f32[16,192]{1,0:T(8,128)} custom-call(bf16[16,24,128]{2,1,0:T(8,128)(2,1)S(1)} %all_to_all.5.arrived), custom_call_target="tpu_custom_call" | custom-call | tf_op jit(solution)/shard_map/sum/pallas_call | solution.py:528
  (2 shorter events, 0.0 us)
Async XLA Ops:
  0.6 8.8 %copy-start = (bf16[1,128,2048]{2,1,0:T(8,128)(2,1)S(1)}, bf16[1,128,2048]{2,1,0:T(8,128)(2,1)}, u32[]{:S(2)}) copy-start(bf16[1,128,2048]{2,1,0:T(8,128)(2,1)} %param.7) | copy-start | bytes 1572868
  0.6 8.8 %copy-start.2 = (bf16[1,128,2048]{2,1,0:T(8,128)(2,1)S(1)}, bf16[1,128,2048]{2,1,0:T(8,128)(2,1)}, u32[]{:S(2)}) copy-start(bf16[1,128,2048]{2,1,0:T(8,128)(2,1)} %param.8) | copy-start | bytes 1572868
  0.7 8.8 %copy-start.3 = (bf16[1,128,2048]{2,1,0:T(8,128)(2,1)S(1)}, bf16[1,128,2048]{2,1,0:T(8,128)(2,1)}, u32[]{:S(2)}) copy-start(bf16[1,128,2048]{2,1,0:T(8,128)(2,1)} %param.9) | copy-start | bytes 1572868
  4.0 5.4 %copy-start.5 = (f32[16,128]{1,0:T(8,128)S(1)}, f32[16,128]{1,0:T(8,128)}, u32[]{:S(2)}) copy-start(f32[16,128]{1,0:T(8,128)} %get-tuple-element.55.cum_ref.refs_4_) | copy-start | bytes 24580
  4.1 6.5 %collective-permute-start.1 = (bf16[3,128,128]{2,1,0:T(8,128)(2,1)}, bf16[3,128,128]{2,1,0:T(8,128)(2,1)S(1)}, u32[]{:S(2)}, u32[]{:S(2)}) collective-permute-start(bf16[3,128,128]{2,1,0:T(8,128)(2,1)} %get-tuple-element.62), channel_id=1, source_target_pairs={{0,1},{1,0},{2,3},{3,2},{4,5},{5,4},{6,7},{7,6},{8,9},{9,8},{10,11... | collective-permute-start | bytes 294920 | tf_op jit(solution)/shard_map/ppermute | solution.py:428
  6.8 6.6 %collective-permute-start = (bf16[3,128,128]{2,1,0:T(8,128)(2,1)}, bf16[3,128,128]{2,1,0:T(8,128)(2,1)S(1)}, u32[]{:S(2)}, u32[]{:S(2)}) collective-permute-start(bf16[3,128,128]{2,1,0:T(8,128)(2,1)} %get-tuple-element.59), channel_id=1, source_target_pairs={{0,1},{1,0},{2,3},{3,2},{4,5},{5,4},{6,7},{7,6},{8,9},{9,8},{10,11... | collective-permute-start | bytes 294920 | tf_op jit(solution)/shard_map/ppermute | solution.py:428
  6.9 8.6 %collective-permute-start.2 = (bf16[2,128,128]{2,1,0:T(8,128)(2,1)}, bf16[2,128,128]{2,1,0:T(8,128)(2,1)S(1)}, u32[]{:S(2)}, u32[]{:S(2)}) collective-permute-start(bf16[2,128,128]{2,1,0:T(8,128)(2,1)} %get-tuple-element.65), channel_id=1, source_target_pairs={{0,1},{1,0},{2,3},{3,2},{4,5},{5,4},{6,7},{7,6},{8,9},{9,8},{10,11... | collective-permute-start | bytes 196616 | tf_op jit(solution)/shard_map/ppermute | solution.py:428
  9.5 1.0 %copy-start.1 = (bf16[1,128,2048]{2,1,0:T(8,128)(2,1)S(1)}, bf16[1,128,2048]{2,1,0:T(8,128)(2,1)}, u32[]{:S(2)}) copy-start(bf16[1,128,2048]{2,1,0:T(8,128)(2,1)} %param.13) | copy-start | bytes 1572868
  11.2 5.8 %collective-permute-start.4 = (bf16[3,128,128]{2,1,0:T(8,128)(2,1)S(1)}, bf16[3,128,128]{2,1,0:T(8,128)(2,1)S(1)}, u32[]{:S(2)}, u32[]{:S(2)}) collective-permute-start(bf16[3,128,128]{2,1,0:T(8,128)(2,1)S(1)} %get-tuple-element.70), channel_id=1, source_target_pairs={{0,1},{1,0},{2,3},{3,2},{4,5},{5,4},{6,7},{7,6},{8,9},{9,8},{10,11... | collective-permute-start | bytes 294920 | tf_op jit(solution)/shard_map/ppermute | solution.py:458
  14.0 5.7 %collective-permute-start.3 = (bf16[3,128,128]{2,1,0:T(8,128)(2,1)S(1)}, bf16[3,128,128]{2,1,0:T(8,128)(2,1)S(1)}, u32[]{:S(2)}, u32[]{:S(2)}) collective-permute-start(bf16[3,128,128]{2,1,0:T(8,128)(2,1)S(1)} %get-tuple-element.68), channel_id=1, source_target_pairs={{0,1},{1,0},{2,3},{3,2},{4,5},{5,4},{6,7},{7,6},{8,9},{9,8},{10,11... | collective-permute-start | bytes 294920 | tf_op jit(solution)/shard_map/ppermute | solution.py:458
  16.0 5.6 %collective-permute-start.5 = (bf16[2,128,128]{2,1,0:T(8,128)(2,1)S(1)}, bf16[2,128,128]{2,1,0:T(8,128)(2,1)S(1)}, u32[]{:S(2)}, u32[]{:S(2)}) collective-permute-start(bf16[2,128,128]{2,1,0:T(8,128)(2,1)S(1)} %get-tuple-element.72), channel_id=1, source_target_pairs={{0,1},{1,0},{2,3},{3,2},{4,5},{5,4},{6,7},{7,6},{8,9},{9,8},{10,11... | collective-permute-start | bytes 196616 | tf_op jit(solution)/shard_map/ppermute | solution.py:458
  17.5 8.8 %collective-permute-start.7 = (bf16[3,128,128]{2,1,0:T(8,128)(2,1)S(1)}, bf16[3,128,128]{2,1,0:T(8,128)(2,1)S(1)}, u32[]{:S(2)}, u32[]{:S(2)}) collective-permute-start(bf16[3,128,128]{2,1,0:T(8,128)(2,1)S(1)} %get-tuple-element.90), channel_id=1, source_target_pairs={{0,1},{1,0},{2,3},{3,2},{4,5},{5,4},{6,7},{7,6},{8,9},{9,8},{10,11... | collective-permute-start | bytes 294920 | tf_op jit(solution)/shard_map/ppermute | solution.py:428
  20.2 6.1 %collective-permute-start.6 = (bf16[3,128,128]{2,1,0:T(8,128)(2,1)S(1)}, bf16[3,128,128]{2,1,0:T(8,128)(2,1)S(1)}, u32[]{:S(2)}, u32[]{:S(2)}) collective-permute-start(bf16[3,128,128]{2,1,0:T(8,128)(2,1)S(1)} %get-tuple-element.89), channel_id=1, source_target_pairs={{0,1},{1,0},{2,3},{3,2},{4,5},{5,4},{6,7},{7,6},{8,9},{9,8},{10,11... | collective-permute-start | bytes 294920 | tf_op jit(solution)/shard_map/ppermute | solution.py:428
  22.0 4.3 %collective-permute-start.8 = (bf16[2,128,128]{2,1,0:T(8,128)(2,1)S(1)}, bf16[2,128,128]{2,1,0:T(8,128)(2,1)S(1)}, u32[]{:S(2)}, u32[]{:S(2)}) collective-permute-start(bf16[2,128,128]{2,1,0:T(8,128)(2,1)S(1)} %get-tuple-element.91), channel_id=1, source_target_pairs={{0,1},{1,0},{2,3},{3,2},{4,5},{5,4},{6,7},{7,6},{8,9},{9,8},{10,11... | collective-permute-start | bytes 196616 | tf_op jit(solution)/shard_map/ppermute | solution.py:428
  25.6 0.7 %copy-start.6 = (f32[16,128]{1,0:T(8,128)S(1)}, f32[16,128]{1,0:T(8,128)}, u32[]{:S(2)}) copy-start(f32[16,128]{1,0:T(8,128)} %get-tuple-element.87.logits_ref) | copy-start | bytes 24580
  26.4 1.4 %copy-start.4 = (bf16[6144,16]{0,1:T(8,128)(2,1)S(1)}, bf16[6144,16]{0,1:T(8,128)(2,1)}, u32[]{:S(2)}) copy-start(bf16[6144,16]{0,1:T(8,128)(2,1)} %param.11) | copy-start | bytes 589828
  27.7 1.8 %collective-permute-start.9 = (bf16[16,24,128]{2,1,0:T(8,128)(2,1)S(1)}, bf16[16,24,128]{2,1,0:T(8,128)(2,1)S(1)}, u32[]{:S(2)}, u32[]{:S(2)}) collective-permute-start(bf16[16,24,128]{2,1,0:T(8,128)(2,1)S(1)} %get-tuple-element.93), channel_id=1, source_target_pairs={{0,2},{2,0},{1,3},{3,1},{4,6},{6,4},{5,7},{7,5},{8,10},{10,8},{9,1... | collective-permute-start | bytes 294920 | tf_op jit(solution)/shard_map/ppermute | solution.py:524

commit v6 on v5

--- a/solution.py
+++ b/solution.py
@@ -95,9 +95,14 @@
             out[i] = product.astype(BF16)
 
 
+def cumulate(logits):
+    soft = jnp.maximum(logits, 0.0) + jnp.log1p(jnp.exp(-jnp.abs(logits)))
+    return exact_dot(-soft, triangle(logits.shape[1], True))
+
+
 def gate_kernel(groups, slots, q_in, k_in, v_in, bias_in, gate_in, *refs):
-    logits_ref, cum_ref, *updates = refs[: 2 + len(groups)]
-    q, k, v, bias, gate, sems = refs[2 + len(groups) :]
+    logits_ref, *updates = refs[: 1 + len(groups)]
+    q, k, v, bias, gate, sems = refs[1 + len(groups) :]
     pairs = ((gate_in, gate), (bias_in, bias), (k_in, k), (q_in, q), (v_in, v))
     copies = [
         pltpu.make_async_copy(source, target, sems.at[i])
@@ -114,17 +119,16 @@
     copies[4].wait()
     logits = logits + dot_nt(gate[:, 2 * width :], v[...])
     logits_ref[...] = logits
-    soft = jnp.maximum(logits, 0.0) + jnp.log1p(jnp.exp(-jnp.abs(logits)))
-    cum = exact_dot(-soft, triangle(logits.shape[1], True))
-    cum_ref[...] = cum
+
+    def run():
+        turned = turn(k, updates[0].shape[1], groups)
+        add_updates(turned, v, cumulate(logits), groups, updates)
+
     if slots > 2:
-        add_updates(turn(k, updates[0].shape[1], groups), v, cum, groups, updates)
+        run()
         return
     opening = lax.axis_index("seq") == 0
-
-    @pl.when(opening)
-    def _():
-        add_updates(turn(k, updates[0].shape[1], groups), v, cum, groups, updates)
+    pl.when(opening)(run)
 
     @pl.when(jnp.logical_not(opening))
     def _():
@@ -132,19 +136,21 @@
             update[...] = jnp.zeros(update.shape, update.dtype)
 
 
-def within_kernel(heads, groups, q, k, v, cum_ref, resets, attn_ref, within, rise_ref, *updates):
-    rise_ref[...] = (1 - resets[...]).astype(F32) * jnp.exp(cum_ref[...])
+def within_kernel(heads, groups, q, k, v, logits, resets, cum_ref, attn_ref, within, rise_ref, *updates):
+    cum = cumulate(logits[...])
+    cum_ref[...] = cum
+    rise_ref[...] = (1 - resets[...]).astype(F32) * jnp.exp(cum)
     size = q.shape[1] // heads
     if groups:
-        add_updates(turn(k, size, groups), v, cum_ref[...], groups, updates)
-    cum_columns = cum_ref[...].T
+        add_updates(turn(k, size, groups), v, cum, groups, updates)
+    cum_columns = cum.T
     step = min(heads, STAGE)
     for first in range(0, heads, step):
         count = min(step, heads - first)
         parts = head_lanes(size, first, count)
         scores = [dot_nt(q[:, p], k[:, p]) for p in parts]
         attns = [
-            (decay_matrix(cum_columns[:, h : h + 1], cum_ref[h : h + 1, :]) * s).astype(BF16)
+            (decay_matrix(cum_columns[:, h : h + 1], cum[h : h + 1, :]) * s).astype(BF16)
             for h, s in enumerate(scores, first)
         ]
         for h, a in enumerate(attns, first):
@@ -272,8 +278,9 @@
         copy.wait()
 
 
-def logit_kernel(groups, early, slots, q, k, v, cum_ref, logits_ref, terms, through, *refs):
+def logit_kernel(groups, early, slots, q, k, v, cum_ref, logits_ref, terms, *refs):
     late = len(groups) - early
+    through, refs = (refs[0], refs[1:]) if slots > 2 else (None, refs)
     grads, (d_ref, *outs) = refs[:late], refs[late:]
     size = grads[0].shape[1]
     width = q.shape[1]
@@ -283,7 +290,7 @@
     parts = head_lanes(size, first, cum.shape[0] - first)
     moved = [dot_nt(v[:, p], grads[g][i]) for p, (g, i) in zip(parts, members(groups[early:]))]
     added = state_terms([k[:, p] for p in parts], moved, fading_rows(cum, slots)[first:])
-    d_cum = terms[...] + through[...]
+    d_cum = terms[...] if through is None else terms[...] + through[...]
     d_cum = jnp.concatenate([d_cum[:first], d_cum[first:] + added], axis=0) if first else d_cum + added
     d_decay = exact_dot(d_cum, triangle(tokens, False))
     d_logits = (-jax.nn.sigmoid(logits_ref[...]) * d_decay).astype(BF16)
@@ -297,22 +304,33 @@
     joined = jnp.concatenate(whole, axis=1)
     cores, others = pieces.shape[:2]
     piece = 3 * width // (cores * others)
+    packed = pack(joined, piece, cores * others)
     for j in range(others):
         for c in range(cores):
             row, slot = j // slots * cores + c, j % slots
-            pieces[c, j] = pack(joined, (row * slots + slot) * piece, piece).astype(BF16)
+            pieces[c, j] = packed[row * slots + slot]
     core = lax.axis_index("core")
     keep[...] = pieces[core]
     send[...] = pieces[1 - core]
 
 
-def pack(joined, first, piece):
-    tiles = [joined[:, first + i : first + i + 128] for i in range(0, piece - 127, 128)]
-    if piece % 128:
-        rest = joined[:, first + piece // 128 * 128 : first + piece]
-        half = rest.shape[0] // 2
-        tiles.append(jnp.concatenate([rest[:half], rest[half:]], axis=1))
-    return jnp.concatenate(tiles, axis=0)
+def pack(joined, piece, count):
+    heads, width = joined.shape
+    half = heads // 2
+    low = lax.broadcasted_iota(jnp.int32, (half, 128), 1) < 64
+    behind = pltpu.roll(joined, width - 64, axis=1)
+    ahead = pltpu.roll(joined, 64, axis=1)
+    packed = []
+    for i in range(count):
+        at = i * piece // 128 * 128
+        source, other = (joined, ahead) if i * piece == at else (behind, joined)
+        tiles = [source[:, at + n : at + n + 128] for n in range(0, piece - 127, 128)]
+        if piece % 128:
+            at += piece // 128 * 128
+            lower, upper = source[:half, at : at + 128], other[half:, at : at + 128]
+            tiles.append(jnp.where(low, lower, upper))
+        packed.append(jnp.concatenate(tiles, axis=0).astype(BF16))
+    return packed
 
 
 def sum_kernel(arrived, out):
@@ -367,9 +385,9 @@
 
 
 def head_groups(heads):
-    sizes=[3, 3, 2, 3, 3, 2]
-    parts=len(sizes)
-    return [(sum(sizes[:i]), sizes[i]) for i in range(parts)]
+    half = heads // 2
+    sizes = [half // 3 + (1 if i < half % 3 else 0) for i in range(3)] * 2
+    return [(sum(sizes[:i]), size) for i, size in enumerate(sizes)]
 
 
 def body(
@@ -389,12 +407,11 @@
         return tuple(shape((count, size, size), BF16) for _, count in some)
 
     ahead = 3 if seq_size == 2 and len(groups) > 2 else len(groups)
-    logits, cum, *updates = pl.pallas_call(
+    logits, *updates = pl.pallas_call(
         functools.partial(gate_kernel, groups[:ahead], seq_size),
-        out_shape=(shape((heads, tokens), F32),) * 2
-        + state_shapes(groups[:ahead]),
+        out_shape=(shape((heads, tokens), F32),) + state_shapes(groups[:ahead]),
         in_specs=[hbm()] * 5,
-        out_specs=(spec(),) * (2 + ahead),
+        out_specs=(spec(),) * (1 + ahead),
         scratch_shapes=[
             pltpu.VMEM((tokens, width), BF16),
             pltpu.VMEM((tokens, width), BF16),
@@ -407,20 +424,21 @@
         cost_estimate=cost(),
         name="gate",
     )(q, k, v, decay_bias[0], gate)
-    attn, within, rise, *made = pl.pallas_call(
+    cum, attn, within, rise, *made = pl.pallas_call(
         functools.partial(within_kernel, heads, groups[ahead:]),
         out_shape=(
+            shape((heads, tokens), F32),
             shape((heads, tokens, tokens), BF16),
             shape((tokens, width), F32),
             shape((heads, tokens), F32),
         )
         + state_shapes(groups[ahead:]),
         in_specs=[spec()] * 5,
-        out_specs=(spec(),) * (3 + len(groups) - ahead),
+        out_specs=(spec(),) * (4 + len(groups) - ahead),
         compiler_params=params(),
         cost_estimate=cost(),
         name="within",
-    )(q, k, v, cum, resets)
+    )(q, k, v, logits, resets)
     updates += made
 
     def chain(own, first, count, pairs):
@@ -474,15 +492,14 @@
         cost_estimate=cost(),
         name="back",
     )(q, k, v, attn, cum, rise, *outs, *d_mixes, *entering, *rows, *grads[:early])
+    through = []
     if seq_size > 2:
-        through = [
+        products = [
             kept * jnp.sum(g.astype(F32) * s.astype(F32), axis=(1, 2))[:, None]
             for g, s in zip(grads, entering)
         ]
-        through = jnp.concatenate(through, axis=0) * jnp.exp(cum[:, -1:])
-        through = through * (jnp.arange(tokens) == tokens - 1).astype(F32)
-    else:
-        through = jnp.zeros((heads, tokens), F32)
+        ends = jnp.concatenate(products, axis=0) * jnp.exp(cum[:, -1:])
+        through = [ends * (jnp.arange(tokens) == tokens - 1).astype(F32)]
 
     piece = 3 * width // (pairs * CORES * seq_size)
     exchanged = cores == CORES and piece >= 128 and piece % 64 == 0 and heads % 16 == 0
@@ -497,13 +514,13 @@
     d_logits, *parts = pl.pallas_call(
         functools.partial(logit_kernel, groups, early, seq_size),
         out_shape=(shape((heads, tokens), BF16),) + part_shapes,
-        in_specs=[spec()] * (7 + len(groups) - early),
+        in_specs=[spec()] * (6 + len(through) + len(groups) - early),
         out_specs=(spec(),) * (1 + len(part_shapes)),
         scratch_shapes=scratch,
         compiler_params=params(),
         cost_estimate=cost(),
         name="logits",
-    )(q, k, v, cum, logits, terms, through, *grads[early:])
+    )(q, k, v, cum, logits, terms, *through, *grads[early:])
 
     input_grads = pl.pallas_call(
         functools.partial(finish_kernel, groups, early, seq_size),

time: 44.4 us -> 43.6 us (0.982)
  transfers between devices with their start and end apart: 10 -> 10, of which waited for: 3 -> 3; matrix products, arithmetic and copies ran while one was open for 0% -> 0% of each run, Pallas kernels for 20% -> 21%
where the time goes in v6:
time: 43.6 us; the launch traced here: 43.4 us
  Pallas kernels  14.1 us (32%)
  blocking collectives  13.6 us (31%)
  starting transfers between devices  13.2 us (30%)
  between operations  1.47 us (3%)
  waiting for transfers between devices  1 us (2%)
    all_to_all x1, blocking collectives, body(): arrived = lax.all_to_all(total, ('pair', 'seq'), 0, 0, tiled=True)  13.6 us
    ppermute x6, starting transfers between devices, chain(): return lax.ppermute(own, 'seq', [(0, 1), (1, 0)])  8.79 us
    ppermute x3, starting transfers between devices, body(): arrived = lax.ppermute(pushed, 'seq', [(0, 1), (1, 0)])  4.33 us
    pallas_call x1, Pallas kernels, body(): pl.pallas_call(functools.partial(gate_kernel, groups[:ahead], seq_size),...  3.39 us
    pallas_call x6, Pallas kernels, body(): pl.pallas_call(functools.partial(mix_kernel, first, count), out_shape=(sh...  3.36 us
    pallas_call x1, Pallas kernels, body(): pl.pallas_call(functools.partial(back_kernel, groups, early, seq_size), o...  2.73 us
    pallas_call x1, Pallas kernels, body(): pl.pallas_call(functools.partial(finish_kernel, groups, early, seq_size),...  1.68 us
    pallas_call x1, Pallas kernels, body(): pl.pallas_call(functools.partial(within_kernel, heads, groups[ahead:]), o...  1.17 us
  transfers between devices with their start and end apart: 10, of which 3 were waited for; matrix products, arithmetic and copies ran while one was open for 0% of the time, Pallas kernels for 21%

profile of v6, /device:TPU:0, one launch (start us, length us, event | category | flops | bytes accessed | tf_op | source)
XLA Modules:
  0.0 43.4 jit_solution(17170369206824095700)
XLA Ops:
  0.6 0.0 copy-start
  0.6 0.0 copy-start.2
  0.7 0.0 copy-start.3
  0.7 3.4 %gate.1 = (f32[16,128]{1,0:T(8,128)}, bf16[3,128,128]{2,1,0:T(8,128)(2,1)}, bf16[3,128,128]{2,1,0:T(8,128)(2,1)}, bf16[2,128,128]{2,1,0:T(8,128)(2,1)}) custom-call(bf16[128,2048]{1,0:T(8,128)(2,1)} %bitcast.11, bf16[128,2048]{1,0:T(8,128)(2,1)} %bitcast.27, bf16[128,2048]{1,0:T(8,128)(2,1)} %bitcast.32, f32[16,128]{1,0:T(8,128)} %bitcast.40, ...), custom_call_target="tpu_custom_call" | custom-call | flops 1000 | bytes 1000 | tf_op jit(solution)/shard_map/gate/pallas_call | solution.py:410
  4.1 0.0 copy-start.5
  4.1 2.6 %collective-permute-start = (bf16[3,128,128]{2,1,0:T(8,128)(2,1)}, bf16[3,128,128]{2,1,0:T(8,128)(2,1)S(1)}, u32[]{:S(2)}, u32[]{:S(2)}) collective-permute-start(bf16[3,128,128]{2,1,0:T(8,128)(2,1)} %get-tuple-element.60), channel_id=1, source_target_pairs={{0,1},{1,0},{2,3},{3,2},{4,5},{5,4},{6,7},{7,6},{8,9},{9,8},{10,11... | collective-permute-start | bytes 294920 | tf_op jit(solution)/shard_map/ppermute | solution.py:446
  6.6 0.1 collective-permute-start.1
  6.7 1.9 %collective-permute-start.2 = (bf16[2,128,128]{2,1,0:T(8,128)(2,1)}, bf16[2,128,128]{2,1,0:T(8,128)(2,1)S(1)}, u32[]{:S(2)}, u32[]{:S(2)}) collective-permute-start(bf16[2,128,128]{2,1,0:T(8,128)(2,1)} %get-tuple-element.66), channel_id=1, source_target_pairs={{0,1},{1,0},{2,3},{3,2},{4,5},{5,4},{6,7},{7,6},{8,9},{9,8},{10,11... | collective-permute-start | bytes 196616 | tf_op jit(solution)/shard_map/ppermute | solution.py:446
  9.3 0.0 copy-done
  9.3 0.0 copy-done.2
  9.3 0.0 copy-done.3
  9.3 0.0 copy-done.5
  9.4 0.0 copy-start.1
  9.4 1.2 %within.1 = (f32[16,128]{1,0:T(8,128)S(1)}, bf16[16,128,128]{2,1,0:T(8,128)(2,1)S(1)}, f32[128,2048]{1,0:T(8,128)S(1)}, f32[16,128]{1,0:T(8,128)S(1)}, bf16[3,12...) custom-call(bf16[128,2048]{1,0:T(8,128)(2,1)S(1)} %bitcast.12, ...), custom_call_target="tpu_custom_call" | custom-call | flops 1000 | bytes 1000 | tf_op jit(solution)/shard_map/within/pallas_call | solution.py:427
  10.5 0.0 collective-permute-done.state.refs_18_
  10.6 0.0 copy-done.1
  10.6 0.6 %mix.6 = (bf16[128,384]{1,0:T(8,128)(2,1)S(1)}, bf16[128,384]{1,0:T(8,128)(2,1)S(1)}, bf16[3,128,128]{2,1,0:T(8,128)(2,1)S(1)}, f32[3,128]{1,0:T(4,128)S(1)}) custom-call(bf16[128,2048]{1,0:T(8,128)(2,1)S(1)} %bitcast.13, f32[128,2048]{1,0:T(8,128)S(1)} %get-tuple-element.59.within, bf16[128,2048]{1,0:T(8,128)(2,1)S(1)} %bitcast.21, ...), custom_call_target="tpu_custom_call" | custom-call | flops 1000 | bytes 1000 | tf_op jit(solution)/shard_map/mix/pallas_call | solution.py:458
  11.2 2.0 %collective-permute-start.3 = (bf16[3,128,128]{2,1,0:T(8,128)(2,1)S(1)}, bf16[3,128,128]{2,1,0:T(8,128)(2,1)S(1)}, u32[]{:S(2)}, u32[]{:S(2)}) collective-permute-start(bf16[3,128,128]{2,1,0:T(8,128)(2,1)S(1)} %get-tuple-element.69), channel_id=1, source_target_pairs={{0,1},{1,0},{2,3},{3,2},{4,5},{5,4},{6,7},{7,6},{8,9},{9,8},{10,11... | collective-permute-start | bytes 294920 | tf_op jit(solution)/shard_map/ppermute | solution.py:476
  13.2 0.0 collective-permute-done.1.state.refs_19_
  13.2 0.6 %mix.7 = (bf16[128,384]{1,0:T(8,128)(2,1)S(1)}, bf16[128,384]{1,0:T(8,128)(2,1)S(1)}, bf16[3,128,128]{2,1,0:T(8,128)(2,1)S(1)}, f32[3,128]{1,0:T(4,128)S(1)}) custom-call(bf16[128,2048]{1,0:T(8,128)(2,1)S(1)} %bitcast.14, f32[128,2048]{1,0:T(8,128)S(1)} %get-tuple-element.59.within, bf16[128,2048]{1,0:T(8,128)(2,1)S(1)} %bitcast.22, ...), custom_call_target="tpu_custom_call" | custom-call | flops 1000 | bytes 1000 | tf_op jit(solution)/shard_map/mix/pallas_call | solution.py:458
  13.8 1.5 %collective-permute-start.4 = (bf16[3,128,128]{2,1,0:T(8,128)(2,1)S(1)}, bf16[3,128,128]{2,1,0:T(8,128)(2,1)S(1)}, u32[]{:S(2)}, u32[]{:S(2)}) collective-permute-start(bf16[3,128,128]{2,1,0:T(8,128)(2,1)S(1)} %get-tuple-element.71), channel_id=1, source_target_pairs={{0,1},{1,0},{2,3},{3,2},{4,5},{5,4},{6,7},{7,6},{8,9},{9,8},{10,11... | collective-permute-start | bytes 294920 | tf_op jit(solution)/shard_map/ppermute | solution.py:476
  15.3 0.0 collective-permute-done.2.state.refs_20_
  15.3 0.5 %mix.8 = (bf16[128,256]{1,0:T(8,128)(2,1)S(1)}, bf16[128,256]{1,0:T(8,128)(2,1)S(1)}, bf16[2,128,128]{2,1,0:T(8,128)(2,1)S(1)}, f32[2,128]{1,0:T(2,128)S(1)}) custom-call(bf16[128,2048]{1,0:T(8,128)(2,1)S(1)} %bitcast.15, f32[128,2048]{1,0:T(8,128)S(1)} %get-tuple-element.59.within, bf16[128,2048]{1,0:T(8,128)(2,1)S(1)} %bitcast.23, ...), custom_call_target="tpu_custom_call" | custom-call | flops 1000 | bytes 1000 | tf_op jit(solution)/shard_map/mix/pallas_call | solution.py:458
  15.8 0.8 %collective-permute-start.5 = (bf16[2,128,128]{2,1,0:T(8,128)(2,1)S(1)}, bf16[2,128,128]{2,1,0:T(8,128)(2,1)S(1)}, u32[]{:S(2)}, u32[]{:S(2)}) collective-permute-start(bf16[2,128,128]{2,1,0:T(8,128)(2,1)S(1)} %get-tuple-element.73), channel_id=1, source_target_pairs={{0,1},{1,0},{2,3},{3,2},{4,5},{5,4},{6,7},{7,6},{8,9},{9,8},{10,11... | collective-permute-start | bytes 196616 | tf_op jit(solution)/shard_map/ppermute | solution.py:476
  16.6 0.2 collective-permute-done.3.state.refs_21_.refs_30_
  16.8 0.6 %mix.9 = (bf16[128,384]{1,0:T(8,128)(2,1)S(1)}, bf16[128,384]{1,0:T(8,128)(2,1)S(1)}, bf16[3,128,128]{2,1,0:T(8,128)(2,1)S(1)}, f32[3,128]{1,0:T(4,128)S(1)}) custom-call(bf16[128,2048]{1,0:T(8,128)(2,1)S(1)} %bitcast.16, f32[128,2048]{1,0:T(8,128)S(1)} %get-tuple-element.59.within, bf16[128,2048]{1,0:T(8,128)(2,1)S(1)} %bitcast.24, ...), custom_call_target="tpu_custom_call" | custom-call | flops 1000 | bytes 1000 | tf_op jit(solution)/shard_map/mix/pallas_call | solution.py:458
  17.4 2.0 %collective-permute-start.6 = (bf16[3,128,128]{2,1,0:T(8,128)(2,1)S(1)}, bf16[3,128,128]{2,1,0:T(8,128)(2,1)S(1)}, u32[]{:S(2)}, u32[]{:S(2)}) collective-permute-start(bf16[3,128,128]{2,1,0:T(8,128)(2,1)S(1)} %get-tuple-element.89), channel_id=1, source_target_pairs={{0,1},{1,0},{2,3},{3,2},{4,5},{5,4},{6,7},{7,6},{8,9},{9,8},{10,11... | collective-permute-start | bytes 294920 | tf_op jit(solution)/shard_map/ppermute | solution.py:446
  19.4 0.1 collective-permute-done.4.state.refs_22_.refs_31_
  19.5 0.6 %mix.10 = (bf16[128,384]{1,0:T(8,128)(2,1)S(1)}, bf16[128,384]{1,0:T(8,128)(2,1)S(1)}, bf16[3,128,128]{2,1,0:T(8,128)(2,1)S(1)}, f32[3,128]{1,0:T(4,128)S(1)}) custom-call(bf16[128,2048]{1,0:T(8,128)(2,1)S(1)} %bitcast.17, f32[128,2048]{1,0:T(8,128)S(1)} %get-tuple-element.59.within, bf16[128,2048]{1,0:T(8,128)(2,1)S(1)} %bitcast.25, ...), custom_call_target="tpu_custom_call" | custom-call | flops 1000 | bytes 1000 | tf_op jit(solution)/shard_map/mix/pallas_call | solution.py:458
  20.1 1.3 %collective-permute-start.7 = (bf16[3,128,128]{2,1,0:T(8,128)(2,1)S(1)}, bf16[3,128,128]{2,1,0:T(8,128)(2,1)S(1)}, u32[]{:S(2)}, u32[]{:S(2)}) collective-permute-start(bf16[3,128,128]{2,1,0:T(8,128)(2,1)S(1)} %get-tuple-element.90), channel_id=1, source_target_pairs={{0,1},{1,0},{2,3},{3,2},{4,5},{5,4},{6,7},{7,6},{8,9},{9,8},{10,11... | collective-permute-start | bytes 294920 | tf_op jit(solution)/shard_map/ppermute | solution.py:446
  21.4 0.0 collective-permute-done.5.state.refs_23_.refs_32_
  21.4 0.5 %mix.11 = (bf16[128,256]{1,0:T(8,128)(2,1)S(1)}, bf16[128,256]{1,0:T(8,128)(2,1)S(1)}, bf16[2,128,128]{2,1,0:T(8,128)(2,1)S(1)}, f32[2,128]{1,0:T(2,128)S(1)}) custom-call(bf16[128,2048]{1,0:T(8,128)(2,1)S(1)} %bitcast.18, f32[128,2048]{1,0:T(8,128)S(1)} %get-tuple-element.59.within, bf16[128,2048]{1,0:T(8,128)(2,1)S(1)} %bitcast.26, ...), custom_call_target="tpu_custom_call" | custom-call | flops 1000 | bytes 1000 | tf_op jit(solution)/shard_map/mix/pallas_call | solution.py:458
  21.9 0.9 %collective-permute-start.8 = (bf16[2,128,128]{2,1,0:T(8,128)(2,1)S(1)}, bf16[2,128,128]{2,1,0:T(8,128)(2,1)S(1)}, u32[]{:S(2)}, u32[]{:S(2)}) collective-permute-start(bf16[2,128,128]{2,1,0:T(8,128)(2,1)S(1)} %get-tuple-element.91), channel_id=1, source_target_pairs={{0,1},{1,0},{2,3},{3,2},{4,5},{5,4},{6,7},{7,6},{8,9},{9,8},{10,11... | collective-permute-start | bytes 196616 | tf_op jit(solution)/shard_map/ppermute | solution.py:446
  22.8 2.7 %back.1 = (bf16[128,2048]{1,0:T(8,128)(2,1)}, f32[128,2048]{1,0:T(8,128)S(1)}, f32[128,2048]{1,0:T(8,128)S(1)}, f32[128,2048]{1,0:T(8,128)S(1)}, f32[16,128]{1,0:T(8,128)S(1)}) custom-call(bf16[128,2048]{1,0:T(8,128)(2,1)S(1)} %bitcast.19, bf16[128,2048]{1,0:T(8,128)(2,1)S(1)} %bitcast.29, bf16[128,2048]{1,0:T(8,128)(2,1)S(1)} %bitcast.34, ...), custom_call_target="tpu_custom_call" | custom-call | flops 1000 | bytes 1000 | tf_op jit(solution)/shard_map/back/pallas_call | solution.py:483
  25.5 0.7 %collective-permute-done.8.refs_2_ = bf16[2,128,128]{2,1,0:T(8,128)(2,1)S(1)} collective-permute-done((bf16[2,128,128]{2,1,0:T(8,128)(2,1)S(1)}, bf16[2,128,128]{2,1,0:T(8,128)(2,1)S(1)}, u32[]{:S(2)}, u32[]{:S(2)}) %collective-permute-start.8) | collective-permute-done | bytes 65568 | tf_op jit(solution)/shard_map/ppermute | solution.py:446
  26.2 0.0 collective-permute-done.6.refs_0_
  26.2 0.0 collective-permute-done.7.refs_1_
  26.2 0.0 copy-start.4
  26.2 1.1 %logits.1 = (bf16[16,128]{1,0:T(8,128)(2,1)S(1)}, bf16[16,24,128]{2,1,0:T(8,128)(2,1)S(1)}, bf16[16,24,128]{2,1,0:T(8,128)(2,1)S(1)}) custom-call(bf16[128,2048]{1,0:T(8,128)(2,1)S(1)} %bitcast.20, bf16[128,2048]{1,0:T(8,128)(2,1)S(1)} %bitcast.30, bf16[128,2048]{1,0:T(8,128)(2,1)S(1)} %bitcast.35, f32[16,128]{1,0:T(8,128)S(1)} %get-tuple-element.57.refs_4_.cum_ref, ...), custom_call_target="tpu_custom_call" | custom-call | flops 1000 | bytes 1000 | tf_op jit(solution)/shard_map/logits/pallas_call | solution.py:514
  27.3 0.1 collective-permute-start.9
  27.4 0.0 copy-done.4
  27.4 1.7 %finish.1 = (bf16[128,2048]{1,0:T(8,128)(2,1)}, bf16[128,2048]{1,0:T(8,128)(2,1)}, bf16[128,2048]{1,0:T(8,128)(2,1)}) custom-call(f32[128,2048]{1,0:T(8,128)S(1)} %get-tuple-element.94.gq, f32[128,2048]{1,0:T(8,128)S(1)} %get-tuple-element.95.gk, f32[128,2048]{1,0:T(8,128)S(1)} %get-tuple-element.96.gv, bf16[128,2048]{1,0:T(8,128)(2,1)S(1)} %bitcast.31, ...), custom_call_target="tpu_custom_call" | custom-call | flops 1000 | bytes 1000 | tf_op jit(solution)/shard_map/finish/pallas_call | solution.py:525
  29.1 0.0 collective-permute-done.9
  29.1 13.6 %all_to_all.5.arrived = bf16[16,24,128]{2,1,0:T(8,128)(2,1)S(1)} all-to-all(bf16[16,24,128]{2,1,0:T(8,128)(2,1)S(1)} %add_convert_fusion), channel_id=1, replica_groups=mesh['pair'=8,'core'=2,'seq'=2] {'pair','seq'}, dimensions={0} | all-to-all | bytes 196608 | tf_op jit(solution)/shard_map/all_to_all | solution.py:544
  42.7 0.7 %sum.1 = f32[16,192]{1,0:T(8,128)} custom-call(bf16[16,24,128]{2,1,0:T(8,128)(2,1)S(1)} %all_to_all.5.arrived), custom_call_target="tpu_custom_call" | custom-call | tf_op jit(solution)/shard_map/sum/pallas_call | solution.py:545
  (1 shorter events, 0.0 us)
Async XLA Ops:
  0.6 8.7 %copy-start = (bf16[1,128,2048]{2,1,0:T(8,128)(2,1)S(1)}, bf16[1,128,2048]{2,1,0:T(8,128)(2,1)}, u32[]{:S(2)}) copy-start(bf16[1,128,2048]{2,1,0:T(8,128)(2,1)} %param.7) | copy-start | bytes 1572868
  0.6 8.7 %copy-start.2 = (bf16[1,128,2048]{2,1,0:T(8,128)(2,1)S(1)}, bf16[1,128,2048]{2,1,0:T(8,128)(2,1)}, u32[]{:S(2)}) copy-start(bf16[1,128,2048]{2,1,0:T(8,128)(2,1)} %param.8) | copy-start | bytes 1572868
  0.7 8.7 %copy-start.3 = (bf16[1,128,2048]{2,1,0:T(8,128)(2,1)S(1)}, bf16[1,128,2048]{2,1,0:T(8,128)(2,1)}, u32[]{:S(2)}) copy-start(bf16[1,128,2048]{2,1,0:T(8,128)(2,1)} %param.9) | copy-start | bytes 1572868
  4.1 5.3 %copy-start.5 = (f32[16,128]{1,0:T(8,128)S(1)}, f32[16,128]{1,0:T(8,128)}, u32[]{:S(2)}) copy-start(f32[16,128]{1,0:T(8,128)} %get-tuple-element.55.logits.logits_ref) | copy-start | bytes 24580
  4.1 6.5 %collective-permute-start = (bf16[3,128,128]{2,1,0:T(8,128)(2,1)}, bf16[3,128,128]{2,1,0:T(8,128)(2,1)S(1)}, u32[]{:S(2)}, u32[]{:S(2)}) collective-permute-start(bf16[3,128,128]{2,1,0:T(8,128)(2,1)} %get-tuple-element.60), channel_id=1, source_target_pairs={{0,1},{1,0},{2,3},{3,2},{4,5},{5,4},{6,7},{7,6},{8,9},{9,8},{10,11... | collective-permute-start | bytes 294920 | tf_op jit(solution)/shard_map/ppermute | solution.py:446
  6.6 6.6 %collective-permute-start.1 = (bf16[3,128,128]{2,1,0:T(8,128)(2,1)}, bf16[3,128,128]{2,1,0:T(8,128)(2,1)S(1)}, u32[]{:S(2)}, u32[]{:S(2)}) collective-permute-start(bf16[3,128,128]{2,1,0:T(8,128)(2,1)} %get-tuple-element.63), channel_id=1, source_target_pairs={{0,1},{1,0},{2,3},{3,2},{4,5},{5,4},{6,7},{7,6},{8,9},{9,8},{10,11... | collective-permute-start | bytes 294920 | tf_op jit(solution)/shard_map/ppermute | solution.py:446
  6.7 8.6 %collective-permute-start.2 = (bf16[2,128,128]{2,1,0:T(8,128)(2,1)}, bf16[2,128,128]{2,1,0:T(8,128)(2,1)S(1)}, u32[]{:S(2)}, u32[]{:S(2)}) collective-permute-start(bf16[2,128,128]{2,1,0:T(8,128)(2,1)} %get-tuple-element.66), channel_id=1, source_target_pairs={{0,1},{1,0},{2,3},{3,2},{4,5},{5,4},{6,7},{7,6},{8,9},{9,8},{10,11... | collective-permute-start | bytes 196616 | tf_op jit(solution)/shard_map/ppermute | solution.py:446
  9.4 1.2 %copy-start.1 = (bf16[1,128,2048]{2,1,0:T(8,128)(2,1)S(1)}, bf16[1,128,2048]{2,1,0:T(8,128)(2,1)}, u32[]{:S(2)}) copy-start(bf16[1,128,2048]{2,1,0:T(8,128)(2,1)} %param.13) | copy-start | bytes 1572868
  11.2 5.6 %collective-permute-start.3 = (bf16[3,128,128]{2,1,0:T(8,128)(2,1)S(1)}, bf16[3,128,128]{2,1,0:T(8,128)(2,1)S(1)}, u32[]{:S(2)}, u32[]{:S(2)}) collective-permute-start(bf16[3,128,128]{2,1,0:T(8,128)(2,1)S(1)} %get-tuple-element.69), channel_id=1, source_target_pairs={{0,1},{1,0},{2,3},{3,2},{4,5},{5,4},{6,7},{7,6},{8,9},{9,8},{10,11... | collective-permute-start | bytes 294920 | tf_op jit(solution)/shard_map/ppermute | solution.py:476
  13.8 5.7 %collective-permute-start.4 = (bf16[3,128,128]{2,1,0:T(8,128)(2,1)S(1)}, bf16[3,128,128]{2,1,0:T(8,128)(2,1)S(1)}, u32[]{:S(2)}, u32[]{:S(2)}) collective-permute-start(bf16[3,128,128]{2,1,0:T(8,128)(2,1)S(1)} %get-tuple-element.71), channel_id=1, source_target_pairs={{0,1},{1,0},{2,3},{3,2},{4,5},{5,4},{6,7},{7,6},{8,9},{9,8},{10,11... | collective-permute-start | bytes 294920 | tf_op jit(solution)/shard_map/ppermute | solution.py:476
  15.8 5.6 %collective-permute-start.5 = (bf16[2,128,128]{2,1,0:T(8,128)(2,1)S(1)}, bf16[2,128,128]{2,1,0:T(8,128)(2,1)S(1)}, u32[]{:S(2)}, u32[]{:S(2)}) collective-permute-start(bf16[2,128,128]{2,1,0:T(8,128)(2,1)S(1)} %get-tuple-element.73), channel_id=1, source_target_pairs={{0,1},{1,0},{2,3},{3,2},{4,5},{5,4},{6,7},{7,6},{8,9},{9,8},{10,11... | collective-permute-start | bytes 196616 | tf_op jit(solution)/shard_map/ppermute | solution.py:476
  17.4 8.8 %collective-permute-start.6 = (bf16[3,128,128]{2,1,0:T(8,128)(2,1)S(1)}, bf16[3,128,128]{2,1,0:T(8,128)(2,1)S(1)}, u32[]{:S(2)}, u32[]{:S(2)}) collective-permute-start(bf16[3,128,128]{2,1,0:T(8,128)(2,1)S(1)} %get-tuple-element.89), channel_id=1, source_target_pairs={{0,1},{1,0},{2,3},{3,2},{4,5},{5,4},{6,7},{7,6},{8,9},{9,8},{10,11... | collective-permute-start | bytes 294920 | tf_op jit(solution)/shard_map/ppermute | solution.py:446
  20.1 6.1 %collective-permute-start.7 = (bf16[3,128,128]{2,1,0:T(8,128)(2,1)S(1)}, bf16[3,128,128]{2,1,0:T(8,128)(2,1)S(1)}, u32[]{:S(2)}, u32[]{:S(2)}) collective-permute-start(bf16[3,128,128]{2,1,0:T(8,128)(2,1)S(1)} %get-tuple-element.90), channel_id=1, source_target_pairs={{0,1},{1,0},{2,3},{3,2},{4,5},{5,4},{6,7},{7,6},{8,9},{9,8},{10,11... | collective-permute-start | bytes 294920 | tf_op jit(solution)/shard_map/ppermute | solution.py:446
  21.9 4.3 %collective-permute-start.8 = (bf16[2,128,128]{2,1,0:T(8,128)(2,1)S(1)}, bf16[2,128,128]{2,1,0:T(8,128)(2,1)S(1)}, u32[]{:S(2)}, u32[]{:S(2)}) collective-permute-start(bf16[2,128,128]{2,1,0:T(8,128)(2,1)S(1)} %get-tuple-element.91), channel_id=1, source_target_pairs={{0,1},{1,0},{2,3},{3,2},{4,5},{5,4},{6,7},{7,6},{8,9},{9,8},{10,11... | collective-permute-start | bytes 196616 | tf_op jit(solution)/shard_map/ppermute | solution.py:446
  26.2 1.2 %copy-start.4 = (bf16[6144,16]{0,1:T(8,128)(2,1)S(1)}, bf16[6144,16]{0,1:T(8,128)(2,1)}, u32[]{:S(2)}) copy-start(bf16[6144,16]{0,1:T(8,128)(2,1)} %param.11) | copy-start | bytes 589828
  27.3 1.8 %collective-permute-start.9 = (bf16[16,24,128]{2,1,0:T(8,128)(2,1)S(1)}, bf16[16,24,128]{2,1,0:T(8,128)(2,1)S(1)}, u32[]{:S(2)}, u32[]{:S(2)}) collective-permute-start(bf16[16,24,128]{2,1,0:T(8,128)(2,1)S(1)} %get-tuple-element.93), channel_id=1, source_target_pairs={{0,2},{2,0},{1,3},{3,1},{4,6},{6,4},{5,7},{7,5},{8,10},{10,8},{9,1... | collective-permute-start | bytes 294920 | tf_op jit(solution)/shard_map/ppermute | solution.py:541

commit v7 on v6

--- a/solution.py
+++ b/solution.py
@@ -114,6 +114,7 @@
     for copy in copies[:3]:
         copy.wait()
     logits = bias[...] + dot_nt(gate[:, width : 2 * width], k[...])
+    turned = turn(k, updates[0].shape[1], groups)
     copies[3].wait()
     logits = logits + dot_nt(gate[:, :width], q[...])
     copies[4].wait()
@@ -121,7 +122,6 @@
     logits_ref[...] = logits
 
     def run():
-        turned = turn(k, updates[0].shape[1], groups)
         add_updates(turned, v, cumulate(logits), groups, updates)
 
     if slots > 2:
@@ -307,7 +307,8 @@
     packed = pack(joined, piece, cores * others)
     for j in range(others):
         for c in range(cores):
-            row, slot = j // slots * cores + c, j % slots
+            slot, pair = j // (others // slots), j % (others // slots)
+            row = pair * cores + c
             pieces[c, j] = packed[row * slots + slot]
     core = lax.axis_index("core")
     keep[...] = pieces[core]
@@ -541,7 +542,7 @@
         arrived = lax.ppermute(send, "core", [(0, 1), (1, 0)])
         total = (keep.astype(F32) + arrived.astype(F32)).astype(BF16)
         total, *input_grads = lax.optimization_barrier((total, *input_grads))
-        arrived = lax.all_to_all(total, ("pair", "seq"), 0, 0, tiled=True)
+        arrived = lax.all_to_all(total, ("seq", "pair"), 0, 0, tiled=True)
         grad_gate = pl.pallas_call(
             sum_kernel,
             out_shape=shape((heads, piece), F32),

time: 43.6 us -> 43.6 us (level)
  no operation moved by 1% of the time
where the time goes in v7:
time: 43.6 us; the launch traced here: 43.4 us
  Pallas kernels  14.1 us (32%)
  blocking collectives  13.6 us (31%)
  starting transfers between devices  13.2 us (30%)
  between operations  1.47 us (3%)
  waiting for transfers between devices  1 us (2%)
    all_to_all x1, blocking collectives, body(): arrived = lax.all_to_all(total, ('seq', 'pair'), 0, 0, tiled=True)  13.6 us
    ppermute x6, starting transfers between devices, chain(): return lax.ppermute(own, 'seq', [(0, 1), (1, 0)])  8.82 us
    ppermute x3, starting transfers between devices, body(): arrived = lax.ppermute(pushed, 'seq', [(0, 1), (1, 0)])  4.33 us
    pallas_call x6, Pallas kernels, body(): pl.pallas_call(functools.partial(mix_kernel, first, count), out_shape=(sh...  3.36 us
    pallas_call x1, Pallas kernels, body(): pl.pallas_call(functools.partial(gate_kernel, groups[:ahead], seq_size),...  3.36 us
    pallas_call x1, Pallas kernels, body(): pl.pallas_call(functools.partial(back_kernel, groups, early, seq_size), o...  2.73 us
    pallas_call x1, Pallas kernels, body(): pl.pallas_call(functools.partial(finish_kernel, groups, early, seq_size),...  1.68 us
    pallas_call x1, Pallas kernels, body(): pl.pallas_call(functools.partial(within_kernel, heads, groups[ahead:]), o...  1.17 us
  transfers between devices with their start and end apart: 10, of which 3 were waited for; matrix products, arithmetic and copies ran while one was open for 0% of the time, Pallas kernels for 21%

profile of v7, /device:TPU:0, one launch (start us, length us, event | category | flops | bytes accessed | tf_op | source)
XLA Modules:
  0.0 43.4 jit_solution(5663802255602231372)
XLA Ops:
  0.6 0.0 copy-start
  0.6 0.0 copy-start.2
  0.7 0.0 copy-start.3
  0.7 3.4 %gate.1 = (f32[16,128]{1,0:T(8,128)}, bf16[3,128,128]{2,1,0:T(8,128)(2,1)}, bf16[3,128,128]{2,1,0:T(8,128)(2,1)}, bf16[2,128,128]{2,1,0:T(8,128)(2,1)}) custom-call(bf16[128,2048]{1,0:T(8,128)(2,1)} %bitcast.11, bf16[128,2048]{1,0:T(8,128)(2,1)} %bitcast.27, bf16[128,2048]{1,0:T(8,128)(2,1)} %bitcast.32, f32[16,128]{1,0:T(8,128)} %bitcast.40, ...), custom_call_target="tpu_custom_call" | custom-call | flops 1000 | bytes 1000 | tf_op jit(solution)/shard_map/gate/pallas_call | solution.py:411
  4.0 0.0 copy-start.5
  4.0 2.6 %collective-permute-start = (bf16[3,128,128]{2,1,0:T(8,128)(2,1)}, bf16[3,128,128]{2,1,0:T(8,128)(2,1)S(1)}, u32[]{:S(2)}, u32[]{:S(2)}) collective-permute-start(bf16[3,128,128]{2,1,0:T(8,128)(2,1)} %get-tuple-element.60), channel_id=1, source_target_pairs={{0,1},{1,0},{2,3},{3,2},{4,5},{5,4},{6,7},{7,6},{8,9},{9,8},{10,11... | collective-permute-start | bytes 294920 | tf_op jit(solution)/shard_map/ppermute | solution.py:447
  6.6 0.1 collective-permute-start.1
  6.7 1.9 %collective-permute-start.2 = (bf16[2,128,128]{2,1,0:T(8,128)(2,1)}, bf16[2,128,128]{2,1,0:T(8,128)(2,1)S(1)}, u32[]{:S(2)}, u32[]{:S(2)}) collective-permute-start(bf16[2,128,128]{2,1,0:T(8,128)(2,1)} %get-tuple-element.66), channel_id=1, source_target_pairs={{0,1},{1,0},{2,3},{3,2},{4,5},{5,4},{6,7},{7,6},{8,9},{9,8},{10,11... | collective-permute-start | bytes 196616 | tf_op jit(solution)/shard_map/ppermute | solution.py:447
  9.3 0.0 copy-done
  9.3 0.0 copy-done.2
  9.3 0.0 copy-done.3
  9.3 0.0 copy-done.5
  9.4 0.0 copy-start.1
  9.4 1.2 %within.1 = (f32[16,128]{1,0:T(8,128)S(1)}, bf16[16,128,128]{2,1,0:T(8,128)(2,1)S(1)}, f32[128,2048]{1,0:T(8,128)S(1)}, f32[16,128]{1,0:T(8,128)S(1)}, bf16[3,12...) custom-call(bf16[128,2048]{1,0:T(8,128)(2,1)S(1)} %bitcast.12, ...), custom_call_target="tpu_custom_call" | custom-call | flops 1000 | bytes 1000 | tf_op jit(solution)/shard_map/within/pallas_call | solution.py:428
  10.5 0.0 collective-permute-done.state.refs_18_
  10.6 0.0 copy-done.1
  10.6 0.6 %mix.6 = (bf16[128,384]{1,0:T(8,128)(2,1)S(1)}, bf16[128,384]{1,0:T(8,128)(2,1)S(1)}, bf16[3,128,128]{2,1,0:T(8,128)(2,1)S(1)}, f32[3,128]{1,0:T(4,128)S(1)}) custom-call(bf16[128,2048]{1,0:T(8,128)(2,1)S(1)} %bitcast.13, f32[128,2048]{1,0:T(8,128)S(1)} %get-tuple-element.59.within, bf16[128,2048]{1,0:T(8,128)(2,1)S(1)} %bitcast.21, ...), custom_call_target="tpu_custom_call" | custom-call | flops 1000 | bytes 1000 | tf_op jit(solution)/shard_map/mix/pallas_call | solution.py:459
  11.2 2.0 %collective-permute-start.3 = (bf16[3,128,128]{2,1,0:T(8,128)(2,1)S(1)}, bf16[3,128,128]{2,1,0:T(8,128)(2,1)S(1)}, u32[]{:S(2)}, u32[]{:S(2)}) collective-permute-start(bf16[3,128,128]{2,1,0:T(8,128)(2,1)S(1)} %get-tuple-element.69), channel_id=1, source_target_pairs={{0,1},{1,0},{2,3},{3,2},{4,5},{5,4},{6,7},{7,6},{8,9},{9,8},{10,11... | collective-permute-start | bytes 294920 | tf_op jit(solution)/shard_map/ppermute | solution.py:477
  13.2 0.0 collective-permute-done.1.state.refs_19_
  13.2 0.6 %mix.7 = (bf16[128,384]{1,0:T(8,128)(2,1)S(1)}, bf16[128,384]{1,0:T(8,128)(2,1)S(1)}, bf16[3,128,128]{2,1,0:T(8,128)(2,1)S(1)}, f32[3,128]{1,0:T(4,128)S(1)}) custom-call(bf16[128,2048]{1,0:T(8,128)(2,1)S(1)} %bitcast.14, f32[128,2048]{1,0:T(8,128)S(1)} %get-tuple-element.59.within, bf16[128,2048]{1,0:T(8,128)(2,1)S(1)} %bitcast.22, ...), custom_call_target="tpu_custom_call" | custom-call | flops 1000 | bytes 1000 | tf_op jit(solution)/shard_map/mix/pallas_call | solution.py:459
  13.8 1.5 %collective-permute-start.4 = (bf16[3,128,128]{2,1,0:T(8,128)(2,1)S(1)}, bf16[3,128,128]{2,1,0:T(8,128)(2,1)S(1)}, u32[]{:S(2)}, u32[]{:S(2)}) collective-permute-start(bf16[3,128,128]{2,1,0:T(8,128)(2,1)S(1)} %get-tuple-element.71), channel_id=1, source_target_pairs={{0,1},{1,0},{2,3},{3,2},{4,5},{5,4},{6,7},{7,6},{8,9},{9,8},{10,11... | collective-permute-start | bytes 294920 | tf_op jit(solution)/shard_map/ppermute | solution.py:477
  15.3 0.0 collective-permute-done.2.state.refs_20_
  15.3 0.5 %mix.8 = (bf16[128,256]{1,0:T(8,128)(2,1)S(1)}, bf16[128,256]{1,0:T(8,128)(2,1)S(1)}, bf16[2,128,128]{2,1,0:T(8,128)(2,1)S(1)}, f32[2,128]{1,0:T(2,128)S(1)}) custom-call(bf16[128,2048]{1,0:T(8,128)(2,1)S(1)} %bitcast.15, f32[128,2048]{1,0:T(8,128)S(1)} %get-tuple-element.59.within, bf16[128,2048]{1,0:T(8,128)(2,1)S(1)} %bitcast.23, ...), custom_call_target="tpu_custom_call" | custom-call | flops 1000 | bytes 1000 | tf_op jit(solution)/shard_map/mix/pallas_call | solution.py:459
  15.8 0.8 %collective-permute-start.5 = (bf16[2,128,128]{2,1,0:T(8,128)(2,1)S(1)}, bf16[2,128,128]{2,1,0:T(8,128)(2,1)S(1)}, u32[]{:S(2)}, u32[]{:S(2)}) collective-permute-start(bf16[2,128,128]{2,1,0:T(8,128)(2,1)S(1)} %get-tuple-element.73), channel_id=1, source_target_pairs={{0,1},{1,0},{2,3},{3,2},{4,5},{5,4},{6,7},{7,6},{8,9},{9,8},{10,11... | collective-permute-start | bytes 196616 | tf_op jit(solution)/shard_map/ppermute | solution.py:477
  16.6 0.2 collective-permute-done.3.state.refs_21_.refs_30_
  16.8 0.6 %mix.9 = (bf16[128,384]{1,0:T(8,128)(2,1)S(1)}, bf16[128,384]{1,0:T(8,128)(2,1)S(1)}, bf16[3,128,128]{2,1,0:T(8,128)(2,1)S(1)}, f32[3,128]{1,0:T(4,128)S(1)}) custom-call(bf16[128,2048]{1,0:T(8,128)(2,1)S(1)} %bitcast.16, f32[128,2048]{1,0:T(8,128)S(1)} %get-tuple-element.59.within, bf16[128,2048]{1,0:T(8,128)(2,1)S(1)} %bitcast.24, ...), custom_call_target="tpu_custom_call" | custom-call | flops 1000 | bytes 1000 | tf_op jit(solution)/shard_map/mix/pallas_call | solution.py:459
  17.4 2.0 %collective-permute-start.6 = (bf16[3,128,128]{2,1,0:T(8,128)(2,1)S(1)}, bf16[3,128,128]{2,1,0:T(8,128)(2,1)S(1)}, u32[]{:S(2)}, u32[]{:S(2)}) collective-permute-start(bf16[3,128,128]{2,1,0:T(8,128)(2,1)S(1)} %get-tuple-element.89), channel_id=1, source_target_pairs={{0,1},{1,0},{2,3},{3,2},{4,5},{5,4},{6,7},{7,6},{8,9},{9,8},{10,11... | collective-permute-start | bytes 294920 | tf_op jit(solution)/shard_map/ppermute | solution.py:447
  19.4 0.1 collective-permute-done.4.state.refs_22_.refs_31_
  19.5 0.6 %mix.10 = (bf16[128,384]{1,0:T(8,128)(2,1)S(1)}, bf16[128,384]{1,0:T(8,128)(2,1)S(1)}, bf16[3,128,128]{2,1,0:T(8,128)(2,1)S(1)}, f32[3,128]{1,0:T(4,128)S(1)}) custom-call(bf16[128,2048]{1,0:T(8,128)(2,1)S(1)} %bitcast.17, f32[128,2048]{1,0:T(8,128)S(1)} %get-tuple-element.59.within, bf16[128,2048]{1,0:T(8,128)(2,1)S(1)} %bitcast.25, ...), custom_call_target="tpu_custom_call" | custom-call | flops 1000 | bytes 1000 | tf_op jit(solution)/shard_map/mix/pallas_call | solution.py:459
  20.1 1.3 %collective-permute-start.7 = (bf16[3,128,128]{2,1,0:T(8,128)(2,1)S(1)}, bf16[3,128,128]{2,1,0:T(8,128)(2,1)S(1)}, u32[]{:S(2)}, u32[]{:S(2)}) collective-permute-start(bf16[3,128,128]{2,1,0:T(8,128)(2,1)S(1)} %get-tuple-element.90), channel_id=1, source_target_pairs={{0,1},{1,0},{2,3},{3,2},{4,5},{5,4},{6,7},{7,6},{8,9},{9,8},{10,11... | collective-permute-start | bytes 294920 | tf_op jit(solution)/shard_map/ppermute | solution.py:447
  21.4 0.0 collective-permute-done.5.state.refs_23_.refs_32_
  21.4 0.5 %mix.11 = (bf16[128,256]{1,0:T(8,128)(2,1)S(1)}, bf16[128,256]{1,0:T(8,128)(2,1)S(1)}, bf16[2,128,128]{2,1,0:T(8,128)(2,1)S(1)}, f32[2,128]{1,0:T(2,128)S(1)}) custom-call(bf16[128,2048]{1,0:T(8,128)(2,1)S(1)} %bitcast.18, f32[128,2048]{1,0:T(8,128)S(1)} %get-tuple-element.59.within, bf16[128,2048]{1,0:T(8,128)(2,1)S(1)} %bitcast.26, ...), custom_call_target="tpu_custom_call" | custom-call | flops 1000 | bytes 1000 | tf_op jit(solution)/shard_map/mix/pallas_call | solution.py:459
  21.9 0.9 %collective-permute-start.8 = (bf16[2,128,128]{2,1,0:T(8,128)(2,1)S(1)}, bf16[2,128,128]{2,1,0:T(8,128)(2,1)S(1)}, u32[]{:S(2)}, u32[]{:S(2)}) collective-permute-start(bf16[2,128,128]{2,1,0:T(8,128)(2,1)S(1)} %get-tuple-element.91), channel_id=1, source_target_pairs={{0,1},{1,0},{2,3},{3,2},{4,5},{5,4},{6,7},{7,6},{8,9},{9,8},{10,11... | collective-permute-start | bytes 196616 | tf_op jit(solution)/shard_map/ppermute | solution.py:447
  22.8 2.7 %back.1 = (bf16[128,2048]{1,0:T(8,128)(2,1)}, f32[128,2048]{1,0:T(8,128)S(1)}, f32[128,2048]{1,0:T(8,128)S(1)}, f32[128,2048]{1,0:T(8,128)S(1)}, f32[16,128]{1,0:T(8,128)S(1)}) custom-call(bf16[128,2048]{1,0:T(8,128)(2,1)S(1)} %bitcast.19, bf16[128,2048]{1,0:T(8,128)(2,1)S(1)} %bitcast.29, bf16[128,2048]{1,0:T(8,128)(2,1)S(1)} %bitcast.34, ...), custom_call_target="tpu_custom_call" | custom-call | flops 1000 | bytes 1000 | tf_op jit(solution)/shard_map/back/pallas_call | solution.py:484
  25.5 0.7 %collective-permute-done.8.refs_2_ = bf16[2,128,128]{2,1,0:T(8,128)(2,1)S(1)} collective-permute-done((bf16[2,128,128]{2,1,0:T(8,128)(2,1)S(1)}, bf16[2,128,128]{2,1,0:T(8,128)(2,1)S(1)}, u32[]{:S(2)}, u32[]{:S(2)}) %collective-permute-start.8) | collective-permute-done | bytes 65568 | tf_op jit(solution)/shard_map/ppermute | solution.py:447
  26.2 0.0 collective-permute-done.6.refs_0_
  26.2 0.0 collective-permute-done.7.refs_1_
  26.2 0.0 copy-start.4
  26.2 1.1 %logits.1 = (bf16[16,128]{1,0:T(8,128)(2,1)S(1)}, bf16[16,24,128]{2,1,0:T(8,128)(2,1)S(1)}, bf16[16,24,128]{2,1,0:T(8,128)(2,1)S(1)}) custom-call(bf16[128,2048]{1,0:T(8,128)(2,1)S(1)} %bitcast.20, bf16[128,2048]{1,0:T(8,128)(2,1)S(1)} %bitcast.30, bf16[128,2048]{1,0:T(8,128)(2,1)S(1)} %bitcast.35, f32[16,128]{1,0:T(8,128)S(1)} %get-tuple-element.57.refs_4_.cum_ref, ...), custom_call_target="tpu_custom_call" | custom-call | flops 1000 | bytes 1000 | tf_op jit(solution)/shard_map/logits/pallas_call | solution.py:515
  27.3 0.1 collective-permute-start.9
  27.4 0.0 copy-done.4
  27.4 1.7 %finish.1 = (bf16[128,2048]{1,0:T(8,128)(2,1)}, bf16[128,2048]{1,0:T(8,128)(2,1)}, bf16[128,2048]{1,0:T(8,128)(2,1)}) custom-call(f32[128,2048]{1,0:T(8,128)S(1)} %get-tuple-element.94.gq, f32[128,2048]{1,0:T(8,128)S(1)} %get-tuple-element.95.gk, f32[128,2048]{1,0:T(8,128)S(1)} %get-tuple-element.96.gv, bf16[128,2048]{1,0:T(8,128)(2,1)S(1)} %bitcast.31, ...), custom_call_target="tpu_custom_call" | custom-call | flops 1000 | bytes 1000 | tf_op jit(solution)/shard_map/finish/pallas_call | solution.py:526
  29.1 0.0 collective-permute-done.9
  29.1 13.6 %all_to_all.5.arrived = bf16[16,24,128]{2,1,0:T(8,128)(2,1)S(1)} all-to-all(bf16[16,24,128]{2,1,0:T(8,128)(2,1)S(1)} %add_convert_fusion), channel_id=1, replica_groups=mesh['pair'=8,'core'=2,'seq'=2] {'seq','pair'}, dimensions={0} | all-to-all | bytes 196608 | tf_op jit(solution)/shard_map/all_to_all | solution.py:545
  42.7 0.7 %sum.1 = f32[16,192]{1,0:T(8,128)} custom-call(bf16[16,24,128]{2,1,0:T(8,128)(2,1)S(1)} %all_to_all.5.arrived), custom_call_target="tpu_custom_call" | custom-call | tf_op jit(solution)/shard_map/sum/pallas_call | solution.py:546
  (1 shorter events, 0.0 us)
Async XLA Ops:
  0.6 8.7 %copy-start = (bf16[1,128,2048]{2,1,0:T(8,128)(2,1)S(1)}, bf16[1,128,2048]{2,1,0:T(8,128)(2,1)}, u32[]{:S(2)}) copy-start(bf16[1,128,2048]{2,1,0:T(8,128)(2,1)} %param.7) | copy-start | bytes 1572868
  0.6 8.7 %copy-start.2 = (bf16[1,128,2048]{2,1,0:T(8,128)(2,1)S(1)}, bf16[1,128,2048]{2,1,0:T(8,128)(2,1)}, u32[]{:S(2)}) copy-start(bf16[1,128,2048]{2,1,0:T(8,128)(2,1)} %param.8) | copy-start | bytes 1572868
  0.7 8.7 %copy-start.3 = (bf16[1,128,2048]{2,1,0:T(8,128)(2,1)S(1)}, bf16[1,128,2048]{2,1,0:T(8,128)(2,1)}, u32[]{:S(2)}) copy-start(bf16[1,128,2048]{2,1,0:T(8,128)(2,1)} %param.9) | copy-start | bytes 1572868
  4.0 5.3 %copy-start.5 = (f32[16,128]{1,0:T(8,128)S(1)}, f32[16,128]{1,0:T(8,128)}, u32[]{:S(2)}) copy-start(f32[16,128]{1,0:T(8,128)} %get-tuple-element.55.logits.logits_ref) | copy-start | bytes 24580
  4.0 6.5 %collective-permute-start = (bf16[3,128,128]{2,1,0:T(8,128)(2,1)}, bf16[3,128,128]{2,1,0:T(8,128)(2,1)S(1)}, u32[]{:S(2)}, u32[]{:S(2)}) collective-permute-start(bf16[3,128,128]{2,1,0:T(8,128)(2,1)} %get-tuple-element.60), channel_id=1, source_target_pairs={{0,1},{1,0},{2,3},{3,2},{4,5},{5,4},{6,7},{7,6},{8,9},{9,8},{10,11... | collective-permute-start | bytes 294920 | tf_op jit(solution)/shard_map/ppermute | solution.py:447
  6.6 6.6 %collective-permute-start.1 = (bf16[3,128,128]{2,1,0:T(8,128)(2,1)}, bf16[3,128,128]{2,1,0:T(8,128)(2,1)S(1)}, u32[]{:S(2)}, u32[]{:S(2)}) collective-permute-start(bf16[3,128,128]{2,1,0:T(8,128)(2,1)} %get-tuple-element.63), channel_id=1, source_target_pairs={{0,1},{1,0},{2,3},{3,2},{4,5},{5,4},{6,7},{7,6},{8,9},{9,8},{10,11... | collective-permute-start | bytes 294920 | tf_op jit(solution)/shard_map/ppermute | solution.py:447
  6.7 8.6 %collective-permute-start.2 = (bf16[2,128,128]{2,1,0:T(8,128)(2,1)}, bf16[2,128,128]{2,1,0:T(8,128)(2,1)S(1)}, u32[]{:S(2)}, u32[]{:S(2)}) collective-permute-start(bf16[2,128,128]{2,1,0:T(8,128)(2,1)} %get-tuple-element.66), channel_id=1, source_target_pairs={{0,1},{1,0},{2,3},{3,2},{4,5},{5,4},{6,7},{7,6},{8,9},{9,8},{10,11... | collective-permute-start | bytes 196616 | tf_op jit(solution)/shard_map/ppermute | solution.py:447
  9.4 1.2 %copy-start.1 = (bf16[1,128,2048]{2,1,0:T(8,128)(2,1)S(1)}, bf16[1,128,2048]{2,1,0:T(8,128)(2,1)}, u32[]{:S(2)}) copy-start(bf16[1,128,2048]{2,1,0:T(8,128)(2,1)} %param.13) | copy-start | bytes 1572868
  11.2 5.6 %collective-permute-start.3 = (bf16[3,128,128]{2,1,0:T(8,128)(2,1)S(1)}, bf16[3,128,128]{2,1,0:T(8,128)(2,1)S(1)}, u32[]{:S(2)}, u32[]{:S(2)}) collective-permute-start(bf16[3,128,128]{2,1,0:T(8,128)(2,1)S(1)} %get-tuple-element.69), channel_id=1, source_target_pairs={{0,1},{1,0},{2,3},{3,2},{4,5},{5,4},{6,7},{7,6},{8,9},{9,8},{10,11... | collective-permute-start | bytes 294920 | tf_op jit(solution)/shard_map/ppermute | solution.py:477
  13.8 5.7 %collective-permute-start.4 = (bf16[3,128,128]{2,1,0:T(8,128)(2,1)S(1)}, bf16[3,128,128]{2,1,0:T(8,128)(2,1)S(1)}, u32[]{:S(2)}, u32[]{:S(2)}) collective-permute-start(bf16[3,128,128]{2,1,0:T(8,128)(2,1)S(1)} %get-tuple-element.71), channel_id=1, source_target_pairs={{0,1},{1,0},{2,3},{3,2},{4,5},{5,4},{6,7},{7,6},{8,9},{9,8},{10,11... | collective-permute-start | bytes 294920 | tf_op jit(solution)/shard_map/ppermute | solution.py:477
  15.8 5.6 %collective-permute-start.5 = (bf16[2,128,128]{2,1,0:T(8,128)(2,1)S(1)}, bf16[2,128,128]{2,1,0:T(8,128)(2,1)S(1)}, u32[]{:S(2)}, u32[]{:S(2)}) collective-permute-start(bf16[2,128,128]{2,1,0:T(8,128)(2,1)S(1)} %get-tuple-element.73), channel_id=1, source_target_pairs={{0,1},{1,0},{2,3},{3,2},{4,5},{5,4},{6,7},{7,6},{8,9},{9,8},{10,11... | collective-permute-start | bytes 196616 | tf_op jit(solution)/shard_map/ppermute | solution.py:477
  17.4 8.8 %collective-permute-start.6 = (bf16[3,128,128]{2,1,0:T(8,128)(2,1)S(1)}, bf16[3,128,128]{2,1,0:T(8,128)(2,1)S(1)}, u32[]{:S(2)}, u32[]{:S(2)}) collective-permute-start(bf16[3,128,128]{2,1,0:T(8,128)(2,1)S(1)} %get-tuple-element.89), channel_id=1, source_target_pairs={{0,1},{1,0},{2,3},{3,2},{4,5},{5,4},{6,7},{7,6},{8,9},{9,8},{10,11... | collective-permute-start | bytes 294920 | tf_op jit(solution)/shard_map/ppermute | solution.py:447
  20.1 6.1 %collective-permute-start.7 = (bf16[3,128,128]{2,1,0:T(8,128)(2,1)S(1)}, bf16[3,128,128]{2,1,0:T(8,128)(2,1)S(1)}, u32[]{:S(2)}, u32[]{:S(2)}) collective-permute-start(bf16[3,128,128]{2,1,0:T(8,128)(2,1)S(1)} %get-tuple-element.90), channel_id=1, source_target_pairs={{0,1},{1,0},{2,3},{3,2},{4,5},{5,4},{6,7},{7,6},{8,9},{9,8},{10,11... | collective-permute-start | bytes 294920 | tf_op jit(solution)/shard_map/ppermute | solution.py:447
  21.9 4.3 %collective-permute-start.8 = (bf16[2,128,128]{2,1,0:T(8,128)(2,1)S(1)}, bf16[2,128,128]{2,1,0:T(8,128)(2,1)S(1)}, u32[]{:S(2)}, u32[]{:S(2)}) collective-permute-start(bf16[2,128,128]{2,1,0:T(8,128)(2,1)S(1)} %get-tuple-element.91), channel_id=1, source_target_pairs={{0,1},{1,0},{2,3},{3,2},{4,5},{5,4},{6,7},{7,6},{8,9},{9,8},{10,11... | collective-permute-start | bytes 196616 | tf_op jit(solution)/shard_map/ppermute | solution.py:447
  26.2 1.2 %copy-start.4 = (bf16[6144,16]{0,1:T(8,128)(2,1)S(1)}, bf16[6144,16]{0,1:T(8,128)(2,1)}, u32[]{:S(2)}) copy-start(bf16[6144,16]{0,1:T(8,128)(2,1)} %param.11) | copy-start | bytes 589828
  27.3 1.8 %collective-permute-start.9 = (bf16[16,24,128]{2,1,0:T(8,128)(2,1)S(1)}, bf16[16,24,128]{2,1,0:T(8,128)(2,1)S(1)}, u32[]{:S(2)}, u32[]{:S(2)}) collective-permute-start(bf16[16,24,128]{2,1,0:T(8,128)(2,1)S(1)} %get-tuple-element.93), channel_id=1, source_target_pairs={{0,2},{2,0},{1,3},{3,1},{4,6},{6,4},{5,7},{7,5},{8,10},{10,8},{9,1... | collective-permute-start | bytes 294920 | tf_op jit(solution)/shard_map/ppermute | solution.py:542
